TPU v7x, 256 devices: a whole 4x4x8 slice. The times are simulated.
256 devices in a mesh: sec: 16 (over y, x), mpo: 16 (over z, core).
Axes of the slice: x: 4, y: 4, z: 8, core: 2. Of those that a mesh axis runs over, the one named last changes fastest.
Arguments:
- wavefunction: bfloat16 [256, 128, 128], P('sec')
- left_size: int32 [256], P('sec'), may hold values from 32 to 128, as said below
- right_size: int32 [256], replicated, may hold values from 32 to 128, as said below
- right_sector: int32 [256], replicated, may hold values from 0 to 255, as said below
- left_environment: bfloat16 [32, 256, 128, 128], P('mpo', 'sec')
- right_environment: bfloat16 [32, 256, 128, 128], P('mpo', 'sec')
- term_weights: float32 [32], P('mpo'), may hold values from -0.4 to 0.4
Outputs:
- next_vector: float32 [256, 128, 128], P('sec', 'mpo')
- residual: float32 [256, 128, 128], P('sec', 'mpo')
- coefficients: float32 [3], replicated
Inputs may be any that keep to these rules, and one draw needn't show every extreme that they name: `left_size`: some left sector has all 128 rows live. `right_size`: some right sector has all 128 columns live. `right_sector`: a permutation of the 256 sectors; of the left sectors of one index of sec (16 in a row) at most 2 pair with right sectors of any one index of sec (also 16 in a row), and some such pair of indices has exactly 2.
All inputs are finite; a program needn't handle non-finite values.
Results may differ from a plain program's by a relative error of at most 0.0064.
Values may be sent and summed in bfloat16 or wider, within the bound.
No kernel may reach another device: no remote copies, remote signals or barrier semaphores. Data moves between devices by JAX's collectives and lax.ppermute only.
A program may use at most 64 MiB of HBM per device.

v0:
```python
import jax
import jax.numpy as jnp
from jax import lax
from jax.sharding import PartitionSpec as P


def route_matches(right_sector, blocks, devices, capacity):
    owners = (right_sector // blocks).reshape(devices, blocks)
    targets = jnp.arange(devices, dtype=jnp.int32)
    onehot = (owners[:, :, None] == targets[None, None, :]).astype(jnp.int32)
    earlier = jnp.cumsum(onehot, axis=1) - onehot
    position = jnp.sum(earlier * onehot, axis=2)
    places = owners * capacity + position
    slot_ids = jnp.arange(devices * capacity, dtype=jnp.int32)
    matches = (places[:, :, None] == slot_ids[None, None, :]).astype(jnp.int32)
    return (places, matches)


def shards(
    wavefunction,
    left_size,
    right_size,
    right_sector,
    left_environment,
    right_environment,
    term_weights,
):
    blocks = wavefunction.shape[0]
    width = wavefunction.shape[1]
    terms = left_environment.shape[0]
    devices = lax.axis_size("sec")
    layers = lax.axis_size("mpo")
    average = blocks // devices
    capacity = average + max(1, average // 2)
    sec_index = lax.axis_index("sec")
    mpo_index = lax.axis_index("mpo")
    entries = float(blocks * devices * width * width)
    places, matches = route_matches(right_sector, blocks, devices, capacity)
    own_places = lax.dynamic_index_in_dim(places, sec_index, 0, keepdims=False)
    own_matches = lax.dynamic_index_in_dim(matches, sec_index, 0, keepdims=False)
    block_ids = jnp.arange(blocks, dtype=jnp.int32)
    send_source = jnp.sum(block_ids[:, None] * own_matches, axis=0)
    send_valid = jnp.sum(own_matches, axis=0) > 0
    incoming = lax.dynamic_slice_in_dim(matches, sec_index * capacity, capacity, 2)
    sector_grid = right_sector.reshape(devices, blocks)
    arrived_valid = jnp.sum(incoming, axis=1) > 0
    arrived_sector = jnp.sum(sector_grid[:, :, None] * incoming, axis=1)
    arrived_local = jnp.where(arrived_valid, arrived_sector - sec_index * blocks, 0).reshape(-1)
    own_sector = lax.dynamic_slice_in_dim(right_sector, sec_index * blocks, blocks, 0)
    positions = jnp.arange(width, dtype=jnp.int32)
    partner_size = jnp.take(right_size, own_sector, axis=0)
    row_live = (positions[None, :] < left_size[:, None]).astype(jnp.float32)
    col_live = (positions[None, :] < partner_size[:, None]).astype(jnp.float32)
    live_mask = row_live[:, :, None] * col_live[:, None, :]

    def apply_operator(vector):
        rounded = vector.astype(jnp.bfloat16)
        half_term = jnp.einsum(
            "wsab,sbc->swac", left_environment, rounded, preferred_element_type=jnp.float32
        )
        half_term = (term_weights[None, :, None, None] * half_term).astype(jnp.bfloat16)
        outgoing = jnp.where(
            send_valid[:, None, None, None],
            jnp.take(half_term, send_source, axis=0),
            jnp.zeros((), jnp.bfloat16),
        )
        outgoing = outgoing.reshape(devices, capacity, terms, width, width)
        arrived = lax.all_to_all(outgoing, "sec", split_axis=0, concat_axis=0, tiled=True)
        arrived = arrived.reshape(devices * capacity, terms, width, width)
        right_terms = jnp.take(right_environment, arrived_local, axis=1)
        partial_value = jnp.einsum(
            "kwac,wkdc->kad", arrived, right_terms, preferred_element_type=jnp.float32
        )
        partial_value = partial_value.reshape(devices, capacity, width, width)
        summed = lax.psum(partial_value, "mpo")
        returned = lax.all_to_all(summed, "sec", split_axis=0, concat_axis=0, tiled=True)
        applied = jnp.take(returned.reshape(devices * capacity, width, width), own_places, axis=0)
        return live_mask * applied

    def rayleigh(basis_vec, applied_vec):
        return lax.psum(jnp.sum(basis_vec * applied_vec), "sec")

    masked_start = live_mask * wavefunction.astype(jnp.float32)
    start_total = lax.psum(jnp.sum(masked_start * masked_start), "sec")
    first_vector = masked_start / jnp.sqrt(start_total / entries + 1e-06)
    image_first = apply_operator(first_vector)
    alpha_first = rayleigh(first_vector, image_first) / entries
    lanczos_rest = image_first - alpha_first * first_vector
    rest_total = lax.psum(jnp.sum(lanczos_rest * lanczos_rest), "sec")
    beta_next = jnp.sqrt(rest_total / entries + 1e-06)
    next_vector = lanczos_rest / beta_next
    image_next = apply_operator(next_vector)
    alpha_next = rayleigh(next_vector, image_next) / entries
    residual = image_next - alpha_next * next_vector - beta_next * first_vector
    row_count = width // layers
    next_slice = lax.dynamic_slice_in_dim(next_vector, mpo_index * row_count, row_count, 1)
    residual_slice = lax.dynamic_slice_in_dim(residual, mpo_index * row_count, row_count, 1)
    coefficients = jnp.stack([alpha_first, beta_next, alpha_next])
    return (next_slice, residual_slice, coefficients)


def solution(mesh):
    placed = (
        P("sec", None, None),
        P("sec"),
        P(),
        P(),
        P("mpo", "sec", None, None),
        P("mpo", "sec", None, None),
        P("mpo"),
    )
    return jax.shard_map(
        shards,
        mesh=mesh,
        in_specs=placed,
        out_specs=(P("sec", "mpo", None), P("sec", "mpo", None), P()),
        check_vma=False,
    )
```

profile of v0, /device:TPU:1, one launch (start us, length us, event | category | flops | bytes accessed | tf_op | source)
XLA Modules:
  0.0 560.7 jit_solution(13970015189947100018)
XLA Ops:
  7.2 0.8 and_select_fusion
  8.0 0.8 mul.122
  8.7 0.1 reshape.119
  8.8 0.1 copy.51
  8.9 0.5 fusion.24
  9.4 0.1 fusion.15
  9.6 0.8 compare_select_fusion.3
  10.4 1.3 gather_fusion
  11.7 0.8 and_select_fusion.1
  12.5 0.7 fusion.19
  13.2 2.0 multiply_reduce_fusion.3
  15.2 34.9 %psum.42 = f32[]{:T(128)} all-reduce(f32[]{:T(128)} %multiply_reduce_fusion.3), channel_id=1, replica_groups=mesh['sec'=16,'mpo'=16] {'sec'}, use_global_device_ids=true, to_apply=%region_4.5 | all-reduce | flops 1 | bytes 8 | tf_op jit(solution)/shard_map/psum | solution.py:84
  50.7 0.2 multiply_reduce_fusion.4
  50.9 0.1 copy.72
  51.0 0.1 copy.71
  51.1 0.1 copy.59
  51.1 0.1 select_n.74
  51.3 3.2 fusion.4
  54.5 2.2 gather_fusion.1
  56.7 1.6 select_select_fusion.1
  58.3 4.4 all-to-all-start
  62.8 1.0 gather_fusion.2
  63.8 21.7 %all-to-all-done = bf16[16,2,2,128,128]{3,4,2,1,0:T(8,128)(2,1)} async-done(((bf16[16,2,2,128,128]{3,4,2,1,0:T(8,128)(2,1)}), bf16[16,2,2,128,128]{3,4,2,1,0:T(8,128)(2,1)}, u32[]{:S(2)}, u32[]{:S(2)}) %all-to-all-start) | async-done | bytes 2097184 | tf_op jit(solution)/shard_map/all_to_all | solution.py:68
  85.5 3.7 fusion.2
  89.2 122.6 %all-reduce.3.cloned.1.call-done = f32[16,2,128,128]{3,2,1,0:T(8,128)} async-done(((f32[16,2,128,128]{3,2,1,0:T(8,128)}), f32[16,2,128,128]{3,2,1,0:T(8,128)}) %all-reduce.3.cloned.1.call-update) | async-done | bytes 2097168 | tf_op jit(solution)/shard_map/psum | solution.py:75
  211.8 6.6 %all-to-all-start.1 = ((f32[16,2,128,128]{3,2,1,0:T(8,128)}), f32[16,2,128,128]{3,2,1,0:T(8,128)}, u32[]{:S(2)}, u32[]{:S(2)}) async-start(f32[16,2,128,128]{3,2,1,0:T(8,128)} %all-reduce.3.cloned.1.call-done), calls=%async_computation.1 | async-start | bytes 4194304 | tf_op jit(solution)/shard_map/all_to_all | solution.py:76
  218.5 0.2 dynamic-slice_reduce_fusion.1
  218.7 29.4 %all-to-all-done.1 = f32[16,2,128,128]{3,2,1,0:T(8,128)} async-done(((f32[16,2,128,128]{3,2,1,0:T(8,128)}), f32[16,2,128,128]{3,2,1,0:T(8,128)}, u32[]{:S(2)}, u32[]{:S(2)}) %all-to-all-start.1) | async-done | bytes 2097184 | tf_op jit(solution)/shard_map/all_to_all | solution.py:76
  248.1 3.2 gather_fusion.3
  251.3 2.3 multiply_reduce_fusion.2
  253.6 29.9 %psum.44 = f32[]{:T(128)} all-reduce(f32[]{:T(128)} %multiply_reduce_fusion.2), channel_id=1, replica_groups=mesh['sec'=16,'mpo'=16] {'sec'}, use_global_device_ids=true, to_apply=%region_10.14 | all-reduce | flops 1 | bytes 8 | tf_op jit(solution)/shard_map/psum | solution.py:81
  284.2 2.4 multiply_reduce_fusion.1
  286.6 29.8 %psum.45 = f32[]{:T(128)} all-reduce(f32[]{:T(128)} %multiply_reduce_fusion.1), channel_id=1, replica_groups=mesh['sec'=16,'mpo'=16] {'sec'}, use_global_device_ids=true, to_apply=%region_12.16 | all-reduce | flops 1 | bytes 8 | tf_op jit(solution)/shard_map/psum | solution.py:89
  317.1 2.9 broadcast_divide_fusion
  320.0 1.0 copy-done.1
  321.0 1.5 fusion.5
  322.5 3.4 gather_fusion.4
  325.9 1.9 select_select_fusion
  327.8 20.2 %all_to_all.20 = bf16[16,2,2,128,128]{3,4,2,1,0:T(8,128)(2,1)S(1)} all-to-all(bf16[16,2,2,128,128]{3,4,2,1,0:T(8,128)(2,1)S(1)} %bitcast.47), channel_id=1, replica_groups=mesh['sec'=16,'mpo'=16] {'sec'}, dimensions={0} | all-to-all | bytes 4194304 | tf_op jit(solution)/shard_map/all_to_all | solution.py:68
  348.0 2.1 fusion
  350.1 130.7 %all-reduce.5.cloned.1.call-done = f32[16,2,128,128]{3,2,1,0:T(8,128)} async-done(((f32[16,2,128,128]{3,2,1,0:T(8,128)}), f32[16,2,128,128]{3,2,1,0:T(8,128)}) %all-reduce.5.cloned.1.call-update) | async-done | bytes 2097168 | tf_op jit(solution)/shard_map/psum | solution.py:75
  480.8 6.6 %all-to-all-start.3 = ((f32[16,2,128,128]{3,2,1,0:T(8,128)}), f32[16,2,128,128]{3,2,1,0:T(8,128)}, u32[]{:S(2)}, u32[]{:S(2)}) async-start(f32[16,2,128,128]{3,2,1,0:T(8,128)} %all-reduce.5.cloned.1.call-done), calls=%async_computation.3 | async-start | bytes 4194304 | tf_op jit(solution)/shard_map/all_to_all | solution.py:76
  487.4 29.7 %all-to-all-done.3 = f32[16,2,128,128]{3,2,1,0:T(8,128)} async-done(((f32[16,2,128,128]{3,2,1,0:T(8,128)}), f32[16,2,128,128]{3,2,1,0:T(8,128)}, u32[]{:S(2)}, u32[]{:S(2)}) %all-to-all-start.3) | async-done | bytes 2097184 | tf_op jit(solution)/shard_map/all_to_all | solution.py:76
  517.0 2.2 gather_fusion.5
  519.2 2.0 multiply_reduce_fusion
  521.2 29.9 %psum.47 = f32[]{:T(128)} all-reduce(f32[]{:T(128)} %get-tuple-element.10), channel_id=1, replica_groups=mesh['sec'=16,'mpo'=16] {'sec'}, use_global_device_ids=true, to_apply=%region_15.19 | all-reduce | flops 1 | bytes 8 | tf_op jit(solution)/shard_map/psum | solution.py:81
  551.8 1.5 fusion.16
  553.3 0.6 pad_maximum_fusion
  (27 shorter events, 0.3 us)
Async XLA Ops:
  7.2 55.6 %copy-start = (bf16[2,16,128,128]{3,2,1,0:T(8,128)(2,1)S(1)}, bf16[2,16,128,128]{3,2,1,0:T(8,128)(2,1)}, u32[]{:S(2)}) copy-start(bf16[2,16,128,128]{3,2,1,0:T(8,128)(2,1)} %param.18) | copy-start | bytes 3145732
  58.3 27.2 %all-to-all-start = ((bf16[16,2,2,128,128]{3,4,2,1,0:T(8,128)(2,1)}), bf16[16,2,2,128,128]{3,4,2,1,0:T(8,128)(2,1)}, u32[]{:S(2)}, u32[]{:S(2)}) async-start(bf16[16,2,2,128,128]{3,4,2,1,0:T(8,128)(2,1)} %bitcast.3), calls=%async_computation | async-start | bytes 4194304 | tf_op jit(solution)/shard_map/all_to_all | solution.py:68
  62.7 149.1 %all-reduce.3.cloned.1.call-start = ((), (), s32[]{:S(2)}) async-start(), calls=%async_computation.4 | async-start | bytes 4194304 | tf_op jit(solution)/shard_map/psum | solution.py:75
  211.8 36.3 %all-to-all-start.1 = ((f32[16,2,128,128]{3,2,1,0:T(8,128)}), f32[16,2,128,128]{3,2,1,0:T(8,128)}, u32[]{:S(2)}, u32[]{:S(2)}) async-start(f32[16,2,128,128]{3,2,1,0:T(8,128)} %all-reduce.3.cloned.1.call-done), calls=%async_computation.1 | async-start | bytes 4194304 | tf_op jit(solution)/shard_map/all_to_all | solution.py:76
  218.4 262.3 %all-reduce.5.cloned.1.call-start = ((), (), s32[]{:S(2)}) async-start(), calls=%async_computation.5 | async-start | bytes 4194304 | tf_op jit(solution)/shard_map/psum | solution.py:75
  286.6 34.4 %copy-start.4 = (f32[2]{0:T(128)S(1)}, f32[2]{0:T(128)}, u32[]{:S(2)}) copy-start(f32[2]{0:T(128)} %param.19) | copy-start | bytes 28
  317.1 3.9 copy-start.3
  320.0 1.0 copy-start.1
  480.8 36.3 %all-to-all-start.3 = ((f32[16,2,128,128]{3,2,1,0:T(8,128)}), f32[16,2,128,128]{3,2,1,0:T(8,128)}, u32[]{:S(2)}, u32[]{:S(2)}) async-start(f32[16,2,128,128]{3,2,1,0:T(8,128)} %all-reduce.5.cloned.1.call-done), calls=%async_computation.3 | async-start | bytes 4194304 | tf_op jit(solution)/shard_map/all_to_all | solution.py:76
  487.3 31.9 %copy-start.2 = (f32[16,128,128]{2,1,0:T(8,128)S(1)}, f32[16,128,128]{2,1,0:T(8,128)}, u32[]{:S(2)}) copy-start(f32[16,128,128]{2,1,0:T(8,128)} %copy-done.1) | copy-start | bytes 3145732
Sparse Core Ops, SparseCore 0:
  89.3 122.4 all-reduce.2
  350.2 130.4 all-reduce.4
where the time goes:
time: 571 us; the launch traced here: 561 us
  waiting for transfers between devices  334 us (58%)
  blocking collectives  145 us (25%)
  other arithmetic  21.2 us (4%)
  starting transfers between devices  17.7 us (3%)
  between operations  16.9 us (3%)
  local copies, waits for them, and re-layouts  15.8 us (3%)
  matrix products  10.5 us (2%)
    psum x2, waiting for transfers between devices, apply_operator(): summed = lax.psum(partial_value, 'mpo')  253 us
    psum x2, blocking collectives, rayleigh(): return lax.psum(jnp.sum(basis_vec * applied_vec), 'sec')  59.8 us
    all_to_all x2, waiting for transfers between devices, apply_operator(): lax.all_to_all(summed, 'sec', split_axis=0, concat_axis=0, tiled=True)  59 us
    psum x1, blocking collectives, shards(): start_total = lax.psum(jnp.sum(masked_start * masked_start), 'sec')  34.9 us
    psum x1, blocking collectives, shards(): rest_total = lax.psum(jnp.sum(lanczos_rest * lanczos_rest), 'sec')  29.8 us
    all_to_all x1, waiting for transfers between devices, apply_operator(): lax.all_to_all(outgoing, 'sec', split_axis=0, concat_axis=0, tiled=True)  21.7 us
    all_to_all x1, blocking collectives, apply_operator(): lax.all_to_all(outgoing, 'sec', split_axis=0, concat_axis=0, tiled=True)  20.2 us
    all_to_all x2, starting transfers between devices, apply_operator(): lax.all_to_all(summed, 'sec', split_axis=0, concat_axis=0, tiled=True)  13.2 us
  transfers between devices with their start and end apart: 5, of which 5 were waited for; matrix products, arithmetic and copies ran while one was open for 0% of the time, Pallas kernels for 0%

commit v1 on v0

v1 whole, which is shorter than its diff:
```python
import jax
import jax.numpy as jnp
from jax import lax
from jax.experimental import pallas as pl
from jax.experimental.pallas import tpu as pltpu
from jax.sharding import PartitionSpec as P

F32 = jnp.float32
BF16 = jnp.bfloat16
SLOTS = 2
PAD = 16
LANES = 8
MIB = 1024 * 1024


def pack_kernel(right_sector, weights, left_env, right_env, right_out, left_out, wbuf, sem):
    terms, blocks, width, _ = left_env.shape
    devices = right_out.shape[0]
    sec = lax.axis_index("sec")
    row = lax.broadcasted_iota(jnp.int32, wbuf.shape, 0)
    vals = jnp.zeros(wbuf.shape, F32)
    for w in range(terms):
        whole = jnp.full(wbuf.shape, weights[w], F32)
        high = whole.astype(BF16).astype(F32)
        mid = (whole - high).astype(BF16).astype(F32)
        low = whole - high - mid
        for j, part in enumerate((high, mid, low)):
            vals = jnp.where(row == w * 3 + j, part, vals)
    wbuf[...] = vals.astype(BF16)
    copies = []
    for q in range(blocks):
        for w in range(terms):
            copies.append(pltpu.make_async_copy(left_env.at[w, q], left_out.at[q, pl.ds(w * width, width)], sem.at[0]))
        copies.append(pltpu.make_async_copy(wbuf, left_out.at[q, pl.ds(terms * width, PAD)], sem.at[0]))
    for copy in copies:
        copy.start()
    for t in range(devices):
        first = jnp.int32(-1)
        last = jnp.int32(0)
        for i in range(blocks):
            sector = right_sector[t * blocks + i]
            match = sector // blocks == sec
            local = sector % blocks
            first = jnp.where(match & (first < 0), local, first)
            last = jnp.where(match, local, last)
        first = jnp.maximum(first, 0)
        for k, index in enumerate((first, last)):
            copy = pltpu.make_async_copy(right_env.at[:, index], right_out.at[t, k], sem.at[1])
            copy.start()
            copies.append(copy)
    for copy in copies:
        copy.wait()


def order_kernel(right_sector, arrived, ordered, sem):
    blocks = ordered.shape[0]
    sec = lax.axis_index("sec")
    sources = [right_sector[sec * blocks + q] // blocks for q in range(blocks)]
    copies = []
    for q in range(blocks):
        again = jnp.bool_(False)
        for other in range(q):
            again = again | (sources[other] == sources[q])
        copy = pltpu.make_async_copy(arrived.at[sources[q], jnp.where(again, 1, 0)], ordered.at[q], sem)
        copy.start()
        copies.append(copy)
    for copy in copies:
        copy.wait()


def live(rows, left, right):
    row = lax.broadcasted_iota(jnp.int32, rows, 0)
    col = lax.broadcasted_iota(jnp.int32, rows, 1)
    return (row < left) & (col < right)


def total(x):
    return jnp.sum(jnp.sum(x, axis=0, keepdims=True), axis=1, keepdims=True)


def lanczos_kernel(left_size, right_size, right_sector, vector, left_terms, right_terms, out):
    sources, _, width = left_terms.shape
    terms = right_terms.shape[1]
    sec = lax.axis_index("sec")
    own = lax.axis_index("mpo")
    blocks = left_size.shape[0]
    mask = live((width, width), left_size[own], right_size[right_sector[sec * blocks + own]])

    def apply(block):
        acc = jnp.zeros((width, width), F32)
        for p in range(sources):
            half = jnp.dot(left_terms[p, : terms * width], block, preferred_element_type=F32)
            scale = left_terms[p, terms * width :].astype(F32)
            for w in range(terms):
                weight = scale[3 * w : 3 * w + 1] + scale[3 * w + 1 : 3 * w + 2] + scale[3 * w + 2 : 3 * w + 3]
                term = (weight * half[w * width : (w + 1) * width]).astype(BF16)
                acc = acc + lax.dot_general(
                    term, right_terms[p, w], (((1,), (1,)), ((), ())), preferred_element_type=F32
                )
        return jnp.where(mask, acc, 0.0)

    start = jnp.where(mask, vector[0].astype(F32), 0.0)
    norm = total(start * start)
    scale = 1.0 / jnp.sqrt(norm / float(width * width) + 1e-06)
    image = apply(start.astype(BF16)) * scale
    unit = start * scale
    length = total(unit * unit)
    overlap = total(unit * image)
    ratio = jnp.where(length > 0.0, overlap / jnp.where(length > 0.0, length, 1.0), 0.0)
    rest = image - ratio * unit
    after = apply(rest.astype(BF16))
    numbers = (
        norm,
        overlap,
        ratio,
        total(rest * rest),
        total(rest * after),
        total(unit * after) + total(rest * image),
        total(rest * unit),
    )
    lane = lax.broadcasted_iota(jnp.int32, (8, width), 1)
    line = jnp.zeros((8, width), F32)
    for j, number in enumerate(numbers):
        line = jnp.where(lane == own * LANES + j, number, line)
    parts = out.shape[0]
    rows = width // parts
    for d in range(parts):
        out[d, :rows] = rest[d * rows : (d + 1) * rows]
        out[d, rows : 2 * rows] = after[d * rows : (d + 1) * rows]
        out[d, 2 * rows :] = line


def finish_kernel(left_size, right_size, right_sector, vector, pieces, shared, next_out, rest_out, coef_out):
    blocks, rows, width = vector.shape
    sec = lax.axis_index("sec")
    part = lax.axis_index("mpo")
    devices = shared.shape[0]
    entries = float(devices * blocks * width * width)
    cells = float(width * width)
    stats = shared[:, 0, :]
    lane = lax.broadcasted_iota(jnp.int32, stats.shape, 1) % LANES

    def field(x, j):
        return x if j == 0 else pltpu.roll(x, x.shape[1] - j, 1)

    lead = lane == 0
    norm = jnp.where(lead, field(stats, 0), 0.0)
    overlap = field(stats, 1)
    ratio = field(stats, 2)
    gain = 1.0 / jnp.sqrt(total(norm) / entries + 1e-06)
    mean = jnp.where(lead, norm, 0.0) / cells + 1e-06
    weight = jnp.where(lead, (gain * gain) * mean, 0.0)
    length = norm / mean
    alpha = total(jnp.where(lead, weight * overlap, 0.0)) / entries
    delta = jnp.where(lead, ratio - alpha, 0.0)
    rest_total = total(jnp.where(lead, weight * (field(stats, 3) + delta * delta * length + 2.0 * delta * field(stats, 6)), 0.0))
    beta = jnp.sqrt(rest_total / entries + 1e-06)
    inner = field(stats, 4) + delta * field(stats, 5) + delta * delta * overlap
    alpha_next = total(jnp.where(lead, weight * inner, 0.0)) / entries / beta / beta
    coef_lane = lax.broadcasted_iota(jnp.int32, coef_out.shape, 1)
    coef_out[...] = jnp.where(coef_lane == 0, alpha, jnp.where(coef_lane == 1, beta, alpha_next))
    for q in range(blocks):
        line = pieces[q, 2 * rows : 2 * rows + 1, :]
        lane_one = lax.broadcasted_iota(jnp.int32, line.shape, 1)
        norm_q = jnp.sum(jnp.where(lane_one == q * LANES, line, 0.0), axis=1, keepdims=True)
        ratio_q = jnp.sum(jnp.where(lane_one == q * LANES + 2, line, 0.0), axis=1, keepdims=True)
        root = jnp.sqrt(norm_q / cells + 1e-06)
        scale = gain * root
        row = lax.broadcasted_iota(jnp.int32, (rows, width), 0) + part * rows
        col = lax.broadcasted_iota(jnp.int32, (rows, width), 1)
        mask = (row < left_size[q]) & (col < right_size[right_sector[sec * blocks + q]])
        unit = jnp.where(mask, vector[q].astype(F32), 0.0) / root
        rest = pieces[q, :rows]
        after = pieces[q, rows : 2 * rows]
        shift = ratio_q - alpha
        second = (scale / beta) * (rest + shift * unit)
        image = (scale / beta) * (after + shift * (rest + ratio_q * unit))
        next_out[q] = second
        rest_out[q] = image - alpha_next * second - (beta * scale) * unit


def shards(
    wavefunction,
    left_size,
    right_size,
    right_sector,
    left_environment,
    right_environment,
    term_weights,
):
    blocks, width, _ = wavefunction.shape
    terms = left_environment.shape[0]
    devices = lax.axis_size("sec")
    layers = lax.axis_size("mpo")
    rows = width // layers
    own = lax.axis_index("mpo")
    anywhere = pl.BlockSpec(memory_space=pl.ANY)
    scalars = pl.BlockSpec(memory_space=pltpu.SMEM)
    vmem = pl.BlockSpec(memory_space=pltpu.VMEM)

    with jax.named_scope("pack"):
        right_out, left_out = pl.pallas_call(
            pack_kernel,
            out_shape=(
                jax.ShapeDtypeStruct((devices, SLOTS, terms, width, width), BF16),
                jax.ShapeDtypeStruct((blocks, terms * width + PAD, width), BF16),
            ),
            in_specs=[scalars, scalars, anywhere, anywhere],
            out_specs=(anywhere, anywhere),
            scratch_shapes=[pltpu.VMEM((PAD, width), BF16), pltpu.SemaphoreType.DMA((2,))],
            compiler_params=pltpu.CompilerParams(vmem_limit_bytes=4 * MIB),
        )(right_sector, term_weights, left_environment, right_environment)
    with jax.named_scope("right_over_sec"):
        arrived = lax.all_to_all(right_out, "sec", 0, 0, tiled=True)
    with jax.named_scope("left_over_mpo"):
        left_terms = lax.all_to_all(left_out, "mpo", 0, 0, tiled=True)
    with jax.named_scope("order"):
        ordered = pl.pallas_call(
            order_kernel,
            out_shape=jax.ShapeDtypeStruct((blocks, terms, width, width), BF16),
            in_specs=[scalars, anywhere],
            out_specs=anywhere,
            scratch_shapes=[pltpu.SemaphoreType.DMA],
            compiler_params=pltpu.CompilerParams(vmem_limit_bytes=4 * MIB),
        )(right_sector, arrived)
    with jax.named_scope("right_over_mpo"):
        right_terms = lax.all_to_all(ordered, "mpo", 0, 0, tiled=True)
    with jax.named_scope("lanczos"):
        vector = lax.dynamic_slice_in_dim(wavefunction, own, 1, 0)
        pieces = pl.pallas_call(
            lanczos_kernel,
            out_shape=jax.ShapeDtypeStruct((layers, 2 * rows + 8, width), F32),
            in_specs=[scalars, scalars, scalars, vmem, vmem, vmem],
            out_specs=vmem,
            compiler_params=pltpu.CompilerParams(vmem_limit_bytes=16 * MIB),
        )(left_size, right_size, right_sector, vector, left_terms, right_terms)
    with jax.named_scope("rows_over_mpo"):
        pieces = lax.all_to_all(pieces, "mpo", 0, 0, tiled=True)
    with jax.named_scope("numbers_over_sec"):
        line = jnp.sum(pieces[:, 2 * rows :, :], axis=0)
        shared = lax.all_to_all(jnp.broadcast_to(line[None], (devices, 8, width)), "sec", 0, 0, tiled=True)
    with jax.named_scope("finish"):
        own_rows = lax.dynamic_slice_in_dim(wavefunction, own * rows, rows, 1)
        next_vector, residual, coefficients = pl.pallas_call(
            finish_kernel,
            out_shape=(
                jax.ShapeDtypeStruct((blocks, rows, width), F32),
                jax.ShapeDtypeStruct((blocks, rows, width), F32),
                jax.ShapeDtypeStruct((1, width), F32),
            ),
            in_specs=[scalars, scalars, scalars, vmem, vmem, vmem],
            out_specs=(vmem, vmem, vmem),
            compiler_params=pltpu.CompilerParams(vmem_limit_bytes=8 * MIB),
        )(left_size, right_size, right_sector, own_rows, pieces, shared)
    return (next_vector, residual, coefficients[0, :3])


def solution(mesh):
    placed = (
        P("sec", None, None),
        P("sec"),
        P(),
        P(),
        P("mpo", "sec", None, None),
        P("mpo", "sec", None, None),
        P("mpo"),
    )
    return jax.shard_map(
        shards,
        mesh=mesh,
        in_specs=placed,
        out_specs=(P("sec", "mpo", None), P("sec", "mpo", None), P()),
        check_vma=False,
    )
```

time: 571 us -> 150 us (0.26); the launches traced: 561 us -> 149 us
  waiting for transfers between devices: 334 us -> 71.3 us
  blocking collectives: 145 us -> 34.7 us
  other arithmetic: 21.2 us -> 0.02 us
  between operations: 16.9 us -> 0.74 us
  Pallas kernels: 0 us -> 15.1 us
  matrix products: 10.5 us -> 0 us
  local copies, waits for them, and re-layouts: 15.8 us -> 6.02 us
    psum x2 -> x0, waiting for transfers between devices: 253 us -> none  [apply_operator(): summed = lax.psum(partial_value, 'mpo')]
    psum x4 -> x0, blocking collectives: 124 us -> none  [the longest x2 59.8 us: rayleigh(): return lax.psum(jnp.sum(basis_vec * applied_vec), 'sec')]
    pallas_call x0 -> x4, Pallas kernels: none -> 15.1 us  [the longest x1 6.25 us: shards(): pl.pallas_call(lanczos_kernel, out_shape=jax.ShapeDtypeStruct((layers, 2...]
    all_to_all x1, blocking collectives: 20.2 us -> 34.7 us  [shards(): arrived = lax.all_to_all(right_out, 'sec', 0, 0, tiled=True)]
    gather x6 -> x0, local copies, waits for them, and re-layouts: 13.3 us -> none  [the longest x2 5.56 us: apply_operator(): jnp.take(half_term, send_source, axis=0)]
    dot_general x4 -> x0, matrix products: 10.5 us -> none  [the longest x2 5.82 us: apply_operator(): jnp.einsum('kwac,wkdc->kad', arrived, right_terms, preferred_element_type...]
    all_to_all x3 -> x4, waiting for transfers between devices: 80.7 us -> 71.3 us  [the longest x1 27.9 us: shards(): right_terms = lax.all_to_all(ordered, 'mpo', 0, 0, tiled=True)]
    reduce_sum x7 -> x1, other arithmetic: 8.88 us -> 0.02 us  [shards(): line = jnp.sum(pieces[:, 2 * rows:, :], axis=0)]
  transfers between devices with their start and end apart: 5 -> 4, of which waited for: 5 -> 4; matrix products, arithmetic and copies ran while one was open for 0% -> 0% of each run, Pallas kernels for 0% -> 1%
where the time goes in v1:
time: 150 us; the launch traced here: 149 us
  waiting for transfers between devices  71.3 us (48%)
  blocking collectives  34.7 us (23%)
  starting transfers between devices  21.2 us (14%)
  Pallas kernels  15.1 us (10%)
  local copies, waits for them, and re-layouts  6.02 us (4%)
    all_to_all x1, blocking collectives, shards(): arrived = lax.all_to_all(right_out, 'sec', 0, 0, tiled=True)  34.7 us
    all_to_all x1, waiting for transfers between devices, shards(): right_terms = lax.all_to_all(ordered, 'mpo', 0, 0, tiled=True)  27.9 us
    all_to_all x1, waiting for transfers between devices, shards(): left_terms = lax.all_to_all(left_out, 'mpo', 0, 0, tiled=True)  26.2 us
    all_to_all x1, starting transfers between devices, shards(): left_terms = lax.all_to_all(left_out, 'mpo', 0, 0, tiled=True)  10.6 us
    all_to_all x1, waiting for transfers between devices, shards(): pieces = lax.all_to_all(pieces, 'mpo', 0, 0, tiled=True)  10.3 us
    all_to_all x1, waiting for transfers between devices, shards(): lax.all_to_all(jnp.broadcast_to(line[None], (devices, 8, width)), 'sec',...  6.88 us
    pallas_call x1, Pallas kernels, shards(): pl.pallas_call(lanczos_kernel, out_shape=jax.ShapeDtypeStruct((layers, 2...  6.25 us
    pallas_call x1, Pallas kernels, shards(): pl.pallas_call(pack_kernel, out_shape=(jax.ShapeDtypeStruct((devices, SLO...  5.23 us
  transfers between devices with their start and end apart: 4, of which 4 were waited for; matrix products, arithmetic and copies ran while one was open for 0% of the time, Pallas kernels for 1%

profile of v1, /device:TPU:1, one launch (start us, length us, event | category | flops | bytes accessed | tf_op | source)
XLA Modules:
  0.0 149.2 jit_solution(4722730511135029142)
XLA Ops:
  0.6 0.0 copy-start
  0.6 0.0 copy-start.3
  0.7 1.3 copy-done.3
  1.9 0.0 copy-start.4
  1.9 1.2 copy-done.4
  3.2 0.0 copy-start.5
  3.2 0.7 copy-done.5
  3.8 0.0 copy-start.9
  3.8 0.7 copy-done.9
  4.5 5.2 %pack.1 = (bf16[16,2,2,128,128]{4,3,2,1,0:T(8,128)(2,1)S(1)}, bf16[16,272,128]{2,1,0:T(8,128)(2,1)S(1)}) custom-call(s32[256]{0:T(256)S(1)} %copy-done.5, f32[2]{0:T(128)S(1)} %copy-done.9, bf16[2,16,128,128]{3,2,1,0:T(8,128)(2,1)S(1)} %copy-done.3, bf16[2,16,128,128]{3,2,1,0:T(8,128)(2,1)S(1)} %copy-done.4), custom_call_target="tpu_custom_call" | custom-call | tf_op jit(solution)/shard_map/pack/pallas_call | solution.py:202
  9.7 0.0 copy-start.2
  9.7 34.7 %all_to_all.25.arrived = bf16[16,2,2,128,128]{4,3,2,1,0:T(8,128)(2,1)S(1)} all-to-all(bf16[16,2,2,128,128]{4,3,2,1,0:T(8,128)(2,1)S(1)} %get-tuple-element.9), channel_id=1, replica_groups=mesh['sec'=16,'mpo'=16] {'sec'}, dimensions={0} | all-to-all | bytes 4194304 | tf_op jit(solution)/shard_map/right_over_sec/all_to_all | solution.py:214
  44.5 0.0 copy-done.2
  44.5 0.0 copy-start.6
  44.5 10.6 %all-to-all-start = ((bf16[16,272,128]{2,1,0:T(8,128)(2,1)}), bf16[16,272,128]{2,1,0:T(8,128)(2,1)}, u32[]{:S(2)}, u32[]{:S(2)}) async-start(bf16[16,272,128]{2,1,0:T(8,128)(2,1)} %copy-done.2), calls=%async_computation | async-start | bytes 2228224 | tf_op jit(solution)/shard_map/left_over_mpo/all_to_all | solution.py:216
  55.1 0.0 copy-done.6
  55.1 0.0 copy-start.7
  55.1 0.0 copy-start.8
  55.1 2.1 %order.1 = bf16[16,2,128,128]{3,2,1,0:T(8,128)(2,1)S(1)} custom-call(s32[256]{0:T(256)S(1)} %copy-done.6, bf16[16,2,2,128,128]{4,3,2,1,0:T(8,128)(2,1)S(1)} %all_to_all.25.arrived), custom_call_target="tpu_custom_call" | custom-call | tf_op jit(solution)/shard_map/order/pallas_call | solution.py:218
  57.3 0.0 copy-start.1
  57.3 1.0 copy-done.1
  58.2 26.2 %all-to-all-done.left_terms = bf16[16,272,128]{2,1,0:T(8,128)(2,1)} async-done(((bf16[16,272,128]{2,1,0:T(8,128)(2,1)}), bf16[16,272,128]{2,1,0:T(8,128)(2,1)}, u32[]{:S(2)}, u32[]{:S(2)}) %all-to-all-start) | async-done | bytes 1114144 | tf_op jit(solution)/shard_map/left_over_mpo/all_to_all | solution.py:216
  84.4 3.6 %all-to-all-start.2 = ((bf16[16,2,128,128]{3,2,1,0:T(8,128)(2,1)}), bf16[16,2,128,128]{3,2,1,0:T(8,128)(2,1)S(1)}, u32[]{:S(2)}, u32[]{:S(2)}) async-start(bf16[16,2,128,128]{3,2,1,0:T(8,128)(2,1)} %copy-done.1), calls=%async_computation.2 | async-start | bytes 2097152 | tf_op jit(solution)/shard_map/right_over_mpo/all_to_all | solution.py:227
  88.0 0.0 copy-done
  88.1 27.9 %all-to-all-done.2.right_terms = bf16[16,2,128,128]{3,2,1,0:T(8,128)(2,1)S(1)} async-done(((bf16[16,2,128,128]{3,2,1,0:T(8,128)(2,1)}), bf16[16,2,128,128]{3,2,1,0:T(8,128)(2,1)S(1)}, u32[]{:S(2)}, u32[]{:S(2)}) %all-to-all-start.2) | async-done | bytes 1048608 | tf_op jit(solution)/shard_map/right_over_mpo/all_to_all | solution.py:227
  116.0 0.0 copy-done.7
  116.0 0.0 copy-done.8
  116.0 6.2 %lanczos.1 = f32[16,24,128]{2,1,0:T(8,128)} custom-call(s32[16]{0:T(128)S(1)} %copy-done.8, s32[256]{0:T(256)S(1)} %copy-done.7, s32[256]{0:T(256)S(1)} %copy-done.6, bf16[1,128,128]{2,1,0:T(8,128)(2,1)S(1)} %constant_dynamic-slice_fusion.vector, bf16[16,272,128]{2,1,0:T(8,128)(2,1)} %all-to-all-done.left_terms, ...), custom_call_target="tpu_custom_call" | custom-call | tf_op jit(solution)/shard_map/lanczos/pallas_call | solution.py:230
  122.2 3.5 %all-to-all-start.3 = ((f32[16,24,128]{2,1,0:T(8,128)}), f32[16,24,128]{2,1,0:T(8,128)S(1)}, u32[]{:S(2)}, u32[]{:S(2)}) async-start(f32[16,24,128]{2,1,0:T(8,128)} %lanczos.1), calls=%async_computation.3 | async-start | bytes 393216 | tf_op jit(solution)/shard_map/rows_over_mpo/all_to_all | solution.py:238
  125.8 10.3 %all-to-all-done.3.pieces = f32[16,24,128]{2,1,0:T(8,128)S(1)} async-done(((f32[16,24,128]{2,1,0:T(8,128)}), f32[16,24,128]{2,1,0:T(8,128)S(1)}, u32[]{:S(2)}, u32[]{:S(2)}) %all-to-all-start.3) | async-done | bytes 196640 | tf_op jit(solution)/shard_map/rows_over_mpo/all_to_all | solution.py:238
  136.1 0.6 broadcast_in_dim.2
  136.7 3.5 %all-to-all-start.4 = ((f32[16,8,128]{2,1,0:T(8,128)}), f32[16,8,128]{2,1,0:T(8,128)S(1)}, u32[]{:S(2)}, u32[]{:S(2)}) async-start(f32[16,8,128]{2,1,0:T(8,128)} %broadcast_in_dim.2), calls=%async_computation.4 | async-start | bytes 131072 | tf_op jit(solution)/shard_map/numbers_over_sec/all_to_all | solution.py:241
  140.3 6.9 %all-to-all-done.4.shared = f32[16,8,128]{2,1,0:T(8,128)S(1)} async-done(((f32[16,8,128]{2,1,0:T(8,128)}), f32[16,8,128]{2,1,0:T(8,128)S(1)}, u32[]{:S(2)}, u32[]{:S(2)}) %all-to-all-start.4) | async-done | bytes 65568 | tf_op jit(solution)/shard_map/numbers_over_sec/all_to_all | solution.py:241
  147.2 1.5 %finish.1 = (f32[16,8,128]{2,1,0:T(8,128)}, f32[16,8,128]{2,1,0:T(8,128)}, f32[1,128]{1,0:T(1,128)S(1)}) custom-call(s32[16]{0:T(128)S(1)} %copy-done.8, s32[256]{0:T(256)S(1)} %copy-done.7, s32[256]{0:T(256)S(1)} %copy-done.6, bf16[16,8,128]{2,1,0:T(8,128)(2,1)S(1)} %constant_dynamic-slice_fusion.1.vector, f32[16,24,128]{2,1,0:T(8,128)S(1)} %all-to-all-done.3.pieces, ...), custom_call_target="tpu_custom_call" | custom-call | tf_op jit(solution)/shard_map/finish/pallas_call | solution.py:244
  148.7 0.5 slice_bitcast_fusion
  (3 shorter events, 0.0 us)
Async XLA Ops:
  0.6 87.4 %copy-start = (bf16[16,128,128]{2,1,0:T(8,128)(2,1)S(1)}, bf16[16,128,128]{2,1,0:T(8,128)(2,1)}, u32[]{:S(2)}) copy-start(bf16[16,128,128]{2,1,0:T(8,128)(2,1)} %param.7) | copy-start | bytes 1572868
  0.6 1.3 copy-start.3
  1.9 1.2 copy-start.4
  3.2 0.7 copy-start.5
  3.8 0.7 copy-start.9
  9.7 34.8 %copy-start.2 = (bf16[16,272,128]{2,1,0:T(8,128)(2,1)}, bf16[16,272,128]{2,1,0:T(8,128)(2,1)S(1)}, u32[]{:S(2)}) copy-start(bf16[16,272,128]{2,1,0:T(8,128)(2,1)S(1)} %get-tuple-element.8) | copy-start | bytes 3342340
  44.5 10.6 %copy-start.6 = (s32[256]{0:T(256)S(1)}, s32[256]{0:T(256)}, u32[]{:S(2)}) copy-start(s32[256]{0:T(256)} %right_sector.7) | copy-start | bytes 3076
  44.5 39.9 %all-to-all-start = ((bf16[16,272,128]{2,1,0:T(8,128)(2,1)}), bf16[16,272,128]{2,1,0:T(8,128)(2,1)}, u32[]{:S(2)}, u32[]{:S(2)}) async-start(bf16[16,272,128]{2,1,0:T(8,128)(2,1)} %copy-done.2), calls=%async_computation | async-start | bytes 2228224 | tf_op jit(solution)/shard_map/left_over_mpo/all_to_all | solution.py:216
  55.1 60.9 %copy-start.7 = (s32[256]{0:T(256)S(1)}, s32[256]{0:T(256)}, u32[]{:S(2)}) copy-start(s32[256]{0:T(256)} %right_size.3) | copy-start | bytes 3076
  55.1 60.9 %copy-start.8 = (s32[16]{0:T(128)S(1)}, s32[16]{0:T(128)}, u32[]{:S(2)}) copy-start(s32[16]{0:T(128)} %left_size.3) | copy-start | bytes 196
  57.3 1.0 copy-start.1
  84.4 31.5 %all-to-all-start.2 = ((bf16[16,2,128,128]{3,2,1,0:T(8,128)(2,1)}), bf16[16,2,128,128]{3,2,1,0:T(8,128)(2,1)S(1)}, u32[]{:S(2)}, u32[]{:S(2)}) async-start(bf16[16,2,128,128]{3,2,1,0:T(8,128)(2,1)} %copy-done.1), calls=%async_computation.2 | async-start | bytes 2097152 | tf_op jit(solution)/shard_map/right_over_mpo/all_to_all | solution.py:227
  122.2 13.9 %all-to-all-start.3 = ((f32[16,24,128]{2,1,0:T(8,128)}), f32[16,24,128]{2,1,0:T(8,128)S(1)}, u32[]{:S(2)}, u32[]{:S(2)}) async-start(f32[16,24,128]{2,1,0:T(8,128)} %lanczos.1), calls=%async_computation.3 | async-start | bytes 393216 | tf_op jit(solution)/shard_map/rows_over_mpo/all_to_all | solution.py:238
  136.7 10.4 %all-to-all-start.4 = ((f32[16,8,128]{2,1,0:T(8,128)}), f32[16,8,128]{2,1,0:T(8,128)S(1)}, u32[]{:S(2)}, u32[]{:S(2)}) async-start(f32[16,8,128]{2,1,0:T(8,128)} %broadcast_in_dim.2), calls=%async_computation.4 | async-start | bytes 131072 | tf_op jit(solution)/shard_map/numbers_over_sec/all_to_all | solution.py:241

commit v2 on v1

--- a/solution.py
+++ b/solution.py
@@ -13,10 +13,39 @@
 MIB = 1024 * 1024
 
 
-def pack_kernel(right_sector, weights, left_env, right_env, right_out, left_out, wbuf, sem):
-    terms, blocks, width, _ = left_env.shape
+def pack_right_kernel(right_sector, right_env, right_out, stage, sem):
+    blocks = right_env.shape[1]
     devices = right_out.shape[0]
     sec = lax.axis_index("sec")
+    load = pltpu.make_async_copy(right_env, stage, sem.at[0])
+    load.start()
+    picks = []
+    for t in range(devices):
+        first = jnp.int32(-1)
+        last = jnp.int32(0)
+        for i in range(blocks):
+            sector = right_sector[t * blocks + i]
+            match = sector // blocks == sec
+            local = sector % blocks
+            first = jnp.where(match & (first < 0), local, first)
+            last = jnp.where(match, local, last)
+        picks.append((jnp.maximum(first, 0), last))
+    load.wait()
+    copies = []
+    for t in range(devices):
+        for k in range(SLOTS):
+            copies.append(pltpu.make_async_copy(stage.at[:, picks[t][k]], right_out.at[t, k], sem.at[1]))
+            copies[-1].start()
+    for copy in copies:
+        copy.wait()
+
+
+def pack_left_kernel(weights, left_env, kept, given, stage, wbuf, sem):
+    terms, _, width, _ = left_env.shape
+    chips = kept.shape[0]
+    own = lax.axis_index("mpo")
+    load = pltpu.make_async_copy(left_env, stage, sem.at[0])
+    load.start()
     row = lax.broadcasted_iota(jnp.int32, wbuf.shape, 0)
     vals = jnp.zeros(wbuf.shape, F32)
     for w in range(terms):
@@ -27,32 +56,34 @@
         for j, part in enumerate((high, mid, low)):
             vals = jnp.where(row == w * 3 + j, part, vals)
     wbuf[...] = vals.astype(BF16)
+    load.wait()
     copies = []
-    for q in range(blocks):
-        for w in range(terms):
-            copies.append(pltpu.make_async_copy(left_env.at[w, q], left_out.at[q, pl.ds(w * width, width)], sem.at[0]))
-        copies.append(pltpu.make_async_copy(wbuf, left_out.at[q, pl.ds(terms * width, PAD)], sem.at[0]))
+    for d in range(chips):
+        chip = (own // 2 + d) % chips
+        for target, core in ((kept, own % 2), (given, 1 - own % 2)):
+            q = 2 * chip + core
+            for w in range(terms):
+                copies.append(pltpu.make_async_copy(stage.at[w, q], target.at[d, pl.ds(w * width, width)], sem.at[1]))
+            copies.append(pltpu.make_async_copy(wbuf, target.at[d, pl.ds(terms * width, PAD)], sem.at[1]))
     for copy in copies:
         copy.start()
-    for t in range(devices):
-        first = jnp.int32(-1)
-        last = jnp.int32(0)
-        for i in range(blocks):
-            sector = right_sector[t * blocks + i]
-            match = sector // blocks == sec
-            local = sector % blocks
-            first = jnp.where(match & (first < 0), local, first)
-            last = jnp.where(match, local, last)
-        first = jnp.maximum(first, 0)
-        for k, index in enumerate((first, last)):
-            copy = pltpu.make_async_copy(right_env.at[:, index], right_out.at[t, k], sem.at[1])
-            copy.start()
-            copies.append(copy)
     for copy in copies:
         copy.wait()
 
 
-def order_kernel(right_sector, arrived, ordered, sem):
+def pair_kernel(kept, taken, *rest):
+    *pairs, sem = rest
+    copies = []
+    for d, pair in enumerate(pairs):
+        for half, source in enumerate((kept, taken)):
+            copies.append(pltpu.make_async_copy(source.at[d], pair.at[half], sem))
+            copies[-1].start()
+    for copy in copies:
+        copy.wait()
+
+
+def order_kernel(right_sector, arrived, *rest):
+    *_, ordered, sem = rest
     blocks = ordered.shape[0]
     sec = lax.axis_index("sec")
     sources = [right_sector[sec * blocks + q] // blocks for q in range(blocks)]
@@ -78,9 +109,10 @@
     return jnp.sum(jnp.sum(x, axis=0, keepdims=True), axis=1, keepdims=True)
 
 
-def lanczos_kernel(left_size, right_size, right_sector, vector, left_terms, right_terms, out):
-    sources, _, width = left_terms.shape
-    terms = right_terms.shape[1]
+def lanczos_kernel(left_size, right_size, right_sector, vector, right_terms, *rest):
+    *left_terms, out = rest
+    sources, terms, width, _ = right_terms.shape
+    chips = len(left_terms)
     sec = lax.axis_index("sec")
     own = lax.axis_index("mpo")
     blocks = left_size.shape[0]
@@ -88,14 +120,16 @@
 
     def apply(block):
         acc = jnp.zeros((width, width), F32)
-        for p in range(sources):
-            half = jnp.dot(left_terms[p, : terms * width], block, preferred_element_type=F32)
-            scale = left_terms[p, terms * width :].astype(F32)
+        for move in range(sources):
+            step, side = move // 2, move % 2
+            source = 2 * ((own // 2 + chips - step) % chips) + (own % 2 + side) % 2
+            half = jnp.dot(left_terms[step][side, : terms * width], block, preferred_element_type=F32)
+            scale = left_terms[step][side, terms * width :].astype(F32)
             for w in range(terms):
                 weight = scale[3 * w : 3 * w + 1] + scale[3 * w + 1 : 3 * w + 2] + scale[3 * w + 2 : 3 * w + 3]
                 term = (weight * half[w * width : (w + 1) * width]).astype(BF16)
                 acc = acc + lax.dot_general(
-                    term, right_terms[p, w], (((1,), (1,)), ((), ())), preferred_element_type=F32
+                    term, right_terms[source, w], (((1,), (1,)), ((), ())), preferred_element_type=F32
                 )
         return jnp.where(mask, acc, 0.0)
 
@@ -198,31 +232,57 @@
     scalars = pl.BlockSpec(memory_space=pltpu.SMEM)
     vmem = pl.BlockSpec(memory_space=pltpu.VMEM)
 
-    with jax.named_scope("pack"):
-        right_out, left_out = pl.pallas_call(
-            pack_kernel,
-            out_shape=(
-                jax.ShapeDtypeStruct((devices, SLOTS, terms, width, width), BF16),
-                jax.ShapeDtypeStruct((blocks, terms * width + PAD, width), BF16),
-            ),
-            in_specs=[scalars, scalars, anywhere, anywhere],
-            out_specs=(anywhere, anywhere),
-            scratch_shapes=[pltpu.VMEM((PAD, width), BF16), pltpu.SemaphoreType.DMA((2,))],
-            compiler_params=pltpu.CompilerParams(vmem_limit_bytes=4 * MIB),
-        )(right_sector, term_weights, left_environment, right_environment)
+    chips = layers // 2
+    long = terms * width + PAD
+    with jax.named_scope("pack_right"):
+        right_out = pl.pallas_call(
+            pack_right_kernel,
+            out_shape=jax.ShapeDtypeStruct((devices, SLOTS, terms, width, width), BF16),
+            in_specs=[scalars, anywhere],
+            out_specs=anywhere,
+            scratch_shapes=[pltpu.VMEM(right_environment.shape, BF16), pltpu.SemaphoreType.DMA((2,))],
+            compiler_params=pltpu.CompilerParams(vmem_limit_bytes=60 * MIB),
+        )(right_sector, right_environment)
     with jax.named_scope("right_over_sec"):
         arrived = lax.all_to_all(right_out, "sec", 0, 0, tiled=True)
-    with jax.named_scope("left_over_mpo"):
-        left_terms = lax.all_to_all(left_out, "mpo", 0, 0, tiled=True)
+    with jax.named_scope("pack_left"):
+        kept, given = pl.pallas_call(
+            pack_left_kernel,
+            out_shape=(jax.ShapeDtypeStruct((chips, long, width), BF16),) * 2,
+            in_specs=[scalars, anywhere],
+            out_specs=(anywhere, anywhere),
+            scratch_shapes=[
+                pltpu.VMEM(left_environment.shape, BF16),
+                pltpu.VMEM((PAD, width), BF16),
+                pltpu.SemaphoreType.DMA((2,)),
+            ],
+            compiler_params=pltpu.CompilerParams(vmem_limit_bytes=8 * MIB),
+        )(term_weights, left_environment)
+    with jax.named_scope("left_over_core"):
+        taken = lax.ppermute(given, "mpo", [(p, p ^ 1) for p in range(layers)])
+    with jax.named_scope("pair"):
+        pairs = pl.pallas_call(
+            pair_kernel,
+            out_shape=(jax.ShapeDtypeStruct((2, long, width), BF16),) * chips,
+            in_specs=[anywhere, anywhere],
+            out_specs=(anywhere,) * chips,
+            scratch_shapes=[pltpu.SemaphoreType.DMA],
+            compiler_params=pltpu.CompilerParams(vmem_limit_bytes=4 * MIB),
+        )(kept, taken)
+    with jax.named_scope("left_over_z"):
+        left_terms = list(pairs)
+        for d in sorted(range(1, chips), key=lambda d: -min(d, chips - d)):
+            route = [(p, (p + 2 * d) % layers) for p in range(layers)]
+            left_terms[d] = lax.ppermute(pairs[d], "mpo", route)
     with jax.named_scope("order"):
         ordered = pl.pallas_call(
             order_kernel,
             out_shape=jax.ShapeDtypeStruct((blocks, terms, width, width), BF16),
-            in_specs=[scalars, anywhere],
+            in_specs=[scalars] + [anywhere] * chips,
             out_specs=anywhere,
             scratch_shapes=[pltpu.SemaphoreType.DMA],
             compiler_params=pltpu.CompilerParams(vmem_limit_bytes=4 * MIB),
-        )(right_sector, arrived)
+        )(right_sector, arrived, *left_terms[1:])
     with jax.named_scope("right_over_mpo"):
         right_terms = lax.all_to_all(ordered, "mpo", 0, 0, tiled=True)
     with jax.named_scope("lanczos"):
@@ -230,10 +290,10 @@
         pieces = pl.pallas_call(
             lanczos_kernel,
             out_shape=jax.ShapeDtypeStruct((layers, 2 * rows + 8, width), F32),
-            in_specs=[scalars, scalars, scalars, vmem, vmem, vmem],
+            in_specs=[scalars, scalars, scalars, vmem, vmem] + [vmem] * chips,
             out_specs=vmem,
             compiler_params=pltpu.CompilerParams(vmem_limit_bytes=16 * MIB),
-        )(left_size, right_size, right_sector, vector, left_terms, right_terms)
+        )(left_size, right_size, right_sector, vector, right_terms, *left_terms)
     with jax.named_scope("rows_over_mpo"):
         pieces = lax.all_to_all(pieces, "mpo", 0, 0, tiled=True)
     with jax.named_scope("numbers_over_sec"):

time: 150 us -> 131 us (0.87)
  blocking collectives: 34.7 us -> 0 us
  starting transfers between devices: 21.2 us -> 42.8 us
  waiting for transfers between devices: 71.3 us -> 64.1 us
  Pallas kernels: 15.1 us -> 16.8 us
    all_to_all x1 -> x0, blocking collectives: 34.7 us -> none  [shards(): arrived = lax.all_to_all(right_out, 'sec', 0, 0, tiled=True)]
    all_to_all x1, waiting for transfers between devices: 26.2 us -> 0.01 us  [shards(): arrived = lax.all_to_all(right_out, 'sec', 0, 0, tiled=True)]
    ppermute x0 -> x8, waiting for transfers between devices: none -> 19.4 us  [the longest x7 17.8 us: shards(): left_terms[d] = lax.ppermute(pairs[d], 'mpo', route)]
    ppermute x0 -> x8, starting transfers between devices: none -> 18.7 us  [the longest x7 17.7 us: shards(): left_terms[d] = lax.ppermute(pairs[d], 'mpo', route)]
    all_to_all x1, starting transfers between devices: 3.5 us -> 6.93 us  [shards(): lax.all_to_all(jnp.broadcast_to(line[None], (devices, 8, width)), 'sec',...]
    all_to_all x1, starting transfers between devices: 10.6 us -> 7.6 us  [shards(): arrived = lax.all_to_all(right_out, 'sec', 0, 0, tiled=True)]
    all_to_all x1, starting transfers between devices: 3.61 us -> 5.99 us  [shards(): right_terms = lax.all_to_all(ordered, 'mpo', 0, 0, tiled=True)]
    pallas_call x1 -> x3, Pallas kernels: 5.23 us -> 7.54 us  [the longest x1 3.97 us: shards(): pl.pallas_call(pack_right_kernel, out_shape=jax.ShapeDtypeStruct((devices...]
  transfers between devices with their start and end apart: 4 -> 12, of which waited for: 4 -> 8; matrix products, arithmetic and copies ran while one was open for 0% -> 0% of each run, Pallas kernels for 1% -> 3%
where the time goes in v2:
time: 131 us; the launch traced here: 130 us
  waiting for transfers between devices  64.1 us (49%)
  starting transfers between devices  42.8 us (33%)
  Pallas kernels  16.8 us (13%)
  local copies, waits for them, and re-layouts  5.65 us (4%)
    all_to_all x1, waiting for transfers between devices, shards(): right_terms = lax.all_to_all(ordered, 'mpo', 0, 0, tiled=True)  27.9 us
    ppermute x7, waiting for transfers between devices, shards(): left_terms[d] = lax.ppermute(pairs[d], 'mpo', route)  17.8 us
    ppermute x7, starting transfers between devices, shards(): left_terms[d] = lax.ppermute(pairs[d], 'mpo', route)  17.7 us
    all_to_all x1, waiting for transfers between devices, shards(): pieces = lax.all_to_all(pieces, 'mpo', 0, 0, tiled=True)  10.3 us
    all_to_all x1, starting transfers between devices, shards(): arrived = lax.all_to_all(right_out, 'sec', 0, 0, tiled=True)  7.6 us
    all_to_all x1, starting transfers between devices, shards(): lax.all_to_all(jnp.broadcast_to(line[None], (devices, 8, width)), 'sec',...  6.93 us
    all_to_all x1, waiting for transfers between devices, shards(): lax.all_to_all(jnp.broadcast_to(line[None], (devices, 8, width)), 'sec',...  6.51 us
    all_to_all x1, starting transfers between devices, shards(): right_terms = lax.all_to_all(ordered, 'mpo', 0, 0, tiled=True)  5.99 us
  transfers between devices with their start and end apart: 12, of which 8 were waited for; matrix products, arithmetic and copies ran while one was open for 0% of the time, Pallas kernels for 3%

profile of v2, /device:TPU:1, one launch (start us, length us, event | category | flops | bytes accessed | tf_op | source)
XLA Modules:
  0.0 130.2 jit_solution(3785149946843972093)
XLA Ops:
  0.6 0.0 copy-start
  0.6 4.0 %pack_right.1 = bf16[16,2,2,128,128]{4,3,2,1,0:T(8,128)(2,1)} custom-call(s32[256]{0:T(256)} %right_sector.7, bf16[2,16,128,128]{3,2,1,0:T(8,128)(2,1)} %right_env.1), custom_call_target="tpu_custom_call" | custom-call | tf_op jit(solution)/shard_map/pack_right/pallas_call | solution.py:238
  4.6 0.0 copy-start.11
  4.6 7.6 %all-to-all-start = ((bf16[16,2,2,128,128]{4,3,2,1,0:T(8,128)(2,1)}), bf16[16,2,2,128,128]{4,3,2,1,0:T(8,128)(2,1)S(1)}, u32[]{:S(2)}, u32[]{:S(2)}) async-start(bf16[16,2,2,128,128]{4,3,2,1,0:T(8,128)(2,1)} %pack_right.1), calls=%async_computation | async-start | bytes 4194304 | tf_op jit(solution)/shard_map/right_over_sec/all_to_all | solution.py:247
  12.2 0.0 copy-done.11
  12.3 0.0 copy-start.2
  12.3 1.2 copy-done.2
  13.5 2.2 %pack_left.1 = (bf16[8,272,128]{2,1,0:T(8,128)(2,1)S(1)}, bf16[8,272,128]{2,1,0:T(8,128)(2,1)S(1)}) custom-call(f32[2]{0:T(128)S(1)} %copy-done.11, bf16[2,16,128,128]{3,2,1,0:T(8,128)(2,1)S(1)} %copy-done.2), custom_call_target="tpu_custom_call" | custom-call | tf_op jit(solution)/shard_map/pack_left/pallas_call | solution.py:249
  15.6 1.0 collective-permute-start
  16.7 1.6 %collective-permute-done.taken = bf16[8,272,128]{2,1,0:T(8,128)(2,1)S(1)} collective-permute-done((bf16[8,272,128]{2,1,0:T(8,128)(2,1)S(1)}, bf16[8,272,128]{2,1,0:T(8,128)(2,1)S(1)}, u32[]{:S(2)}, u32[]{:S(2)}) %collective-permute-start) | collective-permute-done | bytes 557088 | tf_op jit(solution)/shard_map/left_over_core/ppermute | solution.py:262
  18.3 1.4 %pair.1 = (bf16[2,272,128]{2,1,0:T(8,128)(2,1)S(1)}, bf16[2,272,128]{2,1,0:T(8,128)(2,1)S(1)}, bf16[2,272,128]{2,1,0:T(8,128)(2,1)S(1)}, bf16[2,272,128]{2,1,0:T...) custom-call(bf16[8,272,128]{2,1,0:T(8,128)(2,1)S(1)} %get-tuple-elem, ...), custom_call_target="tpu_custom_call" | custom-call | tf_op jit(solution)/shard_map/pair/pallas_call | solution.py:264
  19.7 0.0 copy-start.6
  19.7 0.6 copy-done.6
  20.3 1.6 %collective-permute-start.1 = (bf16[2,272,128]{2,1,0:T(8,128)(2,1)S(1)}, bf16[2,272,128]{2,1,0:T(8,128)(2,1)S(1)}, u32[]{:S(2)}, u32[]{:S(2)}) collective-permute-start(bf16[2,272,128]{2,1,0:T(8,128)(2,1)S(1)} %get-tuple-element.18), channel_id=1, source_target_pairs={{0,2},{1,3},{2,4},{3,5},{4,6},{5,7},{6,8},{7,9},{8,10},{9,11},{10,... | collective-permute-start | bytes 417800 | tf_op jit(solution)/shard_map/left_over_z/ppermute | solution.py:276
  22.0 3.0 %collective-permute-start.2 = (bf16[2,272,128]{2,1,0:T(8,128)(2,1)S(1)}, bf16[2,272,128]{2,1,0:T(8,128)(2,1)S(1)}, u32[]{:S(2)}, u32[]{:S(2)}) collective-permute-start(bf16[2,272,128]{2,1,0:T(8,128)(2,1)S(1)} %get-tuple-element.19), channel_id=1, source_target_pairs={{0,4},{1,5},{2,6},{3,7},{4,8},{5,9},{6,10},{7,11},{8,12},{9,13},{1... | collective-permute-start | bytes 417800 | tf_op jit(solution)/shard_map/left_over_z/ppermute | solution.py:276
  25.0 3.8 %collective-permute-start.3 = (bf16[2,272,128]{2,1,0:T(8,128)(2,1)S(1)}, bf16[2,272,128]{2,1,0:T(8,128)(2,1)S(1)}, u32[]{:S(2)}, u32[]{:S(2)}) collective-permute-start(bf16[2,272,128]{2,1,0:T(8,128)(2,1)S(1)} %get-tuple-element.20), channel_id=1, source_target_pairs={{0,6},{1,7},{2,8},{3,9},{4,10},{5,11},{6,12},{7,13},{8,14},{9,15},... | collective-permute-start | bytes 417800 | tf_op jit(solution)/shard_map/left_over_z/ppermute | solution.py:276
  28.7 0.5 collective-permute-start.4
  29.2 4.5 %collective-permute-start.5 = (bf16[2,272,128]{2,1,0:T(8,128)(2,1)S(1)}, bf16[2,272,128]{2,1,0:T(8,128)(2,1)S(1)}, u32[]{:S(2)}, u32[]{:S(2)}) collective-permute-start(bf16[2,272,128]{2,1,0:T(8,128)(2,1)S(1)} %get-tuple-element.22), channel_id=1, source_target_pairs={{0,10},{1,11},{2,12},{3,13},{4,14},{5,15},{6,0},{7,1},{8,2},{9,3},... | collective-permute-start | bytes 417800 | tf_op jit(solution)/shard_map/left_over_z/ppermute | solution.py:276
  33.7 0.0 collective-permute-done.1.rest_0_.rest_1_
  33.7 2.4 %collective-permute-start.6 = (bf16[2,272,128]{2,1,0:T(8,128)(2,1)S(1)}, bf16[2,272,128]{2,1,0:T(8,128)(2,1)S(1)}, u32[]{:S(2)}, u32[]{:S(2)}) collective-permute-start(bf16[2,272,128]{2,1,0:T(8,128)(2,1)S(1)} %get-tuple-element.23), channel_id=1, source_target_pairs={{0,12},{1,13},{2,14},{3,15},{4,0},{5,1},{6,2},{7,3},{8,4},{9,5},{1... | collective-permute-start | bytes 417800 | tf_op jit(solution)/shard_map/left_over_z/ppermute | solution.py:276
  36.0 0.0 collective-permute-done.2.rest_1_.rest_2_
  36.0 2.0 %collective-permute-start.7 = (bf16[2,272,128]{2,1,0:T(8,128)(2,1)S(1)}, bf16[2,272,128]{2,1,0:T(8,128)(2,1)S(1)}, u32[]{:S(2)}, u32[]{:S(2)}) collective-permute-start(bf16[2,272,128]{2,1,0:T(8,128)(2,1)S(1)} %get-tuple-element.24), channel_id=1, source_target_pairs={{0,14},{1,15},{2,0},{3,1},{4,2},{5,3},{6,4},{7,5},{8,6},{9,7},{10,... | collective-permute-start | bytes 417800 | tf_op jit(solution)/shard_map/left_over_z/ppermute | solution.py:276
  38.0 7.8 %collective-permute-done.3.rest_2_.rest_3_ = bf16[2,272,128]{2,1,0:T(8,128)(2,1)S(1)} collective-permute-done((bf16[2,272,128]{2,1,0:T(8,128)(2,1)S(1)}, bf16[2,272,128]{2,1,0:T(8,128)(2,1)S(1)}, u32[]{:S(2)}, u32[]{:S(2)}) %collective-permute-start.3) | collective-permute-done | bytes 139296 | tf_op jit(solution)/shard_map/left_over_z/ppermute | solution.py:276
  45.9 1.4 %collective-permute-done.4.rest_3_.rest_4_ = bf16[2,272,128]{2,1,0:T(8,128)(2,1)S(1)} collective-permute-done((bf16[2,272,128]{2,1,0:T(8,128)(2,1)S(1)}, bf16[2,272,128]{2,1,0:T(8,128)(2,1)S(1)}, u32[]{:S(2)}, u32[]{:S(2)}) %collective-permute-start.4) | collective-permute-done | bytes 139296 | tf_op jit(solution)/shard_map/left_over_z/ppermute | solution.py:276
  47.3 0.0 collective-permute-done.5.rest_4_.rest_5_
  47.3 7.7 %collective-permute-done.6.rest_5_.rest_6_ = bf16[2,272,128]{2,1,0:T(8,128)(2,1)S(1)} collective-permute-done((bf16[2,272,128]{2,1,0:T(8,128)(2,1)S(1)}, bf16[2,272,128]{2,1,0:T(8,128)(2,1)S(1)}, u32[]{:S(2)}, u32[]{:S(2)}) %collective-permute-start.6) | collective-permute-done | bytes 139296 | tf_op jit(solution)/shard_map/left_over_z/ppermute | solution.py:276
  55.0 0.9 collective-permute-done.7.rest_6_.rest_7_
  55.8 0.7 copy-done.3
  56.5 0.0 all-to-all-done.arrived
  56.5 0.0 copy-done.8
  56.5 0.9 copy-done.4
  57.4 2.1 %order.1 = bf16[16,2,128,128]{3,2,1,0:T(8,128)(2,1)S(1)} custom-call(s32[256]{0:T(256)S(1)} %copy-done.8, bf16[16,2,2,128,128]{4,3,2,1,0:T(8,128)(2,1)S(1)} %all-to-all-done.arrived, bf16[2,272,128]{2,1,0:T(8,128)(2,1)S(1)} %collective-permute-done.1.rest_0_.rest_1_, bf16[2,272,128]{2,1,0:T(8,128)(2,1)S(1)} %collective-permute-done.2.rest_1_.rest_2_, ...), custom_call_target="tpu_custom_call" | custom-call | tf_op jit(solution)/shard_map/order/pallas_call | solution.py:278
  59.6 0.0 copy-start.1
  59.6 1.0 copy-done.1
  60.6 6.0 %all-to-all-start.1 = ((bf16[16,2,128,128]{3,2,1,0:T(8,128)(2,1)}), bf16[16,2,128,128]{3,2,1,0:T(8,128)(2,1)S(1)}, u32[]{:S(2)}, u32[]{:S(2)}) async-start(bf16[16,2,128,128]{3,2,1,0:T(8,128)(2,1)} %copy-done.1), calls=%async_computation.1 | async-start | bytes 2097152 | tf_op jit(solution)/shard_map/right_over_mpo/all_to_all | solution.py:287
  66.6 0.0 copy-done
  66.6 27.9 %all-to-all-done.1.right_terms = bf16[16,2,128,128]{3,2,1,0:T(8,128)(2,1)S(1)} async-done(((bf16[16,2,128,128]{3,2,1,0:T(8,128)(2,1)}), bf16[16,2,128,128]{3,2,1,0:T(8,128)(2,1)S(1)}, u32[]{:S(2)}, u32[]{:S(2)}) %all-to-all-start.1) | async-done | bytes 1048608 | tf_op jit(solution)/shard_map/right_over_mpo/all_to_all | solution.py:287
  94.5 0.0 copy-done.5
  94.5 0.0 copy-done.7
  94.5 0.0 copy-done.9
  94.5 5.6 %lanczos.1 = f32[16,24,128]{2,1,0:T(8,128)} custom-call(s32[16]{0:T(128)S(1)} %copy-done.10, s32[256]{0:T(256)S(1)} %copy-done.9, s32[256]{0:T(256)S(1)} %copy-done.8, bf16[1,128,128]{2,1,0:T(8,128)(2,1)S(1)} %constant_dynamic-slice_fusion.vector, bf16[16,2,128,128]{3,2,1,0:T(8,128)(2,1)S(1)} %all-to-all-done.1.right_terms, ...), custom_call_target="tpu_custom_call" | custom-call | tf_op jit(solution)/shard_map/lanczos/pallas_call | solution.py:290
  100.1 3.5 %all-to-all-start.2 = ((f32[16,24,128]{2,1,0:T(8,128)}), f32[16,24,128]{2,1,0:T(8,128)S(1)}, u32[]{:S(2)}, u32[]{:S(2)}) async-start(f32[16,24,128]{2,1,0:T(8,128)} %lanczos.1), calls=%async_computation.2 | async-start | bytes 393216 | tf_op jit(solution)/shard_map/rows_over_mpo/all_to_all | solution.py:298
  103.7 10.3 %all-to-all-done.2.pieces = f32[16,24,128]{2,1,0:T(8,128)S(1)} async-done(((f32[16,24,128]{2,1,0:T(8,128)}), f32[16,24,128]{2,1,0:T(8,128)S(1)}, u32[]{:S(2)}, u32[]{:S(2)}) %all-to-all-start.2) | async-done | bytes 196640 | tf_op jit(solution)/shard_map/rows_over_mpo/all_to_all | solution.py:298
  114.0 0.6 broadcast_in_dim.2
  114.6 6.9 %all-to-all-start.3 = ((f32[16,8,128]{2,1,0:T(8,128)}), f32[16,8,128]{2,1,0:T(8,128)S(1)}, u32[]{:S(2)}, u32[]{:S(2)}) async-start(f32[16,8,128]{2,1,0:T(8,128)} %broadcast_in_dim.2), calls=%async_computation.3 | async-start | bytes 131072 | tf_op jit(solution)/shard_map/numbers_over_sec/all_to_all | solution.py:301
  121.6 6.5 %all-to-all-done.3.shared = f32[16,8,128]{2,1,0:T(8,128)S(1)} async-done(((f32[16,8,128]{2,1,0:T(8,128)}), f32[16,8,128]{2,1,0:T(8,128)S(1)}, u32[]{:S(2)}, u32[]{:S(2)}) %all-to-all-start.3) | async-done | bytes 65568 | tf_op jit(solution)/shard_map/numbers_over_sec/all_to_all | solution.py:301
  128.1 1.5 %finish.1 = (f32[16,8,128]{2,1,0:T(8,128)}, f32[16,8,128]{2,1,0:T(8,128)}, f32[1,128]{1,0:T(1,128)S(1)}) custom-call(s32[16]{0:T(128)S(1)} %copy-done.10, s32[256]{0:T(256)S(1)} %copy-done.9, s32[256]{0:T(256)S(1)} %copy-done.8, bf16[16,8,128]{2,1,0:T(8,128)(2,1)S(1)} %constant_dynamic-slice_fusion.1.vector, f32[16,24,128]{2,1,0:T(8,128)S(1)} %all-to-all-done.2.pieces, ...), custom_call_target="tpu_custom_call" | custom-call | tf_op jit(solution)/shard_map/finish/pallas_call | solution.py:304
  129.7 0.5 slice_bitcast_fusion
  (11 shorter events, 0.1 us)
Async XLA Ops:
  0.6 65.9 %copy-start = (bf16[16,128,128]{2,1,0:T(8,128)(2,1)S(1)}, bf16[16,128,128]{2,1,0:T(8,128)(2,1)}, u32[]{:S(2)}) copy-start(bf16[16,128,128]{2,1,0:T(8,128)(2,1)} %param.7) | copy-start | bytes 1572868
  4.6 7.6 %copy-start.11 = (f32[2]{0:T(128)S(1)}, f32[2]{0:T(128)}, u32[]{:S(2)}) copy-start(f32[2]{0:T(128)} %weights.1) | copy-start | bytes 28
  4.6 51.9 %all-to-all-start = ((bf16[16,2,2,128,128]{4,3,2,1,0:T(8,128)(2,1)}), bf16[16,2,2,128,128]{4,3,2,1,0:T(8,128)(2,1)S(1)}, u32[]{:S(2)}, u32[]{:S(2)}) async-start(bf16[16,2,2,128,128]{4,3,2,1,0:T(8,128)(2,1)} %pack_right.1), calls=%async_computation | async-start | bytes 4194304 | tf_op jit(solution)/shard_map/right_over_sec/all_to_all | solution.py:247
  12.3 1.2 copy-start.2
  13.5 43.0 %copy-start.8 = (s32[256]{0:T(256)S(1)}, s32[256]{0:T(256)}, u32[]{:S(2)}) copy-start(s32[256]{0:T(256)} %right_sector.7) | copy-start | bytes 3076
  15.6 2.6 %collective-permute-start = (bf16[8,272,128]{2,1,0:T(8,128)(2,1)S(1)}, bf16[8,272,128]{2,1,0:T(8,128)(2,1)S(1)}, u32[]{:S(2)}, u32[]{:S(2)}) collective-permute-start(bf16[8,272,128]{2,1,0:T(8,128)(2,1)S(1)} %get-tuple-element.17), channel_id=1, source_target_pairs={{0,1},{1,0},{2,3},{3,2},{4,5},{5,4},{6,7},{7,6},{8,9},{9,8},{10,11... | collective-permute-start | bytes 1671176 | tf_op jit(solution)/shard_map/left_over_core/ppermute | solution.py:262
  19.7 0.6 copy-start.6
  20.3 13.3 %collective-permute-start.1 = (bf16[2,272,128]{2,1,0:T(8,128)(2,1)S(1)}, bf16[2,272,128]{2,1,0:T(8,128)(2,1)S(1)}, u32[]{:S(2)}, u32[]{:S(2)}) collective-permute-start(bf16[2,272,128]{2,1,0:T(8,128)(2,1)S(1)} %get-tuple-element.18), channel_id=1, source_target_pairs={{0,2},{1,3},{2,4},{3,5},{4,6},{5,7},{6,8},{7,9},{8,10},{9,11},{10,... | collective-permute-start | bytes 417800 | tf_op jit(solution)/shard_map/left_over_z/ppermute | solution.py:276
  22.0 14.1 %collective-permute-start.2 = (bf16[2,272,128]{2,1,0:T(8,128)(2,1)S(1)}, bf16[2,272,128]{2,1,0:T(8,128)(2,1)S(1)}, u32[]{:S(2)}, u32[]{:S(2)}) collective-permute-start(bf16[2,272,128]{2,1,0:T(8,128)(2,1)S(1)} %get-tuple-element.19), channel_id=1, source_target_pairs={{0,4},{1,5},{2,6},{3,7},{4,8},{5,9},{6,10},{7,11},{8,12},{9,13},{1... | collective-permute-start | bytes 417800 | tf_op jit(solution)/shard_map/left_over_z/ppermute | solution.py:276
  25.0 20.9 %collective-permute-start.3 = (bf16[2,272,128]{2,1,0:T(8,128)(2,1)S(1)}, bf16[2,272,128]{2,1,0:T(8,128)(2,1)S(1)}, u32[]{:S(2)}, u32[]{:S(2)}) collective-permute-start(bf16[2,272,128]{2,1,0:T(8,128)(2,1)S(1)} %get-tuple-element.20), channel_id=1, source_target_pairs={{0,6},{1,7},{2,8},{3,9},{4,10},{5,11},{6,12},{7,13},{8,14},{9,15},... | collective-permute-start | bytes 417800 | tf_op jit(solution)/shard_map/left_over_z/ppermute | solution.py:276
  28.7 18.6 %collective-permute-start.4 = (bf16[2,272,128]{2,1,0:T(8,128)(2,1)S(1)}, bf16[2,272,128]{2,1,0:T(8,128)(2,1)S(1)}, u32[]{:S(2)}, u32[]{:S(2)}) collective-permute-start(bf16[2,272,128]{2,1,0:T(8,128)(2,1)S(1)} %get-tuple-element.21), channel_id=1, source_target_pairs={{0,8},{1,9},{2,10},{3,11},{4,12},{5,13},{6,14},{7,15},{8,0},{9,1},... | collective-permute-start | bytes 417800 | tf_op jit(solution)/shard_map/left_over_z/ppermute | solution.py:276
  29.2 18.1 %collective-permute-start.5 = (bf16[2,272,128]{2,1,0:T(8,128)(2,1)S(1)}, bf16[2,272,128]{2,1,0:T(8,128)(2,1)S(1)}, u32[]{:S(2)}, u32[]{:S(2)}) collective-permute-start(bf16[2,272,128]{2,1,0:T(8,128)(2,1)S(1)} %get-tuple-element.22), channel_id=1, source_target_pairs={{0,10},{1,11},{2,12},{3,13},{4,14},{5,15},{6,0},{7,1},{8,2},{9,3},... | collective-permute-start | bytes 417800 | tf_op jit(solution)/shard_map/left_over_z/ppermute | solution.py:276
  33.7 21.3 %collective-permute-start.6 = (bf16[2,272,128]{2,1,0:T(8,128)(2,1)S(1)}, bf16[2,272,128]{2,1,0:T(8,128)(2,1)S(1)}, u32[]{:S(2)}, u32[]{:S(2)}) collective-permute-start(bf16[2,272,128]{2,1,0:T(8,128)(2,1)S(1)} %get-tuple-element.23), channel_id=1, source_target_pairs={{0,12},{1,13},{2,14},{3,15},{4,0},{5,1},{6,2},{7,3},{8,4},{9,5},{1... | collective-permute-start | bytes 417800 | tf_op jit(solution)/shard_map/left_over_z/ppermute | solution.py:276
  36.0 19.8 %collective-permute-start.7 = (bf16[2,272,128]{2,1,0:T(8,128)(2,1)S(1)}, bf16[2,272,128]{2,1,0:T(8,128)(2,1)S(1)}, u32[]{:S(2)}, u32[]{:S(2)}) collective-permute-start(bf16[2,272,128]{2,1,0:T(8,128)(2,1)S(1)} %get-tuple-element.24), channel_id=1, source_target_pairs={{0,14},{1,15},{2,0},{3,1},{4,2},{5,3},{6,4},{7,5},{8,6},{9,7},{10,... | collective-permute-start | bytes 417800 | tf_op jit(solution)/shard_map/left_over_z/ppermute | solution.py:276
  55.8 0.7 copy-start.3
  56.5 0.9 copy-start.4
  59.6 1.0 copy-start.1
  60.6 33.9 %copy-start.5 = (bf16[2,272,128]{2,1,0:T(8,128)(2,1)S(1)}, bf16[2,272,128]{2,1,0:T(8,128)(2,1)}, u32[]{:S(2)}) copy-start(bf16[2,272,128]{2,1,0:T(8,128)(2,1)} %copy-done.3) | copy-start | bytes 417796
  60.6 33.9 %copy-start.7 = (bf16[2,272,128]{2,1,0:T(8,128)(2,1)S(1)}, bf16[2,272,128]{2,1,0:T(8,128)(2,1)}, u32[]{:S(2)}) copy-start(bf16[2,272,128]{2,1,0:T(8,128)(2,1)} %copy-done.6) | copy-start | bytes 417796
  60.6 33.9 %copy-start.9 = (s32[256]{0:T(256)S(1)}, s32[256]{0:T(256)}, u32[]{:S(2)}) copy-start(s32[256]{0:T(256)} %right_size.3) | copy-start | bytes 3076
  60.6 33.9 %copy-start.10 = (s32[16]{0:T(128)S(1)}, s32[16]{0:T(128)}, u32[]{:S(2)}) copy-start(s32[16]{0:T(128)} %left_size.3) | copy-start | bytes 196
  60.6 33.9 %all-to-all-start.1 = ((bf16[16,2,128,128]{3,2,1,0:T(8,128)(2,1)}), bf16[16,2,128,128]{3,2,1,0:T(8,128)(2,1)S(1)}, u32[]{:S(2)}, u32[]{:S(2)}) async-start(bf16[16,2,128,128]{3,2,1,0:T(8,128)(2,1)} %copy-done.1), calls=%async_computation.1 | async-start | bytes 2097152 | tf_op jit(solution)/shard_map/right_over_mpo/all_to_all | solution.py:287
  100.1 13.8 %all-to-all-start.2 = ((f32[16,24,128]{2,1,0:T(8,128)}), f32[16,24,128]{2,1,0:T(8,128)S(1)}, u32[]{:S(2)}, u32[]{:S(2)}) async-start(f32[16,24,128]{2,1,0:T(8,128)} %lanczos.1), calls=%async_computation.2 | async-start | bytes 393216 | tf_op jit(solution)/shard_map/rows_over_mpo/all_to_all | solution.py:298
  114.6 13.5 %all-to-all-start.3 = ((f32[16,8,128]{2,1,0:T(8,128)}), f32[16,8,128]{2,1,0:T(8,128)S(1)}, u32[]{:S(2)}, u32[]{:S(2)}) async-start(f32[16,8,128]{2,1,0:T(8,128)} %broadcast_in_dim.2), calls=%async_computation.3 | async-start | bytes 131072 | tf_op jit(solution)/shard_map/numbers_over_sec/all_to_all | solution.py:301

commit v3 on v2

--- a/solution.py
+++ b/solution.py
@@ -40,9 +40,10 @@
         copy.wait()
 
 
-def pack_left_kernel(weights, left_env, kept, given, stage, wbuf, sem):
+def pack_left_kernel(weights, left_env, *rest):
+    *pairs, stage, wbuf, sem = rest
     terms, _, width, _ = left_env.shape
-    chips = kept.shape[0]
+    chips = len(pairs)
     own = lax.axis_index("mpo")
     load = pltpu.make_async_copy(left_env, stage, sem.at[0])
     load.start()
@@ -58,45 +59,48 @@
     wbuf[...] = vals.astype(BF16)
     load.wait()
     copies = []
-    for d in range(chips):
+    for d, pair in enumerate(pairs):
         chip = (own // 2 + d) % chips
-        for target, core in ((kept, own % 2), (given, 1 - own % 2)):
-            q = 2 * chip + core
+        for side in range(2):
+            q = 2 * chip + (own % 2 + side) % 2
             for w in range(terms):
-                copies.append(pltpu.make_async_copy(stage.at[w, q], target.at[d, pl.ds(w * width, width)], sem.at[1]))
-            copies.append(pltpu.make_async_copy(wbuf, target.at[d, pl.ds(terms * width, PAD)], sem.at[1]))
+                copies.append(pltpu.make_async_copy(stage.at[w, q], pair.at[side, pl.ds(w * width, width)], sem.at[1]))
+            copies.append(pltpu.make_async_copy(wbuf, pair.at[side, pl.ds(terms * width, PAD)], sem.at[1]))
     for copy in copies:
         copy.start()
     for copy in copies:
         copy.wait()
 
 
-def pair_kernel(kept, taken, *rest):
-    *pairs, sem = rest
+def collect_kernel(*refs):
+    *pairs, given, sem = refs
     copies = []
     for d, pair in enumerate(pairs):
-        for half, source in enumerate((kept, taken)):
-            copies.append(pltpu.make_async_copy(source.at[d], pair.at[half], sem))
-            copies[-1].start()
+        copies.append(pltpu.make_async_copy(pair.at[1], given.at[d], sem))
+        copies[-1].start()
     for copy in copies:
         copy.wait()
 
 
-def order_kernel(right_sector, arrived, *rest):
-    *_, ordered, sem = rest
+def order_kernel(right_sector, arrived, ordered, stage, sem):
     blocks = ordered.shape[0]
     sec = lax.axis_index("sec")
     sources = [right_sector[sec * blocks + q] // blocks for q in range(blocks)]
-    copies = []
+    loads = []
     for q in range(blocks):
         again = jnp.bool_(False)
         for other in range(q):
             again = again | (sources[other] == sources[q])
-        copy = pltpu.make_async_copy(arrived.at[sources[q], jnp.where(again, 1, 0)], ordered.at[q], sem)
-        copy.start()
-        copies.append(copy)
-    for copy in copies:
-        copy.wait()
+        load = pltpu.make_async_copy(arrived.at[sources[q], jnp.where(again, 1, 0)], stage.at[q], sem.at[q])
+        load.start()
+        loads.append(load)
+    stores = []
+    for q in range(blocks):
+        loads[q].wait()
+        stores.append(pltpu.make_async_copy(stage.at[q], ordered.at[q], sem.at[blocks]))
+        stores[-1].start()
+    for store in stores:
+        store.wait()
 
 
 def live(rows, left, right):
@@ -109,7 +113,7 @@
     return jnp.sum(jnp.sum(x, axis=0, keepdims=True), axis=1, keepdims=True)
 
 
-def lanczos_kernel(left_size, right_size, right_sector, vector, right_terms, *rest):
+def lanczos_kernel(left_size, right_size, right_sector, vector, right_terms, taken, *rest):
     *left_terms, out = rest
     sources, terms, width, _ = right_terms.shape
     chips = len(left_terms)
@@ -123,8 +127,9 @@
         for move in range(sources):
             step, side = move // 2, move % 2
             source = 2 * ((own // 2 + chips - step) % chips) + (own % 2 + side) % 2
-            half = jnp.dot(left_terms[step][side, : terms * width], block, preferred_element_type=F32)
-            scale = left_terms[step][side, terms * width :].astype(F32)
+            part = left_terms[step].at[0] if side == 0 else taken.at[step]
+            half = jnp.dot(part[: terms * width], block, preferred_element_type=F32)
+            scale = part[terms * width :].astype(F32)
             for w in range(terms):
                 weight = scale[3 * w : 3 * w + 1] + scale[3 * w + 1 : 3 * w + 2] + scale[3 * w + 2 : 3 * w + 3]
                 term = (weight * half[w * width : (w + 1) * width]).astype(BF16)
@@ -246,11 +251,11 @@
     with jax.named_scope("right_over_sec"):
         arrived = lax.all_to_all(right_out, "sec", 0, 0, tiled=True)
     with jax.named_scope("pack_left"):
-        kept, given = pl.pallas_call(
+        pairs = pl.pallas_call(
             pack_left_kernel,
-            out_shape=(jax.ShapeDtypeStruct((chips, long, width), BF16),) * 2,
+            out_shape=(jax.ShapeDtypeStruct((2, long, width), BF16),) * chips,
             in_specs=[scalars, anywhere],
-            out_specs=(anywhere, anywhere),
+            out_specs=(anywhere,) * chips,
             scratch_shapes=[
                 pltpu.VMEM(left_environment.shape, BF16),
                 pltpu.VMEM((PAD, width), BF16),
@@ -258,31 +263,31 @@
             ],
             compiler_params=pltpu.CompilerParams(vmem_limit_bytes=8 * MIB),
         )(term_weights, left_environment)
-    with jax.named_scope("left_over_core"):
-        taken = lax.ppermute(given, "mpo", [(p, p ^ 1) for p in range(layers)])
-    with jax.named_scope("pair"):
-        pairs = pl.pallas_call(
-            pair_kernel,
-            out_shape=(jax.ShapeDtypeStruct((2, long, width), BF16),) * chips,
-            in_specs=[anywhere, anywhere],
-            out_specs=(anywhere,) * chips,
-            scratch_shapes=[pltpu.SemaphoreType.DMA],
-            compiler_params=pltpu.CompilerParams(vmem_limit_bytes=4 * MIB),
-        )(kept, taken)
     with jax.named_scope("left_over_z"):
         left_terms = list(pairs)
         for d in sorted(range(1, chips), key=lambda d: -min(d, chips - d)):
             route = [(p, (p + 2 * d) % layers) for p in range(layers)]
             left_terms[d] = lax.ppermute(pairs[d], "mpo", route)
+        arrived, *left_terms = lax.optimization_barrier((arrived, *left_terms))
+    with jax.named_scope("left_over_core"):
+        given = pl.pallas_call(
+            collect_kernel,
+            out_shape=jax.ShapeDtypeStruct((chips, long, width), BF16),
+            in_specs=[anywhere] * chips,
+            out_specs=anywhere,
+            scratch_shapes=[pltpu.SemaphoreType.DMA],
+            compiler_params=pltpu.CompilerParams(vmem_limit_bytes=4 * MIB),
+        )(*left_terms)
+        taken = lax.ppermute(given, "mpo", [(p, p ^ 1) for p in range(layers)])
     with jax.named_scope("order"):
         ordered = pl.pallas_call(
             order_kernel,
             out_shape=jax.ShapeDtypeStruct((blocks, terms, width, width), BF16),
-            in_specs=[scalars] + [anywhere] * chips,
+            in_specs=[scalars, anywhere],
             out_specs=anywhere,
-            scratch_shapes=[pltpu.SemaphoreType.DMA],
-            compiler_params=pltpu.CompilerParams(vmem_limit_bytes=4 * MIB),
-        )(right_sector, arrived, *left_terms[1:])
+            scratch_shapes=[pltpu.VMEM((blocks, terms, width, width), BF16), pltpu.SemaphoreType.DMA((blocks + 1,))],
+            compiler_params=pltpu.CompilerParams(vmem_limit_bytes=60 * MIB),
+        )(right_sector, arrived)
     with jax.named_scope("right_over_mpo"):
         right_terms = lax.all_to_all(ordered, "mpo", 0, 0, tiled=True)
     with jax.named_scope("lanczos"):
@@ -290,10 +295,10 @@
         pieces = pl.pallas_call(
             lanczos_kernel,
             out_shape=jax.ShapeDtypeStruct((layers, 2 * rows + 8, width), F32),
-            in_specs=[scalars, scalars, scalars, vmem, vmem] + [vmem] * chips,
+            in_specs=[scalars, scalars, scalars, vmem, vmem, vmem] + [vmem] * chips,
             out_specs=vmem,
             compiler_params=pltpu.CompilerParams(vmem_limit_bytes=16 * MIB),
-        )(left_size, right_size, right_sector, vector, right_terms, *left_terms)
+        )(left_size, right_size, right_sector, vector, right_terms, taken, *left_terms)
     with jax.named_scope("rows_over_mpo"):
         pieces = lax.all_to_all(pieces, "mpo", 0, 0, tiled=True)
     with jax.named_scope("numbers_over_sec"):

time: 131 us -> 123 us (0.939)
  local copies, waits for them, and re-layouts: 5.65 us -> 1.21 us
  starting transfers between devices: 42.8 us -> 40.6 us
    unnamed x24 -> x12, local copies, waits for them, and re-layouts: 4.47 us -> 0.04 us
    all_to_all x1, waiting for transfers between devices: 27.9 us -> 24.9 us  [shards(): right_terms = lax.all_to_all(ordered, 'mpo', 0, 0, tiled=True)]
  transfers between devices with their start and end apart: 12 -> 12, of which waited for: 8 -> 9; matrix products, arithmetic and copies ran while one was open for 0% -> 0% of each run, Pallas kernels for 3% -> 3%
where the time goes in v3:
time: 123 us; the launch traced here: 122 us
  waiting for transfers between devices  62.8 us (51%)
  starting transfers between devices  40.6 us (33%)
  Pallas kernels  17 us (14%)
    all_to_all x1, waiting for transfers between devices, shards(): right_terms = lax.all_to_all(ordered, 'mpo', 0, 0, tiled=True)  24.9 us
    ppermute x7, waiting for transfers between devices, shards(): left_terms[d] = lax.ppermute(pairs[d], 'mpo', route)  19.1 us
    ppermute x7, starting transfers between devices, shards(): left_terms[d] = lax.ppermute(pairs[d], 'mpo', route)  16.5 us
    all_to_all x1, waiting for transfers between devices, shards(): pieces = lax.all_to_all(pieces, 'mpo', 0, 0, tiled=True)  10.3 us
    all_to_all x1, starting transfers between devices, shards(): arrived = lax.all_to_all(right_out, 'sec', 0, 0, tiled=True)  7.78 us
    all_to_all x1, starting transfers between devices, shards(): lax.all_to_all(jnp.broadcast_to(line[None], (devices, 8, width)), 'sec',...  6.6 us
    all_to_all x1, waiting for transfers between devices, shards(): lax.all_to_all(jnp.broadcast_to(line[None], (devices, 8, width)), 'sec',...  6.51 us
    all_to_all x1, starting transfers between devices, shards(): right_terms = lax.all_to_all(ordered, 'mpo', 0, 0, tiled=True)  5.98 us
  transfers between devices with their start and end apart: 12, of which 9 were waited for; matrix products, arithmetic and copies ran while one was open for 0% of the time, Pallas kernels for 3%

profile of v3, /device:TPU:1, one launch (start us, length us, event | category | flops | bytes accessed | tf_op | source)
XLA Modules:
  0.0 122.4 jit_solution(4873855821395030909)
XLA Ops:
  0.6 0.0 copy-start
  0.6 3.9 %pack_right.1 = bf16[16,2,2,128,128]{4,3,2,1,0:T(8,128)(2,1)} custom-call(s32[256]{0:T(256)} %right_sector.7, bf16[2,16,128,128]{3,2,1,0:T(8,128)(2,1)} %right_env.1), custom_call_target="tpu_custom_call" | custom-call | tf_op jit(solution)/shard_map/pack_right/pallas_call | solution.py:243
  4.6 0.0 copy-start.1
  4.6 0.0 copy-start.5
  4.6 7.8 %all-to-all-start = ((bf16[16,2,2,128,128]{4,3,2,1,0:T(8,128)(2,1)}), bf16[16,2,2,128,128]{4,3,2,1,0:T(8,128)(2,1)}, u32[]{:S(2)}, u32[]{:S(2)}) async-start(bf16[16,2,2,128,128]{4,3,2,1,0:T(8,128)(2,1)} %pack_right.1), calls=%async_computation | async-start | bytes 4194304 | tf_op jit(solution)/shard_map/right_over_sec/all_to_all | solution.py:252
  12.4 0.0 copy-done.1
  12.4 0.0 copy-done.5
  12.4 2.3 %pack_left.1 = (bf16[2,272,128]{2,1,0:T(8,128)(2,1)S(1)}, bf16[2,272,128]{2,1,0:T(8,128)(2,1)S(1)}, bf16[2,272,128]{2,1,0:T(8,128)(2,1)S(1)}, bf16[2,272,128]{2,...) custom-call(f32[2]{0:T(128)S(1)} %copy-done.5, ...), custom_call_target="tpu_custom_call" | custom-call | tf_op jit(solution)/shard_map/pack_left/pallas_call | solution.py:254
  14.8 1.7 %collective-permute-start = (bf16[2,272,128]{2,1,0:T(8,128)(2,1)S(1)}, bf16[2,272,128]{2,1,0:T(8,128)(2,1)S(1)}, u32[]{:S(2)}, u32[]{:S(2)}) collective-permute-start(bf16[2,272,128]{2,1,0:T(8,128)(2,1)S(1)} %get-tuple-element.24), channel_id=1, source_target_pairs={{0,2},{1,3},{2,4},{3,5},{4,6},{5,7},{6,8},{7,9},{8,10},{9,11},{10,... | collective-permute-start | bytes 417800 | tf_op jit(solution)/shard_map/left_over_z/ppermute | solution.py:270
  16.5 3.0 %collective-permute-start.1 = (bf16[2,272,128]{2,1,0:T(8,128)(2,1)S(1)}, bf16[2,272,128]{2,1,0:T(8,128)(2,1)S(1)}, u32[]{:S(2)}, u32[]{:S(2)}) collective-permute-start(bf16[2,272,128]{2,1,0:T(8,128)(2,1)S(1)} %get-tuple-element.25), channel_id=1, source_target_pairs={{0,4},{1,5},{2,6},{3,7},{4,8},{5,9},{6,10},{7,11},{8,12},{9,13},{1... | collective-permute-start | bytes 417800 | tf_op jit(solution)/shard_map/left_over_z/ppermute | solution.py:270
  19.5 3.8 %collective-permute-start.2 = (bf16[2,272,128]{2,1,0:T(8,128)(2,1)S(1)}, bf16[2,272,128]{2,1,0:T(8,128)(2,1)S(1)}, u32[]{:S(2)}, u32[]{:S(2)}) collective-permute-start(bf16[2,272,128]{2,1,0:T(8,128)(2,1)S(1)} %get-tuple-element.26), channel_id=1, source_target_pairs={{0,6},{1,7},{2,8},{3,9},{4,10},{5,11},{6,12},{7,13},{8,14},{9,15},... | collective-permute-start | bytes 417800 | tf_op jit(solution)/shard_map/left_over_z/ppermute | solution.py:270
  23.2 0.5 collective-permute-start.3
  23.7 4.5 %collective-permute-start.4 = (bf16[2,272,128]{2,1,0:T(8,128)(2,1)S(1)}, bf16[2,272,128]{2,1,0:T(8,128)(2,1)S(1)}, u32[]{:S(2)}, u32[]{:S(2)}) collective-permute-start(bf16[2,272,128]{2,1,0:T(8,128)(2,1)S(1)} %get-tuple-element.28), channel_id=1, source_target_pairs={{0,10},{1,11},{2,12},{3,13},{4,14},{5,15},{6,0},{7,1},{8,2},{9,3},... | collective-permute-start | bytes 417800 | tf_op jit(solution)/shard_map/left_over_z/ppermute | solution.py:270
  28.2 0.0 collective-permute-done.refs_1_.rest_1_
  28.2 2.4 %collective-permute-start.5 = (bf16[2,272,128]{2,1,0:T(8,128)(2,1)S(1)}, bf16[2,272,128]{2,1,0:T(8,128)(2,1)S(1)}, u32[]{:S(2)}, u32[]{:S(2)}) collective-permute-start(bf16[2,272,128]{2,1,0:T(8,128)(2,1)S(1)} %get-tuple-element.29), channel_id=1, source_target_pairs={{0,12},{1,13},{2,14},{3,15},{4,0},{5,1},{6,2},{7,3},{8,4},{9,5},{1... | collective-permute-start | bytes 417800 | tf_op jit(solution)/shard_map/left_over_z/ppermute | solution.py:270
  30.6 0.0 collective-permute-done.1.refs_2_.rest_2_
  30.6 0.7 collective-permute-start.6
  31.3 6.7 %collective-permute-done.2.refs_3_.rest_3_ = bf16[2,272,128]{2,1,0:T(8,128)(2,1)S(1)} collective-permute-done((bf16[2,272,128]{2,1,0:T(8,128)(2,1)S(1)}, bf16[2,272,128]{2,1,0:T(8,128)(2,1)S(1)}, u32[]{:S(2)}, u32[]{:S(2)}) %collective-permute-start.2) | collective-permute-done | bytes 139296 | tf_op jit(solution)/shard_map/left_over_z/ppermute | solution.py:270
  38.0 2.5 %collective-permute-done.3.refs_4_.rest_4_ = bf16[2,272,128]{2,1,0:T(8,128)(2,1)S(1)} collective-permute-done((bf16[2,272,128]{2,1,0:T(8,128)(2,1)S(1)}, bf16[2,272,128]{2,1,0:T(8,128)(2,1)S(1)}, u32[]{:S(2)}, u32[]{:S(2)}) %collective-permute-start.3) | collective-permute-done | bytes 139296 | tf_op jit(solution)/shard_map/left_over_z/ppermute | solution.py:270
  40.5 1.0 collective-permute-done.4.refs_5_.rest_5_
  41.5 7.7 %collective-permute-done.5.refs_6_.rest_6_ = bf16[2,272,128]{2,1,0:T(8,128)(2,1)S(1)} collective-permute-done((bf16[2,272,128]{2,1,0:T(8,128)(2,1)S(1)}, bf16[2,272,128]{2,1,0:T(8,128)(2,1)S(1)}, u32[]{:S(2)}, u32[]{:S(2)}) %collective-permute-start.5) | collective-permute-done | bytes 139296 | tf_op jit(solution)/shard_map/left_over_z/ppermute | solution.py:270
  49.2 1.2 collective-permute-done.6.refs_7_.rest_7_
  50.4 0.0 all-to-all-done.arrived
  50.4 2.8 %order.1 = bf16[16,2,128,128]{3,2,1,0:T(8,128)(2,1)} custom-call(s32[256]{0:T(256)} %right_sector.7, bf16[16,2,2,128,128]{4,3,2,1,0:T(8,128)(2,1)} %all-to-all-done.arrived), custom_call_target="tpu_custom_call" | custom-call | tf_op jit(solution)/shard_map/order/pallas_call | solution.py:283
  53.1 0.0 copy-start.2
  53.1 0.0 copy-start.3
  53.2 0.0 copy-start.4
  53.2 6.0 %all-to-all-start.1 = ((bf16[16,2,128,128]{3,2,1,0:T(8,128)(2,1)}), bf16[16,2,128,128]{3,2,1,0:T(8,128)(2,1)S(1)}, u32[]{:S(2)}, u32[]{:S(2)}) async-start(bf16[16,2,128,128]{3,2,1,0:T(8,128)(2,1)} %order.1), calls=%async_computation.1 | async-start | bytes 2097152 | tf_op jit(solution)/shard_map/right_over_mpo/all_to_all | solution.py:292
  59.1 0.8 left_over_core.1
  60.0 0.2 collective-permute-start.7
  60.2 0.0 copy-done
  60.2 2.1 %collective-permute-done.7.taken = bf16[8,272,128]{2,1,0:T(8,128)(2,1)S(1)} collective-permute-done((bf16[8,272,128]{2,1,0:T(8,128)(2,1)}, bf16[8,272,128]{2,1,0:T(8,128)(2,1)S(1)}, u32[]{:S(2)}, u32[]{:S(2)}) %collective-permute-start.7) | collective-permute-done | bytes 557088 | tf_op jit(solution)/shard_map/left_over_core/ppermute | solution.py:281
  62.2 24.9 %all-to-all-done.1.right_terms = bf16[16,2,128,128]{3,2,1,0:T(8,128)(2,1)S(1)} async-done(((bf16[16,2,128,128]{3,2,1,0:T(8,128)(2,1)}), bf16[16,2,128,128]{3,2,1,0:T(8,128)(2,1)S(1)}, u32[]{:S(2)}, u32[]{:S(2)}) %all-to-all-start.1) | async-done | bytes 1048608 | tf_op jit(solution)/shard_map/right_over_mpo/all_to_all | solution.py:292
  87.1 0.0 copy-done.2
  87.1 0.0 copy-done.3
  87.1 0.0 copy-done.4
  87.1 5.6 %lanczos.1 = f32[16,24,128]{2,1,0:T(8,128)} custom-call(s32[16]{0:T(128)S(1)} %copy-done.4, s32[256]{0:T(256)S(1)} %copy-done.3, s32[256]{0:T(256)S(1)} %copy-done.2, bf16[1,128,128]{2,1,0:T(8,128)(2,1)S(1)} %constant_dynamic-slice_fusion.vector, bf16[16,2,128,128]{3,2,1,0:T(8,128)(2,1)S(1)} %all-to-all-done.1.right_terms, ...), custom_call_target="tpu_custom_call" | custom-call | tf_op jit(solution)/shard_map/lanczos/pallas_call | solution.py:295
  92.7 3.5 %all-to-all-start.2 = ((f32[16,24,128]{2,1,0:T(8,128)}), f32[16,24,128]{2,1,0:T(8,128)S(1)}, u32[]{:S(2)}, u32[]{:S(2)}) async-start(f32[16,24,128]{2,1,0:T(8,128)} %lanczos.1), calls=%async_computation.2 | async-start | bytes 393216 | tf_op jit(solution)/shard_map/rows_over_mpo/all_to_all | solution.py:303
  96.2 10.3 %all-to-all-done.2.pieces = f32[16,24,128]{2,1,0:T(8,128)S(1)} async-done(((f32[16,24,128]{2,1,0:T(8,128)}), f32[16,24,128]{2,1,0:T(8,128)S(1)}, u32[]{:S(2)}, u32[]{:S(2)}) %all-to-all-start.2) | async-done | bytes 196640 | tf_op jit(solution)/shard_map/rows_over_mpo/all_to_all | solution.py:303
  106.5 0.6 broadcast_in_dim.2
  107.2 6.6 %all-to-all-start.3 = ((f32[16,8,128]{2,1,0:T(8,128)}), f32[16,8,128]{2,1,0:T(8,128)S(1)}, u32[]{:S(2)}, u32[]{:S(2)}) async-start(f32[16,8,128]{2,1,0:T(8,128)} %broadcast_in_dim.2), calls=%async_computation.3 | async-start | bytes 131072 | tf_op jit(solution)/shard_map/numbers_over_sec/all_to_all | solution.py:306
  113.8 6.5 %all-to-all-done.3.shared = f32[16,8,128]{2,1,0:T(8,128)S(1)} async-done(((f32[16,8,128]{2,1,0:T(8,128)}), f32[16,8,128]{2,1,0:T(8,128)S(1)}, u32[]{:S(2)}, u32[]{:S(2)}) %all-to-all-start.3) | async-done | bytes 65568 | tf_op jit(solution)/shard_map/numbers_over_sec/all_to_all | solution.py:306
  120.3 1.5 %finish.1 = (f32[16,8,128]{2,1,0:T(8,128)}, f32[16,8,128]{2,1,0:T(8,128)}, f32[1,128]{1,0:T(1,128)S(1)}) custom-call(s32[16]{0:T(128)S(1)} %copy-done.4, s32[256]{0:T(256)S(1)} %copy-done.3, s32[256]{0:T(256)S(1)} %copy-done.2, bf16[16,8,128]{2,1,0:T(8,128)(2,1)S(1)} %constant_dynamic-slice_fusion.1.vector, f32[16,24,128]{2,1,0:T(8,128)S(1)} %all-to-all-done.2.pieces, ...), custom_call_target="tpu_custom_call" | custom-call | tf_op jit(solution)/shard_map/finish/pallas_call | solution.py:309
  121.8 0.5 slice_bitcast_fusion
  (3 shorter events, 0.0 us)
Async XLA Ops:
  0.6 59.5 %copy-start = (bf16[16,128,128]{2,1,0:T(8,128)(2,1)S(1)}, bf16[16,128,128]{2,1,0:T(8,128)(2,1)}, u32[]{:S(2)}) copy-start(bf16[16,128,128]{2,1,0:T(8,128)(2,1)} %param.7) | copy-start | bytes 1572868
  4.6 7.8 %copy-start.1 = (bf16[2,16,128,128]{3,2,1,0:T(8,128)(2,1)S(1)}, bf16[2,16,128,128]{3,2,1,0:T(8,128)(2,1)}, u32[]{:S(2)}) copy-start(bf16[2,16,128,128]{3,2,1,0:T(8,128)(2,1)} %left_env.1) | copy-start | bytes 3145732
  4.6 7.8 %copy-start.5 = (f32[2]{0:T(128)S(1)}, f32[2]{0:T(128)}, u32[]{:S(2)}) copy-start(f32[2]{0:T(128)} %weights.1) | copy-start | bytes 28
  4.6 45.7 %all-to-all-start = ((bf16[16,2,2,128,128]{4,3,2,1,0:T(8,128)(2,1)}), bf16[16,2,2,128,128]{4,3,2,1,0:T(8,128)(2,1)}, u32[]{:S(2)}, u32[]{:S(2)}) async-start(bf16[16,2,2,128,128]{4,3,2,1,0:T(8,128)(2,1)} %pack_right.1), calls=%async_computation | async-start | bytes 4194304 | tf_op jit(solution)/shard_map/right_over_sec/all_to_all | solution.py:252
  14.8 13.4 %collective-permute-start = (bf16[2,272,128]{2,1,0:T(8,128)(2,1)S(1)}, bf16[2,272,128]{2,1,0:T(8,128)(2,1)S(1)}, u32[]{:S(2)}, u32[]{:S(2)}) collective-permute-start(bf16[2,272,128]{2,1,0:T(8,128)(2,1)S(1)} %get-tuple-element.24), channel_id=1, source_target_pairs={{0,2},{1,3},{2,4},{3,5},{4,6},{5,7},{6,8},{7,9},{8,10},{9,11},{10,... | collective-permute-start | bytes 417800 | tf_op jit(solution)/shard_map/left_over_z/ppermute | solution.py:270
  16.5 14.1 %collective-permute-start.1 = (bf16[2,272,128]{2,1,0:T(8,128)(2,1)S(1)}, bf16[2,272,128]{2,1,0:T(8,128)(2,1)S(1)}, u32[]{:S(2)}, u32[]{:S(2)}) collective-permute-start(bf16[2,272,128]{2,1,0:T(8,128)(2,1)S(1)} %get-tuple-element.25), channel_id=1, source_target_pairs={{0,4},{1,5},{2,6},{3,7},{4,8},{5,9},{6,10},{7,11},{8,12},{9,13},{1... | collective-permute-start | bytes 417800 | tf_op jit(solution)/shard_map/left_over_z/ppermute | solution.py:270
  19.5 18.5 %collective-permute-start.2 = (bf16[2,272,128]{2,1,0:T(8,128)(2,1)S(1)}, bf16[2,272,128]{2,1,0:T(8,128)(2,1)S(1)}, u32[]{:S(2)}, u32[]{:S(2)}) collective-permute-start(bf16[2,272,128]{2,1,0:T(8,128)(2,1)S(1)} %get-tuple-element.26), channel_id=1, source_target_pairs={{0,6},{1,7},{2,8},{3,9},{4,10},{5,11},{6,12},{7,13},{8,14},{9,15},... | collective-permute-start | bytes 417800 | tf_op jit(solution)/shard_map/left_over_z/ppermute | solution.py:270
  23.2 17.2 %collective-permute-start.3 = (bf16[2,272,128]{2,1,0:T(8,128)(2,1)S(1)}, bf16[2,272,128]{2,1,0:T(8,128)(2,1)S(1)}, u32[]{:S(2)}, u32[]{:S(2)}) collective-permute-start(bf16[2,272,128]{2,1,0:T(8,128)(2,1)S(1)} %get-tuple-element.27), channel_id=1, source_target_pairs={{0,8},{1,9},{2,10},{3,11},{4,12},{5,13},{6,14},{7,15},{8,0},{9,1},... | collective-permute-start | bytes 417800 | tf_op jit(solution)/shard_map/left_over_z/ppermute | solution.py:270
  23.7 17.8 %collective-permute-start.4 = (bf16[2,272,128]{2,1,0:T(8,128)(2,1)S(1)}, bf16[2,272,128]{2,1,0:T(8,128)(2,1)S(1)}, u32[]{:S(2)}, u32[]{:S(2)}) collective-permute-start(bf16[2,272,128]{2,1,0:T(8,128)(2,1)S(1)} %get-tuple-element.28), channel_id=1, source_target_pairs={{0,10},{1,11},{2,12},{3,13},{4,14},{5,15},{6,0},{7,1},{8,2},{9,3},... | collective-permute-start | bytes 417800 | tf_op jit(solution)/shard_map/left_over_z/ppermute | solution.py:270
  28.2 21.0 %collective-permute-start.5 = (bf16[2,272,128]{2,1,0:T(8,128)(2,1)S(1)}, bf16[2,272,128]{2,1,0:T(8,128)(2,1)S(1)}, u32[]{:S(2)}, u32[]{:S(2)}) collective-permute-start(bf16[2,272,128]{2,1,0:T(8,128)(2,1)S(1)} %get-tuple-element.29), channel_id=1, source_target_pairs={{0,12},{1,13},{2,14},{3,15},{4,0},{5,1},{6,2},{7,3},{8,4},{9,5},{1... | collective-permute-start | bytes 417800 | tf_op jit(solution)/shard_map/left_over_z/ppermute | solution.py:270
  30.6 19.8 %collective-permute-start.6 = (bf16[2,272,128]{2,1,0:T(8,128)(2,1)S(1)}, bf16[2,272,128]{2,1,0:T(8,128)(2,1)S(1)}, u32[]{:S(2)}, u32[]{:S(2)}) collective-permute-start(bf16[2,272,128]{2,1,0:T(8,128)(2,1)S(1)} %get-tuple-element.30), channel_id=1, source_target_pairs={{0,14},{1,15},{2,0},{3,1},{4,2},{5,3},{6,4},{7,5},{8,6},{9,7},{10,... | collective-permute-start | bytes 417800 | tf_op jit(solution)/shard_map/left_over_z/ppermute | solution.py:270
  53.1 34.0 %copy-start.2 = (s32[256]{0:T(256)S(1)}, s32[256]{0:T(256)}, u32[]{:S(2)}) copy-start(s32[256]{0:T(256)} %right_sector.7) | copy-start | bytes 3076
  53.1 33.9 %copy-start.3 = (s32[256]{0:T(256)S(1)}, s32[256]{0:T(256)}, u32[]{:S(2)}) copy-start(s32[256]{0:T(256)} %right_size.3) | copy-start | bytes 3076
  53.2 33.9 %copy-start.4 = (s32[16]{0:T(128)S(1)}, s32[16]{0:T(128)}, u32[]{:S(2)}) copy-start(s32[16]{0:T(128)} %left_size.3) | copy-start | bytes 196
  53.2 33.9 %all-to-all-start.1 = ((bf16[16,2,128,128]{3,2,1,0:T(8,128)(2,1)}), bf16[16,2,128,128]{3,2,1,0:T(8,128)(2,1)S(1)}, u32[]{:S(2)}, u32[]{:S(2)}) async-start(bf16[16,2,128,128]{3,2,1,0:T(8,128)(2,1)} %order.1), calls=%async_computation.1 | async-start | bytes 2097152 | tf_op jit(solution)/shard_map/right_over_mpo/all_to_all | solution.py:292
  60.0 2.3 %collective-permute-start.7 = (bf16[8,272,128]{2,1,0:T(8,128)(2,1)}, bf16[8,272,128]{2,1,0:T(8,128)(2,1)S(1)}, u32[]{:S(2)}, u32[]{:S(2)}) collective-permute-start(bf16[8,272,128]{2,1,0:T(8,128)(2,1)} %left_over_core.1), channel_id=1, source_target_pairs={{0,1},{1,0},{2,3},{3,2},{4,5},{5,4},{6,7},{7,6},{8,9},{9,8},{10,11... | collective-permute-start | bytes 1671176 | tf_op jit(solution)/shard_map/left_over_core/ppermute | solution.py:281
  92.7 13.9 %all-to-all-start.2 = ((f32[16,24,128]{2,1,0:T(8,128)}), f32[16,24,128]{2,1,0:T(8,128)S(1)}, u32[]{:S(2)}, u32[]{:S(2)}) async-start(f32[16,24,128]{2,1,0:T(8,128)} %lanczos.1), calls=%async_computation.2 | async-start | bytes 393216 | tf_op jit(solution)/shard_map/rows_over_mpo/all_to_all | solution.py:303
  107.2 13.1 %all-to-all-start.3 = ((f32[16,8,128]{2,1,0:T(8,128)}), f32[16,8,128]{2,1,0:T(8,128)S(1)}, u32[]{:S(2)}, u32[]{:S(2)}) async-start(f32[16,8,128]{2,1,0:T(8,128)} %broadcast_in_dim.2), calls=%async_computation.3 | async-start | bytes 131072 | tf_op jit(solution)/shard_map/numbers_over_sec/all_to_all | solution.py:306

commit v4 on v3

--- a/solution.py
+++ b/solution.py
@@ -64,8 +64,9 @@
         for side in range(2):
             q = 2 * chip + (own % 2 + side) % 2
             for w in range(terms):
-                copies.append(pltpu.make_async_copy(stage.at[w, q], pair.at[side, pl.ds(w * width, width)], sem.at[1]))
-            copies.append(pltpu.make_async_copy(wbuf, pair.at[side, pl.ds(terms * width, PAD)], sem.at[1]))
+                rows = pl.ds((side * terms + w) * width, width)
+                copies.append(pltpu.make_async_copy(stage.at[w, q], pair.at[rows], sem.at[1]))
+        copies.append(pltpu.make_async_copy(wbuf, pair.at[pl.ds(2 * terms * width, PAD)], sem.at[1]))
     for copy in copies:
         copy.start()
     for copy in copies:
@@ -76,7 +77,8 @@
     *pairs, given, sem = refs
     copies = []
     for d, pair in enumerate(pairs):
-        copies.append(pltpu.make_async_copy(pair.at[1], given.at[d], sem))
+        rows = pl.ds(pair.shape[0] - given.shape[1], given.shape[1])
+        copies.append(pltpu.make_async_copy(pair.at[rows], given.at[d], sem))
         copies[-1].start()
     for copy in copies:
         copy.wait()
@@ -113,13 +115,15 @@
     return jnp.sum(jnp.sum(x, axis=0, keepdims=True), axis=1, keepdims=True)
 
 
-def lanczos_kernel(left_size, right_size, right_sector, vector, right_terms, taken, *rest):
-    *left_terms, out = rest
+def lanczos_kernel(left_size, right_size, right_sector, vectors, right_terms, taken, *rest):
+    *left_terms, out, vector, sem = rest
     sources, terms, width, _ = right_terms.shape
     chips = len(left_terms)
     sec = lax.axis_index("sec")
     own = lax.axis_index("mpo")
     blocks = left_size.shape[0]
+    load = pltpu.make_async_copy(vectors.at[own], vector, sem)
+    load.start()
     mask = live((width, width), left_size[own], right_size[right_sector[sec * blocks + own]])
 
     def apply(block):
@@ -127,18 +131,24 @@
         for move in range(sources):
             step, side = move // 2, move % 2
             source = 2 * ((own // 2 + chips - step) % chips) + (own % 2 + side) % 2
-            part = left_terms[step].at[0] if side == 0 else taken.at[step]
+            part = left_terms[step] if side == 0 else taken.at[step]
             half = jnp.dot(part[: terms * width], block, preferred_element_type=F32)
-            scale = part[terms * width :].astype(F32)
+            scale = part[part.shape[0] - PAD :].astype(F32)
+            halves = []
             for w in range(terms):
                 weight = scale[3 * w : 3 * w + 1] + scale[3 * w + 1 : 3 * w + 2] + scale[3 * w + 2 : 3 * w + 3]
-                term = (weight * half[w * width : (w + 1) * width]).astype(BF16)
-                acc = acc + lax.dot_general(
-                    term, right_terms[source, w], (((1,), (1,)), ((), ())), preferred_element_type=F32
-                )
+                halves.append((weight * half[w * width : (w + 1) * width]).astype(BF16))
+            rights = [right_terms[source, w] for w in range(terms)]
+            acc = acc + lax.dot_general(
+                jnp.concatenate(halves, axis=1),
+                jnp.concatenate(rights, axis=1),
+                (((1,), (1,)), ((), ())),
+                preferred_element_type=F32,
+            )
         return jnp.where(mask, acc, 0.0)
 
-    start = jnp.where(mask, vector[0].astype(F32), 0.0)
+    load.wait()
+    start = jnp.where(mask, vector[...].astype(F32), 0.0)
     norm = total(start * start)
     scale = 1.0 / jnp.sqrt(norm / float(width * width) + 1e-06)
     image = apply(start.astype(BF16)) * scale
@@ -169,11 +179,14 @@
         out[d, 2 * rows :] = line
 
 
-def finish_kernel(left_size, right_size, right_sector, vector, pieces, shared, next_out, rest_out, coef_out):
-    blocks, rows, width = vector.shape
+def finish_kernel(left_size, right_size, right_sector, vectors, pieces, shared, next_out, rest_out, coef_out, vector, sem):
+    blocks, rows, width = next_out.shape
     sec = lax.axis_index("sec")
     part = lax.axis_index("mpo")
     devices = shared.shape[0]
+    groups = PAD // rows
+    load = pltpu.make_async_copy(vectors.at[:, pl.ds(pl.multiple_of(part // groups * PAD, PAD), PAD)], vector, sem)
+    load.start()
     entries = float(devices * blocks * width * width)
     cells = float(width * width)
     stats = shared[:, 0, :]
@@ -196,8 +209,9 @@
     beta = jnp.sqrt(rest_total / entries + 1e-06)
     inner = field(stats, 4) + delta * field(stats, 5) + delta * delta * overlap
     alpha_next = total(jnp.where(lead, weight * inner, 0.0)) / entries / beta / beta
-    coef_lane = lax.broadcasted_iota(jnp.int32, coef_out.shape, 1)
-    coef_out[...] = jnp.where(coef_lane == 0, alpha, jnp.where(coef_lane == 1, beta, alpha_next))
+    for j, number in enumerate((alpha, beta, alpha_next)):
+        coef_out[j] = number[0, 0]
+    load.wait()
     for q in range(blocks):
         line = pieces[q, 2 * rows : 2 * rows + 1, :]
         lane_one = lax.broadcasted_iota(jnp.int32, line.shape, 1)
@@ -208,7 +222,11 @@
         row = lax.broadcasted_iota(jnp.int32, (rows, width), 0) + part * rows
         col = lax.broadcasted_iota(jnp.int32, (rows, width), 1)
         mask = (row < left_size[q]) & (col < right_size[right_sector[sec * blocks + q]])
-        unit = jnp.where(mask, vector[q].astype(F32), 0.0) / root
+        group = vector[q].astype(F32)
+        own_rows = group[:rows]
+        for j in range(1, groups):
+            own_rows = jnp.where(part % groups == j, group[j * rows : (j + 1) * rows], own_rows)
+        unit = jnp.where(mask, own_rows, 0.0) / root
         rest = pieces[q, :rows]
         after = pieces[q, rows : 2 * rows]
         shift = ratio_q - alpha
@@ -232,7 +250,6 @@
     devices = lax.axis_size("sec")
     layers = lax.axis_size("mpo")
     rows = width // layers
-    own = lax.axis_index("mpo")
     anywhere = pl.BlockSpec(memory_space=pl.ANY)
     scalars = pl.BlockSpec(memory_space=pltpu.SMEM)
     vmem = pl.BlockSpec(memory_space=pltpu.VMEM)
@@ -253,7 +270,7 @@
     with jax.named_scope("pack_left"):
         pairs = pl.pallas_call(
             pack_left_kernel,
-            out_shape=(jax.ShapeDtypeStruct((2, long, width), BF16),) * chips,
+            out_shape=(jax.ShapeDtypeStruct((terms * width + long, width), BF16),) * chips,
             in_specs=[scalars, anywhere],
             out_specs=(anywhere,) * chips,
             scratch_shapes=[
@@ -268,7 +285,17 @@
         for d in sorted(range(1, chips), key=lambda d: -min(d, chips - d)):
             route = [(p, (p + 2 * d) % layers) for p in range(layers)]
             left_terms[d] = lax.ppermute(pairs[d], "mpo", route)
-        arrived, *left_terms = lax.optimization_barrier((arrived, *left_terms))
+        arrived, left_terms[4] = lax.optimization_barrier((arrived, left_terms[4]))
+    with jax.named_scope("order"):
+        ordered = pl.pallas_call(
+            order_kernel,
+            out_shape=jax.ShapeDtypeStruct((blocks, terms, width, width), BF16),
+            in_specs=[scalars, anywhere],
+            out_specs=anywhere,
+            scratch_shapes=[pltpu.VMEM((blocks, terms, width, width), BF16), pltpu.SemaphoreType.DMA((blocks + 1,))],
+            compiler_params=pltpu.CompilerParams(vmem_limit_bytes=60 * MIB),
+        )(right_sector, arrived)
+        ordered, left_terms[3], left_terms[5], left_terms[2], left_terms[6], left_terms[1], left_terms[7] = lax.optimization_barrier((ordered, left_terms[3], left_terms[5], left_terms[2], left_terms[6], left_terms[1], left_terms[7]))
     with jax.named_scope("left_over_core"):
         given = pl.pallas_call(
             collect_kernel,
@@ -279,45 +306,36 @@
             compiler_params=pltpu.CompilerParams(vmem_limit_bytes=4 * MIB),
         )(*left_terms)
         taken = lax.ppermute(given, "mpo", [(p, p ^ 1) for p in range(layers)])
-    with jax.named_scope("order"):
-        ordered = pl.pallas_call(
-            order_kernel,
-            out_shape=jax.ShapeDtypeStruct((blocks, terms, width, width), BF16),
-            in_specs=[scalars, anywhere],
-            out_specs=anywhere,
-            scratch_shapes=[pltpu.VMEM((blocks, terms, width, width), BF16), pltpu.SemaphoreType.DMA((blocks + 1,))],
-            compiler_params=pltpu.CompilerParams(vmem_limit_bytes=60 * MIB),
-        )(right_sector, arrived)
     with jax.named_scope("right_over_mpo"):
         right_terms = lax.all_to_all(ordered, "mpo", 0, 0, tiled=True)
     with jax.named_scope("lanczos"):
-        vector = lax.dynamic_slice_in_dim(wavefunction, own, 1, 0)
         pieces = pl.pallas_call(
             lanczos_kernel,
             out_shape=jax.ShapeDtypeStruct((layers, 2 * rows + 8, width), F32),
-            in_specs=[scalars, scalars, scalars, vmem, vmem, vmem] + [vmem] * chips,
+            in_specs=[scalars, scalars, scalars, anywhere, vmem, vmem] + [vmem] * chips,
             out_specs=vmem,
+            scratch_shapes=[pltpu.VMEM((width, width), BF16), pltpu.SemaphoreType.DMA],
             compiler_params=pltpu.CompilerParams(vmem_limit_bytes=16 * MIB),
-        )(left_size, right_size, right_sector, vector, right_terms, taken, *left_terms)
+        )(left_size, right_size, right_sector, wavefunction, right_terms, taken, *left_terms)
     with jax.named_scope("rows_over_mpo"):
         pieces = lax.all_to_all(pieces, "mpo", 0, 0, tiled=True)
     with jax.named_scope("numbers_over_sec"):
         line = jnp.sum(pieces[:, 2 * rows :, :], axis=0)
         shared = lax.all_to_all(jnp.broadcast_to(line[None], (devices, 8, width)), "sec", 0, 0, tiled=True)
     with jax.named_scope("finish"):
-        own_rows = lax.dynamic_slice_in_dim(wavefunction, own * rows, rows, 1)
         next_vector, residual, coefficients = pl.pallas_call(
             finish_kernel,
             out_shape=(
                 jax.ShapeDtypeStruct((blocks, rows, width), F32),
                 jax.ShapeDtypeStruct((blocks, rows, width), F32),
-                jax.ShapeDtypeStruct((1, width), F32),
+                jax.ShapeDtypeStruct((3,), F32),
             ),
-            in_specs=[scalars, scalars, scalars, vmem, vmem, vmem],
-            out_specs=(vmem, vmem, vmem),
+            in_specs=[scalars, scalars, scalars, anywhere, vmem, vmem],
+            out_specs=(vmem, vmem, scalars),
+            scratch_shapes=[pltpu.VMEM((blocks, PAD, width), BF16), pltpu.SemaphoreType.DMA],
             compiler_params=pltpu.CompilerParams(vmem_limit_bytes=8 * MIB),
-        )(left_size, right_size, right_sector, own_rows, pieces, shared)
-    return (next_vector, residual, coefficients[0, :3])
+        )(left_size, right_size, right_sector, wavefunction, pieces, shared)
+    return (next_vector, residual, coefficients)
 
 
 def solution(mesh):

time: 123 us -> 112 us (0.911)
  blocking collectives: 0 us -> 23.2 us
  waiting for transfers between devices: 62.8 us -> 39.9 us
  starting transfers between devices: 40.6 us -> 34.1 us
  Pallas kernels: 17 us -> 14 us
    all_to_all x0 -> x2, blocking collectives: none -> 23.2 us  [the longest x1 13.6 us: shards(): pieces = lax.all_to_all(pieces, 'mpo', 0, 0, tiled=True)]
    all_to_all x2 -> x0, waiting for transfers between devices: 16.8 us -> none  [the longest x1 10.3 us: shards(): pieces = lax.all_to_all(pieces, 'mpo', 0, 0, tiled=True)]
    ppermute x7, waiting for transfers between devices: 19.1 us -> 8.48 us  [shards(): left_terms[d] = lax.ppermute(pairs[d], 'mpo', route)]
    all_to_all x2 -> x0, starting transfers between devices: 10.1 us -> none  [the longest x1 6.6 us: shards(): lax.all_to_all(jnp.broadcast_to(line[None], (devices, 8, width)), 'sec',...]
    all_to_all x1, waiting for transfers between devices: 0.01 us -> 4.42 us  [shards(): arrived = lax.all_to_all(right_out, 'sec', 0, 0, tiled=True)]
    all_to_all x1, starting transfers between devices: 5.98 us -> 10.3 us  [shards(): right_terms = lax.all_to_all(ordered, 'mpo', 0, 0, tiled=True)]
    pallas_call x1, Pallas kernels: 5.57 us -> 2.62 us  [shards(): pl.pallas_call(lanczos_kernel, out_shape=jax.ShapeDtypeStruct((layers, 2...]
  transfers between devices with their start and end apart: 12 -> 10, of which waited for: 9 -> 5; matrix products, arithmetic and copies ran while one was open for 0% -> 0% of each run, Pallas kernels for 3% -> 5%
where the time goes in v4:
time: 112 us
  waiting for transfers between devices  39.9 us (36%)
  starting transfers between devices  34.1 us (30%)
  blocking collectives  23.2 us (21%)
  Pallas kernels  14 us (12%)
    all_to_all x1, waiting for transfers between devices, shards(): right_terms = lax.all_to_all(ordered, 'mpo', 0, 0, tiled=True)  25.2 us
    ppermute x7, starting transfers between devices, shards(): left_terms[d] = lax.ppermute(pairs[d], 'mpo', route)  15.8 us
    all_to_all x1, blocking collectives, shards(): pieces = lax.all_to_all(pieces, 'mpo', 0, 0, tiled=True)  13.6 us
    all_to_all x1, starting transfers between devices, shards(): right_terms = lax.all_to_all(ordered, 'mpo', 0, 0, tiled=True)  10.3 us
    all_to_all x1, blocking collectives, shards(): lax.all_to_all(jnp.broadcast_to(line[None], (devices, 8, width)), 'sec',...  9.6 us
    ppermute x7, waiting for transfers between devices, shards(): left_terms[d] = lax.ppermute(pairs[d], 'mpo', route)  8.48 us
    all_to_all x1, starting transfers between devices, shards(): arrived = lax.all_to_all(right_out, 'sec', 0, 0, tiled=True)  7.78 us
    all_to_all x1, waiting for transfers between devices, shards(): arrived = lax.all_to_all(right_out, 'sec', 0, 0, tiled=True)  4.42 us
  transfers between devices with their start and end apart: 10, of which 5 were waited for; matrix products, arithmetic and copies ran while one was open for 0% of the time, Pallas kernels for 5%

profile of v4, /device:TPU:1, one launch (start us, length us, event | category | flops | bytes accessed | tf_op | source)
XLA Modules:
  0.0 112.1 jit_solution(10202182165502243381)
XLA Ops:
  0.6 3.8 %pack_right.1 = bf16[16,2,2,128,128]{4,3,2,1,0:T(8,128)(2,1)} custom-call(s32[256]{0:T(256)} %right_sector.7, bf16[2,16,128,128]{3,2,1,0:T(8,128)(2,1)} %right_env.1), custom_call_target="tpu_custom_call" | custom-call | tf_op jit(solution)/shard_map/pack_right/pallas_call | solution.py:260
  4.5 0.0 copy-start.1
  4.5 0.0 copy-start.5
  4.5 7.8 %all-to-all-start = ((bf16[16,2,2,128,128]{4,3,2,1,0:T(8,128)(2,1)}), bf16[16,2,2,128,128]{4,3,2,1,0:T(8,128)(2,1)}, u32[]{:S(2)}, u32[]{:S(2)}) async-start(bf16[16,2,2,128,128]{4,3,2,1,0:T(8,128)(2,1)} %pack_right.1), calls=%async_computation | async-start | bytes 4194304 | tf_op jit(solution)/shard_map/right_over_sec/all_to_all | solution.py:269
  12.3 0.0 copy-done.1
  12.3 0.0 copy-done.5
  12.3 2.3 %pack_left.1 = (bf16[528,128]{1,0:T(8,128)(2,1)S(1)}, bf16[528,128]{1,0:T(8,128)(2,1)S(1)}, bf16[528,128]{1,0:T(8,128)(2,1)S(1)}, bf16[528,128]{1,0:T(8,128)(2,1...) custom-call(f32[2]{0:T(128)S(1)} %copy-done.5, ...), custom_call_target="tpu_custom_call" | custom-call | tf_op jit(solution)/shard_map/pack_left/pallas_call | solution.py:271
  14.6 7.0 %collective-permute-start = (bf16[528,128]{1,0:T(8,128)(2,1)S(1)}, bf16[528,128]{1,0:T(8,128)(2,1)S(1)}, u32[]{:S(2)}, u32[]{:S(2)}) collective-permute-start(bf16[528,128]{1,0:T(8,128)(2,1)S(1)} %get-tuple-element.20), channel_id=1, source_target_pairs={{0,8},{1,9},{2,10},{3,11},{4,12},{5,13},{6,14},{7,15},{8,0},{9,1},... | collective-permute-start | bytes 405512 | tf_op jit(solution)/shard_map/left_over_z/ppermute | solution.py:287
  21.6 1.6 %collective-permute-start.1 = (bf16[528,128]{1,0:T(8,128)(2,1)S(1)}, bf16[528,128]{1,0:T(8,128)(2,1)S(1)}, u32[]{:S(2)}, u32[]{:S(2)}) collective-permute-start(bf16[528,128]{1,0:T(8,128)(2,1)S(1)} %get-tuple-element.22), channel_id=1, source_target_pairs={{0,6},{1,7},{2,8},{3,9},{4,10},{5,11},{6,12},{7,13},{8,14},{9,15},... | collective-permute-start | bytes 405512 | tf_op jit(solution)/shard_map/left_over_z/ppermute | solution.py:287
  23.2 2.8 %collective-permute-start.2 = (bf16[528,128]{1,0:T(8,128)(2,1)S(1)}, bf16[528,128]{1,0:T(8,128)(2,1)S(1)}, u32[]{:S(2)}, u32[]{:S(2)}) collective-permute-start(bf16[528,128]{1,0:T(8,128)(2,1)S(1)} %get-tuple-element.23), channel_id=1, source_target_pairs={{0,10},{1,11},{2,12},{3,13},{4,14},{5,15},{6,0},{7,1},{8,2},{9,3},... | collective-permute-start | bytes 405512 | tf_op jit(solution)/shard_map/left_over_z/ppermute | solution.py:287
  26.1 1.2 %collective-permute-start.3 = (bf16[528,128]{1,0:T(8,128)(2,1)S(1)}, bf16[528,128]{1,0:T(8,128)(2,1)S(1)}, u32[]{:S(2)}, u32[]{:S(2)}) collective-permute-start(bf16[528,128]{1,0:T(8,128)(2,1)S(1)} %get-tuple-element.24), channel_id=1, source_target_pairs={{0,4},{1,5},{2,6},{3,7},{4,8},{5,9},{6,10},{7,11},{8,12},{9,13},{1... | collective-permute-start | bytes 405512 | tf_op jit(solution)/shard_map/left_over_z/ppermute | solution.py:287
  27.3 2.4 %collective-permute-start.4 = (bf16[528,128]{1,0:T(8,128)(2,1)S(1)}, bf16[528,128]{1,0:T(8,128)(2,1)S(1)}, u32[]{:S(2)}, u32[]{:S(2)}) collective-permute-start(bf16[528,128]{1,0:T(8,128)(2,1)S(1)} %get-tuple-element.25), channel_id=1, source_target_pairs={{0,12},{1,13},{2,14},{3,15},{4,0},{5,1},{6,2},{7,3},{8,4},{9,5},{1... | collective-permute-start | bytes 405512 | tf_op jit(solution)/shard_map/left_over_z/ppermute | solution.py:287
  29.6 0.0 collective-permute-done.refs_4_.rest_4_
  29.6 0.7 collective-permute-start.5
  30.4 8.0 %collective-permute-done.1.refs_3_.rest_3_ = bf16[528,128]{1,0:T(8,128)(2,1)S(1)} collective-permute-done((bf16[528,128]{1,0:T(8,128)(2,1)S(1)}, bf16[528,128]{1,0:T(8,128)(2,1)S(1)}, u32[]{:S(2)}, u32[]{:S(2)}) %collective-permute-start.1) | collective-permute-done | bytes 135200 | tf_op jit(solution)/shard_map/left_over_z/ppermute | solution.py:287
  38.4 0.0 collective-permute-start.6
  38.4 4.4 %all-to-all-done.arrived = bf16[16,2,2,128,128]{4,3,2,1,0:T(8,128)(2,1)} async-done(((bf16[16,2,2,128,128]{4,3,2,1,0:T(8,128)(2,1)}), bf16[16,2,2,128,128]{4,3,2,1,0:T(8,128)(2,1)}, u32[]{:S(2)}, u32[]{:S(2)}) %all-to-all-start) | async-done | bytes 2097184 | tf_op jit(solution)/shard_map/right_over_sec/all_to_all | solution.py:269
  42.8 2.8 %order.1 = bf16[16,2,128,128]{3,2,1,0:T(8,128)(2,1)} custom-call(s32[256]{0:T(256)} %right_sector.7, bf16[16,2,2,128,128]{4,3,2,1,0:T(8,128)(2,1)} %all-to-all-done.arrived), custom_call_target="tpu_custom_call" | custom-call | tf_op jit(solution)/shard_map/order/pallas_call | solution.py:290
  45.6 0.0 copy-start
  45.6 0.0 copy-start.2
  45.6 0.0 copy-start.3
  45.7 0.0 copy-start.4
  45.7 0.0 collective-permute-done.2.refs_5_.rest_5_
  45.7 0.0 collective-permute-done.3.refs_2_.rest_2_
  45.7 0.0 collective-permute-done.4.refs_6_.rest_6_
  45.7 0.0 collective-permute-done.5.refs_1_.rest_1_
  45.7 0.5 collective-permute-done.6.refs_7_.rest_7_
  46.2 10.3 %all-to-all-start.1 = ((bf16[16,2,128,128]{3,2,1,0:T(8,128)(2,1)}), bf16[16,2,128,128]{3,2,1,0:T(8,128)(2,1)S(1)}, u32[]{:S(2)}, u32[]{:S(2)}) async-start(bf16[16,2,128,128]{3,2,1,0:T(8,128)(2,1)} %order.1), calls=%async_computation.1 | async-start | bytes 2097152 | tf_op jit(solution)/shard_map/right_over_mpo/all_to_all | solution.py:310
  56.5 0.7 left_over_core.1
  57.2 0.2 collective-permute-start.7
  57.4 1.8 %collective-permute-done.7.taken = bf16[8,272,128]{2,1,0:T(8,128)(2,1)S(1)} collective-permute-done((bf16[8,272,128]{2,1,0:T(8,128)(2,1)S(1)}, bf16[8,272,128]{2,1,0:T(8,128)(2,1)S(1)}, u32[]{:S(2)}, u32[]{:S(2)}) %collective-permute-start.7) | collective-permute-done | bytes 557088 | tf_op jit(solution)/shard_map/left_over_core/ppermute | solution.py:308
  59.2 25.2 %all-to-all-done.1.right_terms = bf16[16,2,128,128]{3,2,1,0:T(8,128)(2,1)S(1)} async-done(((bf16[16,2,128,128]{3,2,1,0:T(8,128)(2,1)}), bf16[16,2,128,128]{3,2,1,0:T(8,128)(2,1)S(1)}, u32[]{:S(2)}, u32[]{:S(2)}) %all-to-all-start.1) | async-done | bytes 1048608 | tf_op jit(solution)/shard_map/right_over_mpo/all_to_all | solution.py:310
  84.4 0.0 copy-done
  84.4 0.0 copy-done.2
  84.4 0.0 copy-done.3
  84.4 0.0 copy-done.4
  84.4 2.6 %lanczos.1 = f32[16,24,128]{2,1,0:T(8,128)S(1)} custom-call(s32[16]{0:T(128)S(1)} %copy-done.4, s32[256]{0:T(256)S(1)} %copy-done.3, s32[256]{0:T(256)S(1)} %copy-done.2, bf16[16,128,128]{2,1,0:T(8,128)(2,1)S(1)} %copy-done, bf16[16,2,128,128]{3,2,1,0:T(8,128)(2,1)S(1)} %all-to-all-done.1.right_terms, bf16[8,272,128]{2,1,0:T(8,128)(2,1)S(1)} %collective-permute-done.7.taken, ...), custom_call_target="tpu_custom_call" | custom-call | tf_op jit(solution)/shard_map/lanczos/pallas_call | solution.py:312
  87.0 13.6 %all_to_all.20.pieces = f32[16,24,128]{2,1,0:T(8,128)S(1)} all-to-all(f32[16,24,128]{2,1,0:T(8,128)S(1)} %lanczos.1), channel_id=1, replica_groups=mesh['sec'=16,'mpo'=16] {'mpo'}, dimensions={0} | all-to-all | bytes 393216 | tf_op jit(solution)/shard_map/rows_over_mpo/all_to_all | solution.py:321
  100.7 9.6 %all_to_all.21.shared = f32[16,8,128]{2,1,0:T(8,128)S(1)} all-to-all(f32[16,8,128]{2,1,0:T(8,128)S(1)} %broadcast_in_dim.2), channel_id=1, replica_groups=mesh['sec'=16,'mpo'=16] {'sec'}, dimensions={0} | all-to-all | bytes 131072 | tf_op jit(solution)/shard_map/numbers_over_sec/all_to_all | solution.py:324
  110.3 1.8 %finish.1 = (f32[16,8,128]{2,1,0:T(8,128)}, f32[16,8,128]{2,1,0:T(8,128)}, f32[3]{0:T(128)}) custom-call(s32[16]{0:T(128)S(1)} %copy-done.4, s32[256]{0:T(256)S(1)} %copy-done.3, s32[256]{0:T(256)S(1)} %copy-done.2, bf16[16,128,128]{2,1,0:T(8,128)(2,1)S(1)} %copy-done, f32[16,24,128]{2,1,0:T(8,128)S(1)} %all_to_all.20.pieces, ...), custom_call_target="tpu_custom_call" | custom-call | tf_op jit(solution)/shard_map/finish/pallas_call | solution.py:326
  (2 shorter events, 0.0 us)
Async XLA Ops:
  4.5 7.8 %copy-start.1 = (bf16[2,16,128,128]{3,2,1,0:T(8,128)(2,1)S(1)}, bf16[2,16,128,128]{3,2,1,0:T(8,128)(2,1)}, u32[]{:S(2)}) copy-start(bf16[2,16,128,128]{3,2,1,0:T(8,128)(2,1)} %left_env.1) | copy-start | bytes 3145732
  4.5 7.8 %copy-start.5 = (f32[2]{0:T(128)S(1)}, f32[2]{0:T(128)}, u32[]{:S(2)}) copy-start(f32[2]{0:T(128)} %weights.1) | copy-start | bytes 28
  4.5 38.3 %all-to-all-start = ((bf16[16,2,2,128,128]{4,3,2,1,0:T(8,128)(2,1)}), bf16[16,2,2,128,128]{4,3,2,1,0:T(8,128)(2,1)}, u32[]{:S(2)}, u32[]{:S(2)}) async-start(bf16[16,2,2,128,128]{4,3,2,1,0:T(8,128)(2,1)} %pack_right.1), calls=%async_computation | async-start | bytes 4194304 | tf_op jit(solution)/shard_map/right_over_sec/all_to_all | solution.py:269
  14.6 15.1 %collective-permute-start = (bf16[528,128]{1,0:T(8,128)(2,1)S(1)}, bf16[528,128]{1,0:T(8,128)(2,1)S(1)}, u32[]{:S(2)}, u32[]{:S(2)}) collective-permute-start(bf16[528,128]{1,0:T(8,128)(2,1)S(1)} %get-tuple-element.20), channel_id=1, source_target_pairs={{0,8},{1,9},{2,10},{3,11},{4,12},{5,13},{6,14},{7,15},{8,0},{9,1},... | collective-permute-start | bytes 405512 | tf_op jit(solution)/shard_map/left_over_z/ppermute | solution.py:287
  21.6 16.8 %collective-permute-start.1 = (bf16[528,128]{1,0:T(8,128)(2,1)S(1)}, bf16[528,128]{1,0:T(8,128)(2,1)S(1)}, u32[]{:S(2)}, u32[]{:S(2)}) collective-permute-start(bf16[528,128]{1,0:T(8,128)(2,1)S(1)} %get-tuple-element.22), channel_id=1, source_target_pairs={{0,6},{1,7},{2,8},{3,9},{4,10},{5,11},{6,12},{7,13},{8,14},{9,15},... | collective-permute-start | bytes 405512 | tf_op jit(solution)/shard_map/left_over_z/ppermute | solution.py:287
  23.2 22.4 %collective-permute-start.2 = (bf16[528,128]{1,0:T(8,128)(2,1)S(1)}, bf16[528,128]{1,0:T(8,128)(2,1)S(1)}, u32[]{:S(2)}, u32[]{:S(2)}) collective-permute-start(bf16[528,128]{1,0:T(8,128)(2,1)S(1)} %get-tuple-element.23), channel_id=1, source_target_pairs={{0,10},{1,11},{2,12},{3,13},{4,14},{5,15},{6,0},{7,1},{8,2},{9,3},... | collective-permute-start | bytes 405512 | tf_op jit(solution)/shard_map/left_over_z/ppermute | solution.py:287
  26.1 19.6 %collective-permute-start.3 = (bf16[528,128]{1,0:T(8,128)(2,1)S(1)}, bf16[528,128]{1,0:T(8,128)(2,1)S(1)}, u32[]{:S(2)}, u32[]{:S(2)}) collective-permute-start(bf16[528,128]{1,0:T(8,128)(2,1)S(1)} %get-tuple-element.24), channel_id=1, source_target_pairs={{0,4},{1,5},{2,6},{3,7},{4,8},{5,9},{6,10},{7,11},{8,12},{9,13},{1... | collective-permute-start | bytes 405512 | tf_op jit(solution)/shard_map/left_over_z/ppermute | solution.py:287
  27.3 18.4 %collective-permute-start.4 = (bf16[528,128]{1,0:T(8,128)(2,1)S(1)}, bf16[528,128]{1,0:T(8,128)(2,1)S(1)}, u32[]{:S(2)}, u32[]{:S(2)}) collective-permute-start(bf16[528,128]{1,0:T(8,128)(2,1)S(1)} %get-tuple-element.25), channel_id=1, source_target_pairs={{0,12},{1,13},{2,14},{3,15},{4,0},{5,1},{6,2},{7,3},{8,4},{9,5},{1... | collective-permute-start | bytes 405512 | tf_op jit(solution)/shard_map/left_over_z/ppermute | solution.py:287
  29.6 16.1 %collective-permute-start.5 = (bf16[528,128]{1,0:T(8,128)(2,1)S(1)}, bf16[528,128]{1,0:T(8,128)(2,1)S(1)}, u32[]{:S(2)}, u32[]{:S(2)}) collective-permute-start(bf16[528,128]{1,0:T(8,128)(2,1)S(1)} %get-tuple-element.26), channel_id=1, source_target_pairs={{0,2},{1,3},{2,4},{3,5},{4,6},{5,7},{6,8},{7,9},{8,10},{9,11},{10,... | collective-permute-start | bytes 405512 | tf_op jit(solution)/shard_map/left_over_z/ppermute | solution.py:287
  38.4 7.8 %collective-permute-start.6 = (bf16[528,128]{1,0:T(8,128)(2,1)S(1)}, bf16[528,128]{1,0:T(8,128)(2,1)S(1)}, u32[]{:S(2)}, u32[]{:S(2)}) collective-permute-start(bf16[528,128]{1,0:T(8,128)(2,1)S(1)} %get-tuple-element.27), channel_id=1, source_target_pairs={{0,14},{1,15},{2,0},{3,1},{4,2},{5,3},{6,4},{7,5},{8,6},{9,7},{10,... | collective-permute-start | bytes 405512 | tf_op jit(solution)/shard_map/left_over_z/ppermute | solution.py:287
  45.6 38.8 %copy-start = (bf16[16,128,128]{2,1,0:T(8,128)(2,1)S(1)}, bf16[16,128,128]{2,1,0:T(8,128)(2,1)}, u32[]{:S(2)}) copy-start(bf16[16,128,128]{2,1,0:T(8,128)(2,1)} %vectors.3) | copy-start | bytes 1572868
  45.6 38.8 %copy-start.2 = (s32[256]{0:T(256)S(1)}, s32[256]{0:T(256)}, u32[]{:S(2)}) copy-start(s32[256]{0:T(256)} %right_sector.7) | copy-start | bytes 3076
  45.6 38.8 %copy-start.3 = (s32[256]{0:T(256)S(1)}, s32[256]{0:T(256)}, u32[]{:S(2)}) copy-start(s32[256]{0:T(256)} %right_size.3) | copy-start | bytes 3076
  45.7 38.8 %copy-start.4 = (s32[16]{0:T(128)S(1)}, s32[16]{0:T(128)}, u32[]{:S(2)}) copy-start(s32[16]{0:T(128)} %left_size.3) | copy-start | bytes 196
  46.2 38.2 %all-to-all-start.1 = ((bf16[16,2,128,128]{3,2,1,0:T(8,128)(2,1)}), bf16[16,2,128,128]{3,2,1,0:T(8,128)(2,1)S(1)}, u32[]{:S(2)}, u32[]{:S(2)}) async-start(bf16[16,2,128,128]{3,2,1,0:T(8,128)(2,1)} %order.1), calls=%async_computation.1 | async-start | bytes 2097152 | tf_op jit(solution)/shard_map/right_over_mpo/all_to_all | solution.py:310
  57.2 2.0 %collective-permute-start.7 = (bf16[8,272,128]{2,1,0:T(8,128)(2,1)S(1)}, bf16[8,272,128]{2,1,0:T(8,128)(2,1)S(1)}, u32[]{:S(2)}, u32[]{:S(2)}) collective-permute-start(bf16[8,272,128]{2,1,0:T(8,128)(2,1)S(1)} %left_over_core.1), channel_id=1, source_target_pairs={{0,1},{1,0},{2,3},{3,2},{4,5},{5,4},{6,7},{7,6},{8,9},{9,8},{10,11... | collective-permute-start | bytes 1671176 | tf_op jit(solution)/shard_map/left_over_core/ppermute | solution.py:308

commit v5 on v4

v5 whole, which is shorter than its diff:
```python
import jax
import jax.numpy as jnp
from jax import lax
from jax.experimental import pallas as pl
from jax.experimental.pallas import tpu as pltpu
from jax.sharding import PartitionSpec as P

F32 = jnp.float32
BF16 = jnp.bfloat16
SLOTS = 2
PAD = 16
LANES = 8
MIB = 1024 * 1024


def sector_of(chip, core, kind, chips):
    cuts = chips // 2
    return ((chip + chips - 1 - kind) % cuts) * 4 + kind * 2 + core


MOVES = ((0, (0, 1)), (2, (1,)), (-2, (0,)), (1, (0, 1)), (-1, (0, 1)))


def targets(own, chips):
    chip, core = own // 2, own % 2
    return [
        [sector_of((chip + move + chips) % chips, (core + side) % 2, kind, chips) for side in range(2) for kind in kinds]
        for move, kinds in MOVES
    ]


def parts_of(kind):
    found = []
    base = 0
    for index, (_, kinds) in enumerate(MOVES):
        if kind in kinds:
            found.append((index, kinds.index(kind), base + kinds.index(kind)))
        base += len(kinds)
    return found


def start_all(copies):
    for copy in copies:
        copy.start()
    for copy in copies:
        copy.wait()


def pack_right_kernel(right_sector, right_env, right_out, stage, sem):
    blocks = right_env.shape[1]
    devices = right_out.shape[0]
    sec = lax.axis_index("sec")
    load = pltpu.make_async_copy(right_env, stage, sem.at[0])
    load.start()
    base = sec * blocks
    picks = []
    copies = []
    for t in range(devices):
        first = jnp.int32(blocks * blocks)
        last = jnp.int32(0)
        for i in range(blocks):
            offset = right_sector[t * blocks + i] - base
            match = (offset >= 0) & (offset < blocks)
            first = jnp.where(match, jnp.minimum(first, offset + i * blocks), first)
            last = jnp.where(match, offset, last)
        picks.append((first & (blocks - 1), last))
        if t < devices // 4:
            continue
        if t == devices // 4:
            load.wait()
        for ready in range(t + 1 if t == devices // 4 else 1):
            target = ready if t == devices // 4 else t
            for k in range(SLOTS):
                copies.append(pltpu.make_async_copy(stage.at[:, picks[target][k]], right_out.at[target, k], sem.at[1]))
                copies[-1].start()
    for copy in copies:
        copy.wait()


def pack_left_kernel(weights, left_env, *rest):
    *lefts, stage, wbuf, sem = rest
    terms, _, width, _ = left_env.shape
    own = lax.axis_index("mpo")
    load = pltpu.make_async_copy(left_env, stage, sem.at[0])
    load.start()
    row = lax.broadcasted_iota(jnp.int32, wbuf.shape, 0)
    vals = jnp.zeros(wbuf.shape, F32)
    for w in range(terms):
        whole = jnp.full(wbuf.shape, weights[w], F32)
        high = whole.astype(BF16).astype(F32)
        mid = (whole - high).astype(BF16).astype(F32)
        low = whole - high - mid
        for j, part in enumerate((high, mid, low)):
            vals = jnp.where(row == w * 3 + j, part, vals)
    wbuf[...] = vals.astype(BF16)
    load.wait()
    copies = []
    for left, sectors in zip(lefts, targets(own, lax.axis_size("mpo") // 2)):
        for place, q in enumerate(sectors):
            for w in range(terms):
                rows = pl.ds((place * terms + w) * width, width)
                copies.append(pltpu.make_async_copy(stage.at[w, q], left.at[rows], sem.at[1]))
        copies.append(pltpu.make_async_copy(wbuf, left.at[pl.ds(len(sectors) * terms * width, PAD)], sem.at[1]))
    start_all(copies)


def collect_left_kernel(*refs):
    *lefts, given, sem = refs
    size = given.shape[1] - PAD
    copies = []
    place = 0
    for left, (_, kinds) in zip(lefts, MOVES):
        for j in range(len(kinds)):
            rows = pl.ds((len(kinds) + j) * size, size)
            copies.append(pltpu.make_async_copy(left.at[rows], given.at[place, pl.ds(0, size)], sem))
            pad = pl.ds(2 * len(kinds) * size, PAD)
            copies.append(pltpu.make_async_copy(left.at[pad], given.at[place, pl.ds(size, PAD)], sem))
            place += 1
    start_all(copies)


def collect_right_kernel(*refs):
    *rights, given, sem = refs
    copies = []
    place = 0
    for right, (_, kinds) in zip(rights, MOVES):
        count = len(kinds)
        copies.append(pltpu.make_async_copy(right.at[pl.ds(count, count)], given.at[pl.ds(place, count)], sem))
        place += count
    start_all(copies)


def order_kernel(right_sector, arrived, *rest):
    *rights, stage, places, sem = rest
    blocks = stage.shape[0]
    sec = lax.axis_index("sec")
    own = lax.axis_index("mpo")
    shift = blocks.bit_length() - 1
    sources = [lax.shift_right_logical(right_sector[sec * blocks + q], shift) for q in range(blocks)]
    for q in range(blocks):
        again = jnp.bool_(False)
        for other in range(q):
            again = again | (sources[other] == sources[q])
        places[q] = sources[q] * SLOTS + jnp.where(again, 1, 0)
    loads = []
    for sectors in targets(own, lax.axis_size("mpo") // 2):
        for q in sectors:
            index = len(loads)
            load = pltpu.make_async_copy(arrived.at[places[q]], stage.at[index], sem.at[index])
            load.start()
            loads.append(load)
    stores = []
    first = 0
    for right in rights:
        count = right.shape[0]
        for index in range(first, first + count):
            loads[index].wait()
        stores.append(pltpu.make_async_copy(stage.at[pl.ds(first, count)], right, sem.at[blocks]))
        stores[-1].start()
        first += count
    for store in stores:
        store.wait()


def live(rows, left, right):
    row = lax.broadcasted_iota(jnp.int32, rows, 0)
    col = lax.broadcasted_iota(jnp.int32, rows, 1)
    return (row < left) & (col < right)


def total(x):
    return jnp.sum(jnp.sum(x, axis=0, keepdims=True), axis=1, keepdims=True)


def apply(block, kind, lefts, given_left, rights, given_right):
    _, terms, width, _ = given_right.shape
    size = terms * width
    acc = jnp.zeros((width, width), F32)
    for index, place, other in parts_of(kind):
        for side in range(2):
            if side == 0:
                left = lefts[index][place * size : (place + 1) * size]
                scale = lefts[index][lefts[index].shape[0] - PAD :].astype(F32)
                right = [rights[index][place, w] for w in range(terms)]
            else:
                left = given_left[other, :size]
                scale = given_left[other, size:].astype(F32)
                right = [given_right[other, w] for w in range(terms)]
            half = jnp.dot(left, block, preferred_element_type=F32)
            halves = []
            for w in range(terms):
                weight = scale[3 * w : 3 * w + 1] + scale[3 * w + 1 : 3 * w + 2] + scale[3 * w + 2 : 3 * w + 3]
                halves.append((weight * half[w * width : (w + 1) * width]).astype(BF16))
            acc = acc + lax.dot_general(
                jnp.concatenate(halves, axis=1),
                jnp.concatenate(right, axis=1),
                (((1,), (1,)), ((), ())),
                preferred_element_type=F32,
            )
    return acc


def own_sector(kind):
    own = lax.axis_index("mpo")
    return sector_of(own // 2, own % 2, kind, lax.axis_size("mpo") // 2)


def start_vector(kind, left_size, right_size, right_sector, vector):
    width = vector.shape[1]
    q = own_sector(kind)
    sec = lax.axis_index("sec")
    mask = live((width, width), left_size[q], right_size[right_sector[sec * left_size.shape[0] + q]])
    return mask, jnp.where(mask, vector[kind].astype(F32), 0.0)


def load_vectors(vectors, vector, sem):
    start_all([pltpu.make_async_copy(vectors.at[own_sector(kind)], vector.at[kind], sem) for kind in range(2)])


def first_kernel(left_size, right_size, right_sector, vectors, *rest):
    *blocks, out, vector, sem = rest
    half = len(blocks) // 2
    lefts, rights = blocks[: half - 1], blocks[half:-1]
    load_vectors(vectors, vector, sem)
    for kind in range(2):
        _, start = start_vector(kind, left_size, right_size, right_sector, vector)
        out[kind] = apply(start.astype(BF16), kind, lefts, blocks[half - 1], rights, blocks[-1])


def second_kernel(left_size, right_size, right_sector, vectors, image_here, image_there, *rest):
    *blocks, out, vector, sem = rest
    half = len(blocks) // 2
    lefts, rights = blocks[: half - 1], blocks[half:-1]
    width = vector.shape[1]
    upper = lax.axis_index("mpo") // 2 >= lax.axis_size("mpo") // 4
    load_vectors(vectors, vector, sem)
    parts = out.shape[0]
    rows = width // parts
    lane = lax.broadcasted_iota(jnp.int32, (8, width), 1)
    line = jnp.zeros((8, width), F32)
    rests = []
    for kind in range(2):
        mask, start = start_vector(kind, left_size, right_size, right_sector, vector)
        norm = total(start * start)
        scale = 1.0 / jnp.sqrt(norm / float(width * width) + 1e-06)
        image = jnp.where(mask, image_here[kind] + image_there[kind], 0.0) * scale
        unit = start * scale
        length = total(unit * unit)
        overlap = total(unit * image)
        ratio = jnp.where(length > 0.0, overlap / jnp.where(length > 0.0, length, 1.0), 0.0)
        rest = image - ratio * unit
        after = jnp.where(mask, apply(rest.astype(BF16), kind, lefts, blocks[half - 1], rights, blocks[-1]), 0.0)
        share = jnp.where(upper == (kind == 1), 1.0, 0.0)
        numbers = (
            share * norm,
            share * overlap,
            share * ratio,
            share * total(rest * rest),
            total(rest * after),
            total(unit * after) + share * total(rest * image),
            share * total(rest * unit),
        )
        place = own_sector(kind) * LANES
        for j, number in enumerate(numbers):
            line = jnp.where(lane == place + j, number, line)
        rests.append(rest)
        for d in range(parts):
            out[d, (1 + kind) * rows : (2 + kind) * rows] = after[d * rows : (d + 1) * rows]
    chosen = jnp.where(upper, rests[1], rests[0])
    for d in range(parts):
        out[d, :rows] = chosen[d * rows : (d + 1) * rows]
        out[d, 3 * rows :] = line


def finish_kernel(left_size, right_size, right_sector, vectors, pieces, shared, next_out, rest_out, coef_out, vector, sem):
    blocks, rows, width = next_out.shape
    sec = lax.axis_index("sec")
    part = lax.axis_index("mpo")
    devices = shared.shape[0]
    groups = PAD // rows
    load = pltpu.make_async_copy(vectors.at[:, pl.ds(pl.multiple_of(part // groups * PAD, PAD), PAD)], vector, sem)
    load.start()
    entries = float(devices * blocks * width * width)
    cells = float(width * width)
    stats = shared[:, 0, :]
    line = shared[sec][:1]
    chips = lax.axis_size("mpo") // 2
    lane = lax.broadcasted_iota(jnp.int32, stats.shape, 1) % LANES

    def field(x, j):
        return x if j == 0 else pltpu.roll(x, x.shape[1] - j, 1)

    lead = lane == 0
    norm = jnp.where(lead, field(stats, 0), 0.0)
    overlap = field(stats, 1)
    ratio = field(stats, 2)
    gain = 1.0 / jnp.sqrt(total(norm) / entries + 1e-06)
    mean = jnp.where(lead, norm, 0.0) / cells + 1e-06
    weight = jnp.where(lead, (gain * gain) * mean, 0.0)
    length = norm / mean
    alpha = total(jnp.where(lead, weight * overlap, 0.0)) / entries
    delta = jnp.where(lead, ratio - alpha, 0.0)
    rest_total = total(jnp.where(lead, weight * (field(stats, 3) + delta * delta * length + 2.0 * delta * field(stats, 6)), 0.0))
    beta = jnp.sqrt(rest_total / entries + 1e-06)
    inner = field(stats, 4) + delta * field(stats, 5) + delta * delta * overlap
    alpha_next = total(jnp.where(lead, weight * inner, 0.0)) / entries / beta / beta
    for j, number in enumerate((alpha, beta, alpha_next)):
        coef_out[j] = number[0, 0]
    load.wait()
    for q in range(blocks):
        cut, kind, core = q // 4, q // 2 % 2, q % 2
        lower = 2 * ((cut + 1 + kind) % (chips // 2)) + core
        higher = lower + chips
        lane_one = lax.broadcasted_iota(jnp.int32, line.shape, 1)
        norm_q = jnp.sum(jnp.where(lane_one == q * LANES, line, 0.0), axis=1, keepdims=True)
        ratio_q = jnp.sum(jnp.where(lane_one == q * LANES + 2, line, 0.0), axis=1, keepdims=True)
        root = jnp.sqrt(norm_q / cells + 1e-06)
        scale = gain * root
        row = lax.broadcasted_iota(jnp.int32, (rows, width), 0) + part * rows
        col = lax.broadcasted_iota(jnp.int32, (rows, width), 1)
        mask = (row < left_size[q]) & (col < right_size[right_sector[sec * blocks + q]])
        group = vector[q].astype(F32)
        own_rows = group[:rows]
        for j in range(1, groups):
            own_rows = jnp.where(part % groups == j, group[j * rows : (j + 1) * rows], own_rows)
        unit = jnp.where(mask, own_rows, 0.0) / root
        rest = pieces[higher if kind else lower, :rows]
        after_rows = slice((1 + kind) * rows, (2 + kind) * rows)
        after = pieces[lower, after_rows] + pieces[higher, after_rows]
        shift = ratio_q - alpha
        second = (scale / beta) * (rest + shift * unit)
        image = (scale / beta) * (after + shift * (rest + ratio_q * unit))
        next_out[q] = second
        rest_out[q] = image - alpha_next * second - (beta * scale) * unit


def shards(
    wavefunction,
    left_size,
    right_size,
    right_sector,
    left_environment,
    right_environment,
    term_weights,
):
    blocks, width, _ = wavefunction.shape
    terms = left_environment.shape[0]
    devices = lax.axis_size("sec")
    layers = lax.axis_size("mpo")
    rows = width // layers
    anywhere = pl.BlockSpec(memory_space=pl.ANY)
    scalars = pl.BlockSpec(memory_space=pltpu.SMEM)
    vmem = pl.BlockSpec(memory_space=pltpu.VMEM)

    chips = layers // 2
    long = terms * width
    routes = [[(p, (p + 2 * move) % layers) for p in range(layers)] for move, _ in MOVES]
    counts = [2 * len(kinds) for _, kinds in MOVES]
    cores = [(p, p ^ 1) for p in range(layers)]
    with jax.named_scope("pack_right"):
        right_out = pl.pallas_call(
            pack_right_kernel,
            out_shape=jax.ShapeDtypeStruct((devices, SLOTS, terms, width, width), BF16),
            in_specs=[scalars, anywhere],
            out_specs=anywhere,
            scratch_shapes=[pltpu.VMEM(right_environment.shape, BF16), pltpu.SemaphoreType.DMA((2,))],
            compiler_params=pltpu.CompilerParams(vmem_limit_bytes=60 * MIB),
        )(right_sector, right_environment)
    with jax.named_scope("right_over_sec"):
        arrived = lax.all_to_all(right_out, "sec", 0, 0, tiled=True)
    with jax.named_scope("pack_left"):
        lefts = pl.pallas_call(
            pack_left_kernel,
            out_shape=[jax.ShapeDtypeStruct((count * long + PAD, width), BF16) for count in counts],
            in_specs=[scalars, anywhere],
            out_specs=[anywhere] * len(MOVES),
            scratch_shapes=[
                pltpu.VMEM(left_environment.shape, BF16),
                pltpu.VMEM((PAD, width), BF16),
                pltpu.SemaphoreType.DMA((2,)),
            ],
            compiler_params=pltpu.CompilerParams(vmem_limit_bytes=8 * MIB),
        )(term_weights, left_environment)
    with jax.named_scope("left_over_z"):
        lefts = [lefts[0]] + [lax.ppermute(left, "mpo", route) for left, route in zip(lefts[1:], routes[1:])]
    with jax.named_scope("left_over_core"):
        given = pl.pallas_call(
            collect_left_kernel,
            out_shape=jax.ShapeDtypeStruct((blocks // 2, long + PAD, width), BF16),
            in_specs=[anywhere] * len(MOVES),
            out_specs=anywhere,
            scratch_shapes=[pltpu.SemaphoreType.DMA],
            compiler_params=pltpu.CompilerParams(vmem_limit_bytes=4 * MIB),
        )(*lefts)
        lefts.append(lax.ppermute(given, "mpo", cores))
        arrived, *lefts = lax.optimization_barrier((arrived, *lefts))
    with jax.named_scope("order"):
        rights = pl.pallas_call(
            order_kernel,
            out_shape=[jax.ShapeDtypeStruct((count, terms, width, width), BF16) for count in counts],
            in_specs=[scalars, anywhere],
            out_specs=[anywhere] * len(MOVES),
            scratch_shapes=[
                pltpu.VMEM((blocks, terms, width, width), BF16),
                pltpu.SMEM((blocks,), jnp.int32),
                pltpu.SemaphoreType.DMA((blocks + 1,)),
            ],
            compiler_params=pltpu.CompilerParams(vmem_limit_bytes=60 * MIB),
        )(right_sector, arrived.reshape(devices * SLOTS, terms, width, width))
    with jax.named_scope("right_over_z"):
        rights = [rights[0]] + [lax.ppermute(right, "mpo", route) for right, route in zip(rights[1:], routes[1:])]
    with jax.named_scope("right_over_core"):
        given = pl.pallas_call(
            collect_right_kernel,
            out_shape=jax.ShapeDtypeStruct((blocks // 2, terms, width, width), BF16),
            in_specs=[anywhere] * len(MOVES),
            out_specs=anywhere,
            scratch_shapes=[pltpu.SemaphoreType.DMA],
            compiler_params=pltpu.CompilerParams(vmem_limit_bytes=4 * MIB),
        )(*rights)
        rights.append(lax.ppermute(given, "mpo", cores))
    with jax.named_scope("first_image"):
        image_here = pl.pallas_call(
            first_kernel,
            out_shape=jax.ShapeDtypeStruct((2, width, width), F32),
            in_specs=[scalars, scalars, scalars, anywhere] + [vmem] * (2 * len(MOVES) + 2),
            out_specs=vmem,
            scratch_shapes=[pltpu.VMEM((2, width, width), BF16), pltpu.SemaphoreType.DMA],
            compiler_params=pltpu.CompilerParams(vmem_limit_bytes=16 * MIB),
        )(left_size, right_size, right_sector, wavefunction, *lefts, *rights)
    with jax.named_scope("swap_images"):
        image_there = lax.ppermute(image_here, "mpo", [(p, (p + chips) % layers) for p in range(layers)])
    with jax.named_scope("second_image"):
        pieces = pl.pallas_call(
            second_kernel,
            out_shape=jax.ShapeDtypeStruct((layers, 3 * rows + 8, width), F32),
            in_specs=[scalars, scalars, scalars, anywhere] + [vmem] * (2 * len(MOVES) + 4),
            out_specs=vmem,
            scratch_shapes=[pltpu.VMEM((2, width, width), BF16), pltpu.SemaphoreType.DMA],
            compiler_params=pltpu.CompilerParams(vmem_limit_bytes=16 * MIB),
        )(left_size, right_size, right_sector, wavefunction, image_here, image_there, *lefts, *rights)
    with jax.named_scope("rows_over_mpo"):
        pieces = lax.all_to_all(pieces, "mpo", 0, 0, tiled=True)
    with jax.named_scope("numbers_over_sec"):
        line = jnp.sum(pieces[:, 3 * rows :, :], axis=0)
        shared = lax.all_to_all(jnp.broadcast_to(line[None], (devices, 8, width)), "sec", 0, 0, tiled=True)
    with jax.named_scope("finish"):
        next_vector, residual, coefficients = pl.pallas_call(
            finish_kernel,
            out_shape=(
                jax.ShapeDtypeStruct((blocks, rows, width), F32),
                jax.ShapeDtypeStruct((blocks, rows, width), F32),
                jax.ShapeDtypeStruct((3,), F32),
            ),
            in_specs=[scalars, scalars, scalars, anywhere, vmem, vmem],
            out_specs=(vmem, vmem, scalars),
            scratch_shapes=[pltpu.VMEM((blocks, PAD, width), BF16), pltpu.SemaphoreType.DMA],
            compiler_params=pltpu.CompilerParams(vmem_limit_bytes=8 * MIB),
        )(left_size, right_size, right_sector, wavefunction, pieces, shared)
    return (next_vector, residual, coefficients)


def solution(mesh):
    placed = (
        P("sec", None, None),
        P("sec"),
        P(),
        P(),
        P("mpo", "sec", None, None),
        P("mpo", "sec", None, None),
        P("mpo"),
    )
    return jax.shard_map(
        shards,
        mesh=mesh,
        in_specs=placed,
        out_specs=(P("sec", "mpo", None), P("sec", "mpo", None), P()),
        check_vma=False,
    )
```

time: 112 us -> 114 us (1.018)
  waiting for transfers between devices: 39.9 us -> 28.1 us
  blocking collectives: 23.2 us -> 31.5 us
  starting transfers between devices: 34.1 us -> 36.4 us
  local copies, waits for them, and re-layouts: 0.05 us -> 1.93 us
    all_to_all x1 -> x0, waiting for transfers between devices: 25.2 us -> none  [shards(): right_terms = lax.all_to_all(ordered, 'mpo', 0, 0, tiled=True)]
    ppermute x8 -> x11, starting transfers between devices: 16 us -> 28.6 us  [the longest x4 9.32 us: shards(): lax.ppermute(left, 'mpo', route)]
    all_to_all x1 -> x0, starting transfers between devices: 10.3 us -> none  [shards(): right_terms = lax.all_to_all(ordered, 'mpo', 0, 0, tiled=True)]
    ppermute x8 -> x11, waiting for transfers between devices: 10.3 us -> 20.5 us  [the longest x4 7.04 us: shards(): lax.ppermute(left, 'mpo', route)]
    all_to_all x1, blocking collectives: 13.6 us -> 20.7 us  [shards(): pieces = lax.all_to_all(pieces, 'mpo', 0, 0, tiled=True)]
    all_to_all x1, waiting for transfers between devices: 4.42 us -> 7.59 us  [shards(): arrived = lax.all_to_all(right_out, 'sec', 0, 0, tiled=True)]
    unnamed x12 -> x16, local copies, waits for them, and re-layouts: 0.04 us -> 1.92 us
    pallas_call x4 -> x6, Pallas kernels: 8.41 us -> 10.1 us  [the longest x1 2.92 us: shards(): pl.pallas_call(order_kernel, out_shape=[jax.ShapeDtypeStruct((count, term...]
  transfers between devices with their start and end apart: 10 -> 12, of which waited for: 5 -> 6; matrix products, arithmetic and copies ran while one was open for 0% -> 0% of each run, Pallas kernels for 5% -> 3%
where the time goes in v5:
time: 114 us
  starting transfers between devices  36.4 us (32%)
  blocking collectives  31.5 us (28%)
  waiting for transfers between devices  28.1 us (25%)
  Pallas kernels  15.1 us (13%)
  local copies, waits for them, and re-layouts  1.93 us (2%)
    all_to_all x1, blocking collectives, shards(): pieces = lax.all_to_all(pieces, 'mpo', 0, 0, tiled=True)  20.7 us
    all_to_all x1, blocking collectives, shards(): lax.all_to_all(jnp.broadcast_to(line[None], (devices, 8, width)), 'sec',...  10.9 us
    ppermute x4, starting transfers between devices, shards(): lax.ppermute(left, 'mpo', route)  9.32 us
    ppermute x4, starting transfers between devices, shards(): lax.ppermute(right, 'mpo', route)  9.32 us
    all_to_all x1, starting transfers between devices, shards(): arrived = lax.all_to_all(right_out, 'sec', 0, 0, tiled=True)  7.78 us
    all_to_all x1, waiting for transfers between devices, shards(): arrived = lax.all_to_all(right_out, 'sec', 0, 0, tiled=True)  7.59 us
    ppermute x4, waiting for transfers between devices, shards(): lax.ppermute(left, 'mpo', route)  7.04 us
    ppermute x4, waiting for transfers between devices, shards(): lax.ppermute(right, 'mpo', route)  5.58 us
  transfers between devices with their start and end apart: 12, of which 6 were waited for; matrix products, arithmetic and copies ran while one was open for 0% of the time, Pallas kernels for 3%

profile of v5, /device:TPU:1, one launch (start us, length us, event | category | flops | bytes accessed | tf_op | source)
XLA Modules:
  0.0 114.0 jit_solution(15782043985598792080)
XLA Ops:
  0.6 3.2 %pack_right.1 = bf16[16,2,2,128,128]{4,3,2,1,0:T(8,128)(2,1)} custom-call(s32[256]{0:T(256)} %right_sector.9, bf16[2,16,128,128]{3,2,1,0:T(8,128)(2,1)} %right_env.1), custom_call_target="tpu_custom_call" | custom-call | tf_op jit(solution)/shard_map/pack_right/pallas_call | solution.py:361
  3.9 0.0 copy-start.3
  3.9 0.0 copy-start.7
  3.9 7.8 %all-to-all-start = ((bf16[16,2,2,128,128]{4,3,2,1,0:T(8,128)(2,1)}), bf16[16,2,2,128,128]{4,3,2,1,0:T(8,128)(2,1)}, u32[]{:S(2)}, u32[]{:S(2)}) async-start(bf16[16,2,2,128,128]{4,3,2,1,0:T(8,128)(2,1)} %pack_right.1), calls=%async_computation | async-start | bytes 4194304 | tf_op jit(solution)/shard_map/right_over_sec/all_to_all | solution.py:370
  11.7 0.0 copy-done.3
  11.7 0.0 copy-done.7
  11.7 2.2 %pack_left.1 = (bf16[1040,128]{1,0:T(8,128)(2,1)S(1)}, bf16[528,128]{1,0:T(8,128)(2,1)S(1)}, bf16[528,128]{1,0:T(8,128)(2,1)S(1)}, bf16[1040,128]{1,0:T(8,128)(2,1)S(1)}, bf16[1040,128]{1,0:T(8,128)(2,1)S(1)}) custom-call(f32[2]{0:T(128)S(1)} %copy-done.7, bf16[2,16,128,128]{3,2,1,0:T(8,128)(2,1)S(1)} %copy-done.3), custom_call_target="tpu_custom_call" | custom-call | tf_op jit(solution)/shard_map/pack_left/pallas_call | solution.py:372
  13.9 1.7 %collective-permute-start.2 = (bf16[1040,128]{1,0:T(8,128)(2,1)S(1)}, bf16[1040,128]{1,0:T(8,128)(2,1)S(1)}, u32[]{:S(2)}, u32[]{:S(2)}) collective-permute-start(bf16[1040,128]{1,0:T(8,128)(2,1)S(1)} %get-tuple-element.23), channel_id=1, source_target_pairs={{0,2},{1,3},{2,4},{3,5},{4,6},{5,7},{6,8},{7,9},{8,10},{9,11},{10,... | collective-permute-start | bytes 798728 | tf_op jit(solution)/shard_map/left_over_z/ppermute | solution.py:385
  15.6 4.0 %collective-permute-start.3 = (bf16[1040,128]{1,0:T(8,128)(2,1)S(1)}, bf16[1040,128]{1,0:T(8,128)(2,1)S(1)}, u32[]{:S(2)}, u32[]{:S(2)}) collective-permute-start(bf16[1040,128]{1,0:T(8,128)(2,1)S(1)} %get-tuple-element.24), channel_id=1, source_target_pairs={{0,14},{1,15},{2,0},{3,1},{4,2},{5,3},{6,4},{7,5},{8,6},{9,7},{10,... | collective-permute-start | bytes 798728 | tf_op jit(solution)/shard_map/left_over_z/ppermute | solution.py:385
  19.6 0.0 collective-permute-start
  19.6 3.6 %collective-permute-start.1 = (bf16[528,128]{1,0:T(8,128)(2,1)S(1)}, bf16[528,128]{1,0:T(8,128)(2,1)S(1)}, u32[]{:S(2)}, u32[]{:S(2)}) collective-permute-start(bf16[528,128]{1,0:T(8,128)(2,1)S(1)} %get-tuple-element.22), channel_id=1, source_target_pairs={{0,12},{1,13},{2,14},{3,15},{4,0},{5,1},{6,2},{7,3},{8,4},{9,5},{1... | collective-permute-start | bytes 405512 | tf_op jit(solution)/shard_map/left_over_z/ppermute | solution.py:385
  23.2 7.0 %collective-permute-done.refs_1_.rest_1_ = bf16[528,128]{1,0:T(8,128)(2,1)S(1)} collective-permute-done((bf16[528,128]{1,0:T(8,128)(2,1)S(1)}, bf16[528,128]{1,0:T(8,128)(2,1)S(1)}, u32[]{:S(2)}, u32[]{:S(2)}) %collective-permute-start) | collective-permute-done | bytes 135200 | tf_op jit(solution)/shard_map/left_over_z/ppermute | solution.py:385
  30.3 0.0 collective-permute-done.1.refs_2_.rest_2_
  30.3 0.0 collective-permute-done.2.refs_3_.rest_3_
  30.3 0.0 collective-permute-done.3.refs_4_.rest_4_
  30.3 0.7 left_over_core.1
  31.0 0.0 copy-start
  31.0 0.0 copy-start.4
  31.0 0.0 copy-start.5
  31.0 0.0 copy-start.6
  31.1 2.0 %collective-permute-start.4 = (bf16[8,272,128]{2,1,0:T(8,128)(2,1)S(1)}, bf16[8,272,128]{2,1,0:T(8,128)(2,1)S(1)}, u32[]{:S(2)}, u32[]{:S(2)}) collective-permute-start(bf16[8,272,128]{2,1,0:T(8,128)(2,1)S(1)} %left_over_core.1), channel_id=1, source_target_pairs={{0,1},{1,0},{2,3},{3,2},{4,5},{5,4},{6,7},{7,6},{8,9},{9,8},{10,11... | collective-permute-start | bytes 1671176 | tf_op jit(solution)/shard_map/left_over_core/ppermute | solution.py:395
  33.1 1.6 %collective-permute-done.4.rest_5_ = bf16[8,272,128]{2,1,0:T(8,128)(2,1)S(1)} collective-permute-done((bf16[8,272,128]{2,1,0:T(8,128)(2,1)S(1)}, bf16[8,272,128]{2,1,0:T(8,128)(2,1)S(1)}, u32[]{:S(2)}, u32[]{:S(2)}) %collective-permute-start.4) | collective-permute-done | bytes 557088 | tf_op jit(solution)/shard_map/left_over_core/ppermute | solution.py:395
  34.6 7.6 %all-to-all-done = bf16[16,2,2,128,128]{4,3,2,1,0:T(8,128)(2,1)} async-done(((bf16[16,2,2,128,128]{4,3,2,1,0:T(8,128)(2,1)}), bf16[16,2,2,128,128]{4,3,2,1,0:T(8,128)(2,1)}, u32[]{:S(2)}, u32[]{:S(2)}) %all-to-all-start) | async-done | bytes 2097184 | tf_op jit(solution)/shard_map/right_over_sec/all_to_all | solution.py:370
  42.2 2.9 %order.1 = (bf16[4,2,128,128]{3,2,1,0:T(8,128)(2,1)}, bf16[2,2,128,128]{3,2,1,0:T(8,128)(2,1)}, bf16[2,2,128,128]{3,2,1,0:T(8,128)(2,1)}, bf16[4,2,128,128]{3,2,1,0:T(8,128)(2,1)}, bf16[4,2,128,128]{3,2,1,0:T(8,128)(2,1)}) custom-call(s32[256]{0:T(256)} %right_sector.9, bf16[32,2,128,128]{3,2,1,0:T(8,128)(2,1)} %bitcast.arrived), custom_call_target="tpu_custom_call" | custom-call | tf_op jit(solution)/shard_map/order/pallas_call | solution.py:398
  45.2 1.7 %collective-permute-start.7 = (bf16[4,2,128,128]{3,2,1,0:T(8,128)(2,1)}, bf16[4,2,128,128]{3,2,1,0:T(8,128)(2,1)S(1)}, u32[]{:S(2)}, u32[]{:S(2)}) collective-permute-start(bf16[4,2,128,128]{3,2,1,0:T(8,128)(2,1)} %get-tuple-element.35), channel_id=1, source_target_pairs={{0,2},{1,3},{2,4},{3,5},{4,6},{5,7},{6,8},{7,9},{8,10},{9,11},{10,... | collective-permute-start | bytes 786440 | tf_op jit(solution)/shard_map/right_over_z/ppermute | solution.py:411
  46.9 4.0 %collective-permute-start.8 = (bf16[4,2,128,128]{3,2,1,0:T(8,128)(2,1)}, bf16[4,2,128,128]{3,2,1,0:T(8,128)(2,1)S(1)}, u32[]{:S(2)}, u32[]{:S(2)}) collective-permute-start(bf16[4,2,128,128]{3,2,1,0:T(8,128)(2,1)} %get-tuple-element.36), channel_id=1, source_target_pairs={{0,14},{1,15},{2,0},{3,1},{4,2},{5,3},{6,4},{7,5},{8,6},{9,7},{10,... | collective-permute-start | bytes 786440 | tf_op jit(solution)/shard_map/right_over_z/ppermute | solution.py:411
  50.9 0.0 collective-permute-start.5
  50.9 3.6 %collective-permute-start.6 = (bf16[2,2,128,128]{3,2,1,0:T(8,128)(2,1)}, bf16[2,2,128,128]{3,2,1,0:T(8,128)(2,1)S(1)}, u32[]{:S(2)}, u32[]{:S(2)}) collective-permute-start(bf16[2,2,128,128]{3,2,1,0:T(8,128)(2,1)} %get-tuple-element.34), channel_id=1, source_target_pairs={{0,12},{1,13},{2,14},{3,15},{4,0},{5,1},{6,2},{7,3},{8,4},{9,5},{1... | collective-permute-start | bytes 393224 | tf_op jit(solution)/shard_map/right_over_z/ppermute | solution.py:411
  54.5 5.6 %collective-permute-done.5.refs_1_.rest_7_ = bf16[2,2,128,128]{3,2,1,0:T(8,128)(2,1)S(1)} collective-permute-done((bf16[2,2,128,128]{3,2,1,0:T(8,128)(2,1)}, bf16[2,2,128,128]{3,2,1,0:T(8,128)(2,1)S(1)}, u32[]{:S(2)}, u32[]{:S(2)}) %collective-permute-start.5) | collective-permute-done | bytes 131104 | tf_op jit(solution)/shard_map/right_over_z/ppermute | solution.py:411
  60.1 0.0 collective-permute-done.6.refs_2_.rest_8_
  60.1 0.0 collective-permute-done.7.refs_3_.rest_9_
  60.1 0.0 collective-permute-done.8.refs_4_.rest_10_
  60.1 0.0 copy-start.1
  60.1 0.9 copy-done.1
  61.0 0.7 right_over_core.1
  61.7 4.1 %collective-permute-start.9 = (bf16[8,2,128,128]{3,2,1,0:T(8,128)(2,1)S(1)}, bf16[8,2,128,128]{3,2,1,0:T(8,128)(2,1)S(1)}, u32[]{:S(2)}, u32[]{:S(2)}) collective-permute-start(bf16[8,2,128,128]{3,2,1,0:T(8,128)(2,1)S(1)} %right_over_core.1), channel_id=1, source_target_pairs={{0,1},{1,0},{2,3},{3,2},{4,5},{5,4},{6,7},{7,6},{8,9},{9,8},{10,11... | collective-permute-start | bytes 1572872 | tf_op jit(solution)/shard_map/right_over_core/ppermute | solution.py:421
  65.8 1.5 %collective-permute-done.9.rest_11_ = bf16[8,2,128,128]{3,2,1,0:T(8,128)(2,1)S(1)} collective-permute-done((bf16[8,2,128,128]{3,2,1,0:T(8,128)(2,1)S(1)}, bf16[8,2,128,128]{3,2,1,0:T(8,128)(2,1)S(1)}, u32[]{:S(2)}, u32[]{:S(2)}) %collective-permute-start.9) | collective-permute-done | bytes 524320 | tf_op jit(solution)/shard_map/right_over_core/ppermute | solution.py:421
  67.3 0.0 copy-done
  67.3 0.0 copy-done.4
  67.3 0.0 copy-done.5
  67.3 0.9 copy-done.2
  68.3 1.7 %first_image.1.image_here = f32[2,128,128]{2,1,0:T(8,128)S(1)} custom-call(s32[16]{0:T(128)S(1)} %copy-done.6, s32[256]{0:T(256)S(1)} %copy-done.5, s32[256]{0:T(256)S(1)} %copy-done.4, bf16[16,128,128]{2,1,0:T(8,128)(2,1)S(1)} %copy-done, bf16[1040,128]{1,0:T(8,128)(2,1)S(1)} %get-tuple-element.25.refs_0_.rest_0_, ...), custom_call_target="tpu_custom_call" | custom-call | tf_op jit(solution)/shard_map/first_image/pallas_call | solution.py:423
  69.9 3.9 %collective-permute-start.10 = (f32[2,128,128]{2,1,0:T(8,128)S(1)}, f32[2,128,128]{2,1,0:T(8,128)S(1)}, u32[]{:S(2)}, u32[]{:S(2)}) collective-permute-start(f32[2,128,128]{2,1,0:T(8,128)S(1)} %first_image.1.image_here), channel_id=1, source_target_pairs={{0,8},{1,9},{2,10},{3,11},{4,12},{5,13},{6,14},{7,15},{8,0},{9,1},... | collective-permute-start | bytes 393224 | tf_op jit(solution)/shard_map/swap_images/ppermute | solution.py:432
  73.9 4.8 %collective-permute-done.10.image_there = f32[2,128,128]{2,1,0:T(8,128)S(1)} collective-permute-done((f32[2,128,128]{2,1,0:T(8,128)S(1)}, f32[2,128,128]{2,1,0:T(8,128)S(1)}, u32[]{:S(2)}, u32[]{:S(2)}) %collective-permute-start.10) | collective-permute-done | bytes 131104 | tf_op jit(solution)/shard_map/swap_images/ppermute | solution.py:432
  78.6 2.0 %second_image.1 = f32[16,32,128]{2,1,0:T(8,128)S(1)} custom-call(s32[16]{0:T(128)S(1)} %copy-done.6, s32[256]{0:T(256)S(1)} %copy-done.5, s32[256]{0:T(256)S(1)} %copy-done.4, bf16[16,128,128]{2,1,0:T(8,128)(2,1)S(1)} %copy-done, f32[2,128,128]{2,1,0:T(8,128)S(1)} %first_image.1.image_here, f32[2,128,128]{2,1,0:T(8,128)S(1)} %collective-permute-done.10.image_there, ...), custom_call_target="tpu_custom_call" | custom-call | tf_op jit(solution)/shard_map/second_image/pallas_call | solution.py:434
  80.6 20.7 %all_to_all.15.pieces = f32[16,32,128]{2,1,0:T(8,128)S(1)} all-to-all(f32[16,32,128]{2,1,0:T(8,128)S(1)} %second_image.1), channel_id=1, replica_groups=mesh['sec'=16,'mpo'=16] {'mpo'}, dimensions={0} | all-to-all | bytes 524288 | tf_op jit(solution)/shard_map/rows_over_mpo/all_to_all | solution.py:443
  101.3 10.9 %all_to_all.16.shared = f32[16,8,128]{2,1,0:T(8,128)S(1)} all-to-all(f32[16,8,128]{2,1,0:T(8,128)S(1)} %broadcast_in_dim.2), channel_id=1, replica_groups=mesh['sec'=16,'mpo'=16] {'sec'}, dimensions={0} | all-to-all | bytes 131072 | tf_op jit(solution)/shard_map/numbers_over_sec/all_to_all | solution.py:446
  112.2 1.8 %finish.1 = (f32[16,8,128]{2,1,0:T(8,128)}, f32[16,8,128]{2,1,0:T(8,128)}, f32[3]{0:T(128)}) custom-call(s32[16]{0:T(128)S(1)} %copy-done.6, s32[256]{0:T(256)S(1)} %copy-done.5, s32[256]{0:T(256)S(1)} %copy-done.4, bf16[16,128,128]{2,1,0:T(8,128)(2,1)S(1)} %copy-done, f32[16,32,128]{2,1,0:T(8,128)S(1)} %all_to_all.15.pieces, ...), custom_call_target="tpu_custom_call" | custom-call | tf_op jit(solution)/shard_map/finish/pallas_call | solution.py:448
  (4 shorter events, 0.0 us)
Async XLA Ops:
  3.9 7.8 %copy-start.3 = (bf16[2,16,128,128]{3,2,1,0:T(8,128)(2,1)S(1)}, bf16[2,16,128,128]{3,2,1,0:T(8,128)(2,1)}, u32[]{:S(2)}) copy-start(bf16[2,16,128,128]{3,2,1,0:T(8,128)(2,1)} %left_env.1) | copy-start | bytes 3145732
  3.9 7.8 %copy-start.7 = (f32[2]{0:T(128)S(1)}, f32[2]{0:T(128)}, u32[]{:S(2)}) copy-start(f32[2]{0:T(128)} %weights.1) | copy-start | bytes 28
  3.9 38.3 %all-to-all-start = ((bf16[16,2,2,128,128]{4,3,2,1,0:T(8,128)(2,1)}), bf16[16,2,2,128,128]{4,3,2,1,0:T(8,128)(2,1)}, u32[]{:S(2)}, u32[]{:S(2)}) async-start(bf16[16,2,2,128,128]{4,3,2,1,0:T(8,128)(2,1)} %pack_right.1), calls=%async_computation | async-start | bytes 4194304 | tf_op jit(solution)/shard_map/right_over_sec/all_to_all | solution.py:370
  13.9 16.4 %collective-permute-start.2 = (bf16[1040,128]{1,0:T(8,128)(2,1)S(1)}, bf16[1040,128]{1,0:T(8,128)(2,1)S(1)}, u32[]{:S(2)}, u32[]{:S(2)}) collective-permute-start(bf16[1040,128]{1,0:T(8,128)(2,1)S(1)} %get-tuple-element.23), channel_id=1, source_target_pairs={{0,2},{1,3},{2,4},{3,5},{4,6},{5,7},{6,8},{7,9},{8,10},{9,11},{10,... | collective-permute-start | bytes 798728 | tf_op jit(solution)/shard_map/left_over_z/ppermute | solution.py:385
  15.6 14.6 %collective-permute-start.3 = (bf16[1040,128]{1,0:T(8,128)(2,1)S(1)}, bf16[1040,128]{1,0:T(8,128)(2,1)S(1)}, u32[]{:S(2)}, u32[]{:S(2)}) collective-permute-start(bf16[1040,128]{1,0:T(8,128)(2,1)S(1)} %get-tuple-element.24), channel_id=1, source_target_pairs={{0,14},{1,15},{2,0},{3,1},{4,2},{5,3},{6,4},{7,5},{8,6},{9,7},{10,... | collective-permute-start | bytes 798728 | tf_op jit(solution)/shard_map/left_over_z/ppermute | solution.py:385
  19.6 10.6 %collective-permute-start = (bf16[528,128]{1,0:T(8,128)(2,1)S(1)}, bf16[528,128]{1,0:T(8,128)(2,1)S(1)}, u32[]{:S(2)}, u32[]{:S(2)}) collective-permute-start(bf16[528,128]{1,0:T(8,128)(2,1)S(1)} %get-tuple-element.21), channel_id=1, source_target_pairs={{0,4},{1,5},{2,6},{3,7},{4,8},{5,9},{6,10},{7,11},{8,12},{9,13},{1... | collective-permute-start | bytes 405512 | tf_op jit(solution)/shard_map/left_over_z/ppermute | solution.py:385
  19.6 10.6 %collective-permute-start.1 = (bf16[528,128]{1,0:T(8,128)(2,1)S(1)}, bf16[528,128]{1,0:T(8,128)(2,1)S(1)}, u32[]{:S(2)}, u32[]{:S(2)}) collective-permute-start(bf16[528,128]{1,0:T(8,128)(2,1)S(1)} %get-tuple-element.22), channel_id=1, source_target_pairs={{0,12},{1,13},{2,14},{3,15},{4,0},{5,1},{6,2},{7,3},{8,4},{9,5},{1... | collective-permute-start | bytes 405512 | tf_op jit(solution)/shard_map/left_over_z/ppermute | solution.py:385
  31.0 36.3 %copy-start = (bf16[16,128,128]{2,1,0:T(8,128)(2,1)S(1)}, bf16[16,128,128]{2,1,0:T(8,128)(2,1)}, u32[]{:S(2)}) copy-start(bf16[16,128,128]{2,1,0:T(8,128)(2,1)} %vectors.5) | copy-start | bytes 1572868
  31.0 36.3 %copy-start.4 = (s32[256]{0:T(256)S(1)}, s32[256]{0:T(256)}, u32[]{:S(2)}) copy-start(s32[256]{0:T(256)} %right_sector.9) | copy-start | bytes 3076
  31.0 36.3 %copy-start.5 = (s32[256]{0:T(256)S(1)}, s32[256]{0:T(256)}, u32[]{:S(2)}) copy-start(s32[256]{0:T(256)} %right_size.5) | copy-start | bytes 3076
  31.0 36.3 %copy-start.6 = (s32[16]{0:T(128)S(1)}, s32[16]{0:T(128)}, u32[]{:S(2)}) copy-start(s32[16]{0:T(128)} %left_size.5) | copy-start | bytes 196
  31.1 3.6 %collective-permute-start.4 = (bf16[8,272,128]{2,1,0:T(8,128)(2,1)S(1)}, bf16[8,272,128]{2,1,0:T(8,128)(2,1)S(1)}, u32[]{:S(2)}, u32[]{:S(2)}) collective-permute-start(bf16[8,272,128]{2,1,0:T(8,128)(2,1)S(1)} %left_over_core.1), channel_id=1, source_target_pairs={{0,1},{1,0},{2,3},{3,2},{4,5},{5,4},{6,7},{7,6},{8,9},{9,8},{10,11... | collective-permute-start | bytes 1671176 | tf_op jit(solution)/shard_map/left_over_core/ppermute | solution.py:395
  45.2 14.9 %collective-permute-start.7 = (bf16[4,2,128,128]{3,2,1,0:T(8,128)(2,1)}, bf16[4,2,128,128]{3,2,1,0:T(8,128)(2,1)S(1)}, u32[]{:S(2)}, u32[]{:S(2)}) collective-permute-start(bf16[4,2,128,128]{3,2,1,0:T(8,128)(2,1)} %get-tuple-element.35), channel_id=1, source_target_pairs={{0,2},{1,3},{2,4},{3,5},{4,6},{5,7},{6,8},{7,9},{8,10},{9,11},{10,... | collective-permute-start | bytes 786440 | tf_op jit(solution)/shard_map/right_over_z/ppermute | solution.py:411
  46.9 13.2 %collective-permute-start.8 = (bf16[4,2,128,128]{3,2,1,0:T(8,128)(2,1)}, bf16[4,2,128,128]{3,2,1,0:T(8,128)(2,1)S(1)}, u32[]{:S(2)}, u32[]{:S(2)}) collective-permute-start(bf16[4,2,128,128]{3,2,1,0:T(8,128)(2,1)} %get-tuple-element.36), channel_id=1, source_target_pairs={{0,14},{1,15},{2,0},{3,1},{4,2},{5,3},{6,4},{7,5},{8,6},{9,7},{10,... | collective-permute-start | bytes 786440 | tf_op jit(solution)/shard_map/right_over_z/ppermute | solution.py:411
  50.9 9.1 %collective-permute-start.5 = (bf16[2,2,128,128]{3,2,1,0:T(8,128)(2,1)}, bf16[2,2,128,128]{3,2,1,0:T(8,128)(2,1)S(1)}, u32[]{:S(2)}, u32[]{:S(2)}) collective-permute-start(bf16[2,2,128,128]{3,2,1,0:T(8,128)(2,1)} %get-tuple-element.33), channel_id=1, source_target_pairs={{0,4},{1,5},{2,6},{3,7},{4,8},{5,9},{6,10},{7,11},{8,12},{9,13},{1... | collective-permute-start | bytes 393224 | tf_op jit(solution)/shard_map/right_over_z/ppermute | solution.py:411
  50.9 9.1 %collective-permute-start.6 = (bf16[2,2,128,128]{3,2,1,0:T(8,128)(2,1)}, bf16[2,2,128,128]{3,2,1,0:T(8,128)(2,1)S(1)}, u32[]{:S(2)}, u32[]{:S(2)}) collective-permute-start(bf16[2,2,128,128]{3,2,1,0:T(8,128)(2,1)} %get-tuple-element.34), channel_id=1, source_target_pairs={{0,12},{1,13},{2,14},{3,15},{4,0},{5,1},{6,2},{7,3},{8,4},{9,5},{1... | collective-permute-start | bytes 393224 | tf_op jit(solution)/shard_map/right_over_z/ppermute | solution.py:411
  60.1 1.0 copy-start.1
  61.7 5.6 %collective-permute-start.9 = (bf16[8,2,128,128]{3,2,1,0:T(8,128)(2,1)S(1)}, bf16[8,2,128,128]{3,2,1,0:T(8,128)(2,1)S(1)}, u32[]{:S(2)}, u32[]{:S(2)}) collective-permute-start(bf16[8,2,128,128]{3,2,1,0:T(8,128)(2,1)S(1)} %right_over_core.1), channel_id=1, source_target_pairs={{0,1},{1,0},{2,3},{3,2},{4,5},{5,4},{6,7},{7,6},{8,9},{9,8},{10,11... | collective-permute-start | bytes 1572872 | tf_op jit(solution)/shard_map/right_over_core/ppermute | solution.py:421
  67.3 1.0 copy-start.2
  69.9 8.7 %collective-permute-start.10 = (f32[2,128,128]{2,1,0:T(8,128)S(1)}, f32[2,128,128]{2,1,0:T(8,128)S(1)}, u32[]{:S(2)}, u32[]{:S(2)}) collective-permute-start(f32[2,128,128]{2,1,0:T(8,128)S(1)} %first_image.1.image_here), channel_id=1, source_target_pairs={{0,8},{1,9},{2,10},{3,11},{4,12},{5,13},{6,14},{7,15},{8,0},{9,1},... | collective-permute-start | bytes 393224 | tf_op jit(solution)/shard_map/swap_images/ppermute | solution.py:432

commit v6 on v5

--- a/solution.py
+++ b/solution.py
@@ -123,7 +123,7 @@
     *rights, given, sem = refs
     copies = []
     place = 0
-    for right, (_, kinds) in zip(rights, MOVES):
+    for right, (_, kinds) in zip(rights, MOVES[1:]):
         count = len(kinds)
         copies.append(pltpu.make_async_copy(right.at[pl.ds(count, count)], given.at[pl.ds(place, count)], sem))
         place += count
@@ -176,16 +176,16 @@
     _, terms, width, _ = given_right.shape
     size = terms * width
     acc = jnp.zeros((width, width), F32)
-    for index, place, other in parts_of(kind):
+    for index, place, other in reversed(parts_of(kind)):
         for side in range(2):
             if side == 0:
                 left = lefts[index][place * size : (place + 1) * size]
                 scale = lefts[index][lefts[index].shape[0] - PAD :].astype(F32)
-                right = [rights[index][place, w] for w in range(terms)]
+                right = [rights[index + 1 if index else 0][place, w] for w in range(terms)]
             else:
                 left = given_left[other, :size]
                 scale = given_left[other, size:].astype(F32)
-                right = [given_right[other, w] for w in range(terms)]
+                right = [rights[1][place, w] if index == 0 else given_right[other - 2, w] for w in range(terms)]
             half = jnp.dot(left, block, preferred_element_type=F32)
             halves = []
             for w in range(terms):
@@ -219,17 +219,17 @@
 
 def first_kernel(left_size, right_size, right_sector, vectors, *rest):
     *blocks, out, vector, sem = rest
-    half = len(blocks) // 2
+    half = len(MOVES) + 1
     lefts, rights = blocks[: half - 1], blocks[half:-1]
     load_vectors(vectors, vector, sem)
     for kind in range(2):
         _, start = start_vector(kind, left_size, right_size, right_sector, vector)
-        out[kind] = apply(start.astype(BF16), kind, lefts, blocks[half - 1], rights, blocks[-1])
+        out[kind] = apply(start.astype(BF16), kind, lefts, blocks[half - 1], rights, blocks[-1]).astype(BF16)
 
 
 def second_kernel(left_size, right_size, right_sector, vectors, image_here, image_there, *rest):
     *blocks, out, vector, sem = rest
-    half = len(blocks) // 2
+    half = len(MOVES) + 1
     lefts, rights = blocks[: half - 1], blocks[half:-1]
     width = vector.shape[1]
     upper = lax.axis_index("mpo") // 2 >= lax.axis_size("mpo") // 4
@@ -243,7 +243,7 @@
         mask, start = start_vector(kind, left_size, right_size, right_sector, vector)
         norm = total(start * start)
         scale = 1.0 / jnp.sqrt(norm / float(width * width) + 1e-06)
-        image = jnp.where(mask, image_here[kind] + image_there[kind], 0.0) * scale
+        image = jnp.where(mask, image_here[kind].astype(F32) + image_there[kind].astype(F32), 0.0) * scale
         unit = start * scale
         length = total(unit * unit)
         overlap = total(unit * image)
@@ -397,33 +397,34 @@
     with jax.named_scope("order"):
         rights = pl.pallas_call(
             order_kernel,
-            out_shape=[jax.ShapeDtypeStruct((count, terms, width, width), BF16) for count in counts],
+            out_shape=[jax.ShapeDtypeStruct((count, terms, width, width), BF16) for count in [2, 2] + counts[1:]],
             in_specs=[scalars, anywhere],
-            out_specs=[anywhere] * len(MOVES),
+            out_specs=[anywhere] * (len(MOVES) + 1),
             scratch_shapes=[
                 pltpu.VMEM((blocks, terms, width, width), BF16),
                 pltpu.SMEM((blocks,), jnp.int32),
                 pltpu.SemaphoreType.DMA((blocks + 1,)),
             ],
-            compiler_params=pltpu.CompilerParams(vmem_limit_bytes=60 * MIB),
+            compiler_params=pltpu.CompilerParams(vmem_limit_bytes=40 * MIB),
         )(right_sector, arrived.reshape(devices * SLOTS, terms, width, width))
     with jax.named_scope("right_over_z"):
-        rights = [rights[0]] + [lax.ppermute(right, "mpo", route) for right, route in zip(rights[1:], routes[1:])]
+        stayed = [rights[0], lax.ppermute(rights[1], "mpo", cores)]
+        rights = [lax.ppermute(right, "mpo", route) for right, route in zip(rights[2:], routes[1:])]
     with jax.named_scope("right_over_core"):
         given = pl.pallas_call(
             collect_right_kernel,
-            out_shape=jax.ShapeDtypeStruct((blocks // 2, terms, width, width), BF16),
-            in_specs=[anywhere] * len(MOVES),
+            out_shape=jax.ShapeDtypeStruct((blocks // 2 - 2, terms, width, width), BF16),
+            in_specs=[anywhere] * (len(MOVES) - 1),
             out_specs=anywhere,
             scratch_shapes=[pltpu.SemaphoreType.DMA],
             compiler_params=pltpu.CompilerParams(vmem_limit_bytes=4 * MIB),
         )(*rights)
-        rights.append(lax.ppermute(given, "mpo", cores))
+        rights = stayed + rights + [lax.ppermute(given, "mpo", cores)]
     with jax.named_scope("first_image"):
         image_here = pl.pallas_call(
             first_kernel,
-            out_shape=jax.ShapeDtypeStruct((2, width, width), F32),
-            in_specs=[scalars, scalars, scalars, anywhere] + [vmem] * (2 * len(MOVES) + 2),
+            out_shape=jax.ShapeDtypeStruct((2, width, width), BF16),
+            in_specs=[scalars, scalars, scalars, anywhere] + [vmem] * (2 * len(MOVES) + 3),
             out_specs=vmem,
             scratch_shapes=[pltpu.VMEM((2, width, width), BF16), pltpu.SemaphoreType.DMA],
             compiler_params=pltpu.CompilerParams(vmem_limit_bytes=16 * MIB),
@@ -434,7 +435,7 @@
         pieces = pl.pallas_call(
             second_kernel,
             out_shape=jax.ShapeDtypeStruct((layers, 3 * rows + 8, width), F32),
-            in_specs=[scalars, scalars, scalars, anywhere] + [vmem] * (2 * len(MOVES) + 4),
+            in_specs=[scalars, scalars, scalars, anywhere] + [vmem] * (2 * len(MOVES) + 5),
             out_specs=vmem,
             scratch_shapes=[pltpu.VMEM((2, width, width), BF16), pltpu.SemaphoreType.DMA],
             compiler_params=pltpu.CompilerParams(vmem_limit_bytes=16 * MIB),

time: 114 us -> 110 us (0.965)
  waiting for transfers between devices: 28.1 us -> 24.1 us
  blocking collectives: 31.5 us -> 30.3 us
    all_to_all x1, waiting for transfers between devices: 7.59 us -> 5.54 us  [shards(): arrived = lax.all_to_all(right_out, 'sec', 0, 0, tiled=True)]
    ppermute x1, waiting for transfers between devices: 4.78 us -> 3.21 us  [shards(): lax.ppermute(image_here, 'mpo', [(p, (p + chips) % layers) for p in range...]
    all_to_all x1, blocking collectives: 20.7 us -> 19.4 us  [shards(): pieces = lax.all_to_all(pieces, 'mpo', 0, 0, tiled=True)]
    unnamed x16 -> x20, local copies, waits for them, and re-layouts: 1.92 us -> 2.8 us
    ppermute x1 -> x2, starting transfers between devices: 4.1 us -> 4.2 us  [the longest x1 4.1 us: shards(): rights = stayed + rights + [lax.ppermute(given, 'mpo', cores)]]
  transfers between devices with their start and end apart: 12 -> 13, of which waited for: 6 -> 6; matrix products, arithmetic and copies ran while one was open for 0% -> 0% of each run, Pallas kernels for 3% -> 3%
where the time goes in v6:
time: 110 us
  starting transfers between devices  36.4 us (33%)
  blocking collectives  30.3 us (28%)
  waiting for transfers between devices  24.1 us (22%)
  Pallas kernels  15.2 us (14%)
  local copies, waits for them, and re-layouts  2.81 us (3%)
    all_to_all x1, blocking collectives, shards(): pieces = lax.all_to_all(pieces, 'mpo', 0, 0, tiled=True)  19.4 us
    all_to_all x1, blocking collectives, shards(): lax.all_to_all(jnp.broadcast_to(line[None], (devices, 8, width)), 'sec',...  10.9 us
    ppermute x4, starting transfers between devices, shards(): lax.ppermute(right, 'mpo', route)  9.32 us
    ppermute x4, starting transfers between devices, shards(): lax.ppermute(left, 'mpo', route)  9.32 us
    all_to_all x1, starting transfers between devices, shards(): arrived = lax.all_to_all(right_out, 'sec', 0, 0, tiled=True)  7.6 us
    ppermute x4, waiting for transfers between devices, shards(): lax.ppermute(left, 'mpo', route)  6.94 us
    all_to_all x1, waiting for transfers between devices, shards(): arrived = lax.all_to_all(right_out, 'sec', 0, 0, tiled=True)  5.54 us
    ppermute x4, waiting for transfers between devices, shards(): lax.ppermute(right, 'mpo', route)  5.37 us
  transfers between devices with their start and end apart: 13, of which 6 were waited for; matrix products, arithmetic and copies ran while one was open for 0% of the time, Pallas kernels for 3%

profile of v6, /device:TPU:1, one launch (start us, length us, event | category | flops | bytes accessed | tf_op | source)
XLA Modules:
  0.0 109.6 jit_solution(15534350308739287220)
XLA Ops:
  0.6 3.3 %pack_right.1 = bf16[16,2,2,128,128]{4,3,2,1,0:T(8,128)(2,1)} custom-call(s32[256]{0:T(256)} %right_sector.9, bf16[2,16,128,128]{3,2,1,0:T(8,128)(2,1)} %right_env.1), custom_call_target="tpu_custom_call" | custom-call | tf_op jit(solution)/shard_map/pack_right/pallas_call | solution.py:361
  3.9 0.0 copy-start.9
  3.9 7.6 %all-to-all-start = ((bf16[16,2,2,128,128]{4,3,2,1,0:T(8,128)(2,1)}), bf16[16,2,2,128,128]{4,3,2,1,0:T(8,128)(2,1)S(1)}, u32[]{:S(2)}, u32[]{:S(2)}) async-start(bf16[16,2,2,128,128]{4,3,2,1,0:T(8,128)(2,1)} %pack_right.1), calls=%async_computation | async-start | bytes 4194304 | tf_op jit(solution)/shard_map/right_over_sec/all_to_all | solution.py:370
  11.5 0.0 copy-done.9
  11.5 0.0 copy-start.5
  11.5 1.2 %copy-done.5 = bf16[2,16,128,128]{3,2,1,0:T(8,128)(2,1)S(1)} copy-done((bf16[2,16,128,128]{3,2,1,0:T(8,128)(2,1)S(1)}, bf16[2,16,128,128]{3,2,1,0:T(8,128)(2,1)}, u32[]{:S(2)}) %copy-start.5) | copy-done | bytes 1048600
  12.7 2.2 %pack_left.1 = (bf16[1040,128]{1,0:T(8,128)(2,1)S(1)}, bf16[528,128]{1,0:T(8,128)(2,1)S(1)}, bf16[528,128]{1,0:T(8,128)(2,1)S(1)}, bf16[1040,128]{1,0:T(8,128)(2,1)S(1)}, bf16[1040,128]{1,0:T(8,128)(2,1)S(1)}) custom-call(f32[2]{0:T(128)S(1)} %copy-done.9, bf16[2,16,128,128]{3,2,1,0:T(8,128)(2,1)S(1)} %copy-done.5), custom_call_target="tpu_custom_call" | custom-call | tf_op jit(solution)/shard_map/pack_left/pallas_call | solution.py:372
  14.9 1.7 %collective-permute-start.2 = (bf16[1040,128]{1,0:T(8,128)(2,1)S(1)}, bf16[1040,128]{1,0:T(8,128)(2,1)S(1)}, u32[]{:S(2)}, u32[]{:S(2)}) collective-permute-start(bf16[1040,128]{1,0:T(8,128)(2,1)S(1)} %get-tuple-element.24), channel_id=1, source_target_pairs={{0,2},{1,3},{2,4},{3,5},{4,6},{5,7},{6,8},{7,9},{8,10},{9,11},{10,... | collective-permute-start | bytes 798728 | tf_op jit(solution)/shard_map/left_over_z/ppermute | solution.py:385
  16.7 4.0 %collective-permute-start.3 = (bf16[1040,128]{1,0:T(8,128)(2,1)S(1)}, bf16[1040,128]{1,0:T(8,128)(2,1)S(1)}, u32[]{:S(2)}, u32[]{:S(2)}) collective-permute-start(bf16[1040,128]{1,0:T(8,128)(2,1)S(1)} %get-tuple-element.25), channel_id=1, source_target_pairs={{0,14},{1,15},{2,0},{3,1},{4,2},{5,3},{6,4},{7,5},{8,6},{9,7},{10,... | collective-permute-start | bytes 798728 | tf_op jit(solution)/shard_map/left_over_z/ppermute | solution.py:385
  20.7 0.0 collective-permute-start
  20.7 3.6 %collective-permute-start.1 = (bf16[528,128]{1,0:T(8,128)(2,1)S(1)}, bf16[528,128]{1,0:T(8,128)(2,1)S(1)}, u32[]{:S(2)}, u32[]{:S(2)}) collective-permute-start(bf16[528,128]{1,0:T(8,128)(2,1)S(1)} %get-tuple-element.23), channel_id=1, source_target_pairs={{0,12},{1,13},{2,14},{3,15},{4,0},{5,1},{6,2},{7,3},{8,4},{9,5},{1... | collective-permute-start | bytes 405512 | tf_op jit(solution)/shard_map/left_over_z/ppermute | solution.py:385
  24.3 6.9 %collective-permute-done.refs_1_.rest_1_ = bf16[528,128]{1,0:T(8,128)(2,1)S(1)} collective-permute-done((bf16[528,128]{1,0:T(8,128)(2,1)S(1)}, bf16[528,128]{1,0:T(8,128)(2,1)S(1)}, u32[]{:S(2)}, u32[]{:S(2)}) %collective-permute-start) | collective-permute-done | bytes 135200 | tf_op jit(solution)/shard_map/left_over_z/ppermute | solution.py:385
  31.2 0.0 collective-permute-done.1.refs_2_.rest_2_
  31.2 0.0 collective-permute-done.2.refs_3_.rest_3_
  31.2 0.0 collective-permute-done.3.refs_4_.rest_4_
  31.2 0.0 copy-start
  31.2 0.7 left_over_core.1
  32.0 2.1 %collective-permute-start.4 = (bf16[8,272,128]{2,1,0:T(8,128)(2,1)S(1)}, bf16[8,272,128]{2,1,0:T(8,128)(2,1)S(1)}, u32[]{:S(2)}, u32[]{:S(2)}) collective-permute-start(bf16[8,272,128]{2,1,0:T(8,128)(2,1)S(1)} %left_over_core.1), channel_id=1, source_target_pairs={{0,1},{1,0},{2,3},{3,2},{4,5},{5,4},{6,7},{7,6},{8,9},{9,8},{10,11... | collective-permute-start | bytes 1671176 | tf_op jit(solution)/shard_map/left_over_core/ppermute | solution.py:395
  34.1 0.0 copy-done.3
  34.1 1.6 %collective-permute-done.4.rest_5_ = bf16[8,272,128]{2,1,0:T(8,128)(2,1)S(1)} collective-permute-done((bf16[8,272,128]{2,1,0:T(8,128)(2,1)S(1)}, bf16[8,272,128]{2,1,0:T(8,128)(2,1)S(1)}, u32[]{:S(2)}, u32[]{:S(2)}) %collective-permute-start.4) | collective-permute-done | bytes 557088 | tf_op jit(solution)/shard_map/left_over_core/ppermute | solution.py:395
  35.7 0.8 copy-done.1
  36.5 5.5 %all-to-all-done = bf16[16,2,2,128,128]{4,3,2,1,0:T(8,128)(2,1)S(1)} async-done(((bf16[16,2,2,128,128]{4,3,2,1,0:T(8,128)(2,1)}), bf16[16,2,2,128,128]{4,3,2,1,0:T(8,128)(2,1)S(1)}, u32[]{:S(2)}, u32[]{:S(2)}) %all-to-all-start) | async-done | bytes 2097184 | tf_op jit(solution)/shard_map/right_over_sec/all_to_all | solution.py:370
  42.0 0.7 copy-done.6
  42.8 3.1 %order.1 = (bf16[2,2,128,128]{3,2,1,0:T(8,128)(2,1)S(1)}, bf16[2,2,128,128]{3,2,1,0:T(8,128)(2,1)S(1)}, bf16[2,2,128,128]{3,2,1,0:T(8,128)(2,1)S(1)}, bf16[2,2,1...) custom-call(s32[256]{0:T(256)S(1)} %copy-done.6, ...), custom_call_target="tpu_custom_call" | custom-call | tf_op jit(solution)/shard_map/order/pallas_call | solution.py:398
  45.8 1.7 %collective-permute-start.8 = (bf16[4,2,128,128]{3,2,1,0:T(8,128)(2,1)S(1)}, bf16[4,2,128,128]{3,2,1,0:T(8,128)(2,1)S(1)}, u32[]{:S(2)}, u32[]{:S(2)}) collective-permute-start(bf16[4,2,128,128]{3,2,1,0:T(8,128)(2,1)S(1)} %get-tuple-element.37), channel_id=1, source_target_pairs={{0,2},{1,3},{2,4},{3,5},{4,6},{5,7},{6,8},{7,9},{8,10},{9,11},{10,... | collective-permute-start | bytes 786440 | tf_op jit(solution)/shard_map/right_over_z/ppermute | solution.py:412
  47.5 4.0 %collective-permute-start.9 = (bf16[4,2,128,128]{3,2,1,0:T(8,128)(2,1)S(1)}, bf16[4,2,128,128]{3,2,1,0:T(8,128)(2,1)S(1)}, u32[]{:S(2)}, u32[]{:S(2)}) collective-permute-start(bf16[4,2,128,128]{3,2,1,0:T(8,128)(2,1)S(1)} %get-tuple-element.38), channel_id=1, source_target_pairs={{0,14},{1,15},{2,0},{3,1},{4,2},{5,3},{6,4},{7,5},{8,6},{9,7},{10,... | collective-permute-start | bytes 786440 | tf_op jit(solution)/shard_map/right_over_z/ppermute | solution.py:412
  51.6 0.0 collective-permute-start.6
  51.6 3.6 %collective-permute-start.7 = (bf16[2,2,128,128]{3,2,1,0:T(8,128)(2,1)S(1)}, bf16[2,2,128,128]{3,2,1,0:T(8,128)(2,1)S(1)}, u32[]{:S(2)}, u32[]{:S(2)}) collective-permute-start(bf16[2,2,128,128]{3,2,1,0:T(8,128)(2,1)S(1)} %get-tuple-element.36), channel_id=1, source_target_pairs={{0,12},{1,13},{2,14},{3,15},{4,0},{5,1},{6,2},{7,3},{8,4},{9,5},{1... | collective-permute-start | bytes 393224 | tf_op jit(solution)/shard_map/right_over_z/ppermute | solution.py:412
  55.1 5.4 %collective-permute-done.6.refs_0_.rest_8_ = bf16[2,2,128,128]{3,2,1,0:T(8,128)(2,1)S(1)} collective-permute-done((bf16[2,2,128,128]{3,2,1,0:T(8,128)(2,1)S(1)}, bf16[2,2,128,128]{3,2,1,0:T(8,128)(2,1)S(1)}, u32[]{:S(2)}, u32[]{:S(2)}) %collective-permute-start.6) | collective-permute-done | bytes 131104 | tf_op jit(solution)/shard_map/right_over_z/ppermute | solution.py:412
  60.5 0.0 collective-permute-done.7.refs_1_.rest_9_
  60.5 0.0 collective-permute-done.8.refs_2_.rest_10_
  60.5 0.0 collective-permute-done.9.refs_3_.rest_11_
  60.5 0.5 right_over_core.1
  61.0 4.1 %collective-permute-start.10 = (bf16[6,2,128,128]{3,2,1,0:T(8,128)(2,1)S(1)}, bf16[6,2,128,128]{3,2,1,0:T(8,128)(2,1)S(1)}, u32[]{:S(2)}, u32[]{:S(2)}) collective-permute-start(bf16[6,2,128,128]{3,2,1,0:T(8,128)(2,1)S(1)} %right_over_core.1), channel_id=1, source_target_pairs={{0,1},{1,0},{2,3},{3,2},{4,5},{5,4},{6,7},{7,6},{8,9},{9,8},{10,11... | collective-permute-start | bytes 1179656 | tf_op jit(solution)/shard_map/right_over_core/ppermute | solution.py:422
  65.1 0.1 collective-permute-start.5
  65.2 1.4 %collective-permute-done.5.rest_7_ = bf16[2,2,128,128]{3,2,1,0:T(8,128)(2,1)S(1)} collective-permute-done((bf16[2,2,128,128]{3,2,1,0:T(8,128)(2,1)S(1)}, bf16[2,2,128,128]{3,2,1,0:T(8,128)(2,1)S(1)}, u32[]{:S(2)}, u32[]{:S(2)}) %collective-permute-start.5) | collective-permute-done | bytes 131104 | tf_op jit(solution)/shard_map/right_over_z/ppermute | solution.py:411
  66.7 0.0 collective-permute-done.10.rest_12_
  66.7 0.0 copy-done
  66.7 0.0 copy-done.2
  66.7 0.0 copy-done.4
  66.7 0.0 copy-done.7
  66.7 1.7 %first_image.1.image_here = bf16[2,128,128]{2,1,0:T(8,128)(2,1)S(1)} custom-call(s32[16]{0:T(128)S(1)} %copy-done.8, s32[256]{0:T(256)S(1)} %copy-done.7, s32[256]{0:T(256)S(1)} %copy-done.6, bf16[16,128,128]{2,1,0:T(8,128)(2,1)S(1)} %copy-done, bf16[1040,128]{1,0:T(8,128)(2,1)S(1)} %get-tuple-element.26.refs_0_.rest_0_, ...), custom_call_target="tpu_custom_call" | custom-call | tf_op jit(solution)/shard_map/first_image/pallas_call | solution.py:424
  68.4 3.9 %collective-permute-start.11 = (bf16[2,128,128]{2,1,0:T(8,128)(2,1)S(1)}, bf16[2,128,128]{2,1,0:T(8,128)(2,1)S(1)}, u32[]{:S(2)}, u32[]{:S(2)}) collective-permute-start(bf16[2,128,128]{2,1,0:T(8,128)(2,1)S(1)} %first_image.1.image_here), channel_id=1, source_target_pairs={{0,8},{1,9},{2,10},{3,11},{4,12},{5,13},{6,14},{7,15},{8,0},{9,1},... | collective-permute-start | bytes 196616 | tf_op jit(solution)/shard_map/swap_images/ppermute | solution.py:433
  72.3 3.2 %collective-permute-done.11.image_there = bf16[2,128,128]{2,1,0:T(8,128)(2,1)S(1)} collective-permute-done((bf16[2,128,128]{2,1,0:T(8,128)(2,1)S(1)}, bf16[2,128,128]{2,1,0:T(8,128)(2,1)S(1)}, u32[]{:S(2)}, u32[]{:S(2)}) %collective-permute-start.11) | collective-permute-done | bytes 65568 | tf_op jit(solution)/shard_map/swap_images/ppermute | solution.py:433
  75.5 2.0 %second_image.1 = f32[16,32,128]{2,1,0:T(8,128)S(1)} custom-call(s32[16]{0:T(128)S(1)} %copy-done.8, s32[256]{0:T(256)S(1)} %copy-done.7, s32[256]{0:T(256)S(1)} %copy-done.6, bf16[16,128,128]{2,1,0:T(8,128)(2,1)S(1)} %copy-done, bf16[2,128,128]{2,1,0:T(8,128)(2,1)S(1)} %first_image.1.image_here, ...), custom_call_target="tpu_custom_call" | custom-call | tf_op jit(solution)/shard_map/second_image/pallas_call | solution.py:435
  77.5 19.4 %all_to_all.15.pieces = f32[16,32,128]{2,1,0:T(8,128)S(1)} all-to-all(f32[16,32,128]{2,1,0:T(8,128)S(1)} %second_image.1), channel_id=1, replica_groups=mesh['sec'=16,'mpo'=16] {'mpo'}, dimensions={0} | all-to-all | bytes 524288 | tf_op jit(solution)/shard_map/rows_over_mpo/all_to_all | solution.py:444
  96.9 10.9 %all_to_all.16.shared = f32[16,8,128]{2,1,0:T(8,128)S(1)} all-to-all(f32[16,8,128]{2,1,0:T(8,128)S(1)} %broadcast_in_dim.2), channel_id=1, replica_groups=mesh['sec'=16,'mpo'=16] {'sec'}, dimensions={0} | all-to-all | bytes 131072 | tf_op jit(solution)/shard_map/numbers_over_sec/all_to_all | solution.py:447
  107.8 1.8 %finish.1 = (f32[16,8,128]{2,1,0:T(8,128)}, f32[16,8,128]{2,1,0:T(8,128)}, f32[3]{0:T(128)}) custom-call(s32[16]{0:T(128)S(1)} %copy-done.8, s32[256]{0:T(256)S(1)} %copy-done.7, s32[256]{0:T(256)S(1)} %copy-done.6, bf16[16,128,128]{2,1,0:T(8,128)(2,1)S(1)} %copy-done, f32[16,32,128]{2,1,0:T(8,128)S(1)} %all_to_all.15.pieces, ...), custom_call_target="tpu_custom_call" | custom-call | tf_op jit(solution)/shard_map/finish/pallas_call | solution.py:449
  (10 shorter events, 0.0 us)
Async XLA Ops:
  3.9 7.6 %copy-start.9 = (f32[2]{0:T(128)S(1)}, f32[2]{0:T(128)}, u32[]{:S(2)}) copy-start(f32[2]{0:T(128)} %weights.1) | copy-start | bytes 28
  3.9 38.1 %all-to-all-start = ((bf16[16,2,2,128,128]{4,3,2,1,0:T(8,128)(2,1)}), bf16[16,2,2,128,128]{4,3,2,1,0:T(8,128)(2,1)S(1)}, u32[]{:S(2)}, u32[]{:S(2)}) async-start(bf16[16,2,2,128,128]{4,3,2,1,0:T(8,128)(2,1)} %pack_right.1), calls=%async_computation | async-start | bytes 4194304 | tf_op jit(solution)/shard_map/right_over_sec/all_to_all | solution.py:370
  11.5 1.2 %copy-start.5 = (bf16[2,16,128,128]{3,2,1,0:T(8,128)(2,1)S(1)}, bf16[2,16,128,128]{3,2,1,0:T(8,128)(2,1)}, u32[]{:S(2)}) copy-start(bf16[2,16,128,128]{3,2,1,0:T(8,128)(2,1)} %left_env.1) | copy-start | bytes 3145732
  14.9 16.3 %collective-permute-start.2 = (bf16[1040,128]{1,0:T(8,128)(2,1)S(1)}, bf16[1040,128]{1,0:T(8,128)(2,1)S(1)}, u32[]{:S(2)}, u32[]{:S(2)}) collective-permute-start(bf16[1040,128]{1,0:T(8,128)(2,1)S(1)} %get-tuple-element.24), channel_id=1, source_target_pairs={{0,2},{1,3},{2,4},{3,5},{4,6},{5,7},{6,8},{7,9},{8,10},{9,11},{10,... | collective-permute-start | bytes 798728 | tf_op jit(solution)/shard_map/left_over_z/ppermute | solution.py:385
  16.7 14.5 %collective-permute-start.3 = (bf16[1040,128]{1,0:T(8,128)(2,1)S(1)}, bf16[1040,128]{1,0:T(8,128)(2,1)S(1)}, u32[]{:S(2)}, u32[]{:S(2)}) collective-permute-start(bf16[1040,128]{1,0:T(8,128)(2,1)S(1)} %get-tuple-element.25), channel_id=1, source_target_pairs={{0,14},{1,15},{2,0},{3,1},{4,2},{5,3},{6,4},{7,5},{8,6},{9,7},{10,... | collective-permute-start | bytes 798728 | tf_op jit(solution)/shard_map/left_over_z/ppermute | solution.py:385
  20.7 10.5 %collective-permute-start = (bf16[528,128]{1,0:T(8,128)(2,1)S(1)}, bf16[528,128]{1,0:T(8,128)(2,1)S(1)}, u32[]{:S(2)}, u32[]{:S(2)}) collective-permute-start(bf16[528,128]{1,0:T(8,128)(2,1)S(1)} %get-tuple-element.22), channel_id=1, source_target_pairs={{0,4},{1,5},{2,6},{3,7},{4,8},{5,9},{6,10},{7,11},{8,12},{9,13},{1... | collective-permute-start | bytes 405512 | tf_op jit(solution)/shard_map/left_over_z/ppermute | solution.py:385
  20.7 10.5 %collective-permute-start.1 = (bf16[528,128]{1,0:T(8,128)(2,1)S(1)}, bf16[528,128]{1,0:T(8,128)(2,1)S(1)}, u32[]{:S(2)}, u32[]{:S(2)}) collective-permute-start(bf16[528,128]{1,0:T(8,128)(2,1)S(1)} %get-tuple-element.23), channel_id=1, source_target_pairs={{0,12},{1,13},{2,14},{3,15},{4,0},{5,1},{6,2},{7,3},{8,4},{9,5},{1... | collective-permute-start | bytes 405512 | tf_op jit(solution)/shard_map/left_over_z/ppermute | solution.py:385
  31.2 2.9 %copy-start.3 = (bf16[528,128]{1,0:T(8,128)(2,1)}, bf16[528,128]{1,0:T(8,128)(2,1)S(1)}, u32[]{:S(2)}) copy-start(bf16[528,128]{1,0:T(8,128)(2,1)S(1)} %collective-permute-done.1.refs_2_.rest_2_) | copy-start | bytes 405508
  31.2 35.5 %copy-start = (bf16[16,128,128]{2,1,0:T(8,128)(2,1)S(1)}, bf16[16,128,128]{2,1,0:T(8,128)(2,1)}, u32[]{:S(2)}) copy-start(bf16[16,128,128]{2,1,0:T(8,128)(2,1)} %vectors.5) | copy-start | bytes 1572868
  32.0 3.7 %collective-permute-start.4 = (bf16[8,272,128]{2,1,0:T(8,128)(2,1)S(1)}, bf16[8,272,128]{2,1,0:T(8,128)(2,1)S(1)}, u32[]{:S(2)}, u32[]{:S(2)}) collective-permute-start(bf16[8,272,128]{2,1,0:T(8,128)(2,1)S(1)} %left_over_core.1), channel_id=1, source_target_pairs={{0,1},{1,0},{2,3},{3,2},{4,5},{5,4},{6,7},{7,6},{8,9},{9,8},{10,11... | collective-permute-start | bytes 1671176 | tf_op jit(solution)/shard_map/left_over_core/ppermute | solution.py:395
  35.7 0.8 copy-start.1
  42.0 24.7 %copy-start.2 = (bf16[8,272,128]{2,1,0:T(8,128)(2,1)S(1)}, bf16[8,272,128]{2,1,0:T(8,128)(2,1)}, u32[]{:S(2)}) copy-start(bf16[8,272,128]{2,1,0:T(8,128)(2,1)} %copy-done.1) | copy-start | bytes 1671172
  42.0 24.7 %copy-start.4 = (bf16[528,128]{1,0:T(8,128)(2,1)S(1)}, bf16[528,128]{1,0:T(8,128)(2,1)}, u32[]{:S(2)}) copy-start(bf16[528,128]{1,0:T(8,128)(2,1)} %copy-done.3) | copy-start | bytes 405508
  42.0 0.7 copy-start.6
  42.7 23.9 %copy-start.7 = (s32[256]{0:T(256)S(1)}, s32[256]{0:T(256)}, u32[]{:S(2)}) copy-start(s32[256]{0:T(256)} %right_size.5) | copy-start | bytes 3076
  42.8 24.0 %copy-start.8 = (s32[16]{0:T(128)S(1)}, s32[16]{0:T(128)}, u32[]{:S(2)}) copy-start(s32[16]{0:T(128)} %left_size.5) | copy-start | bytes 196
  45.8 14.7 %collective-permute-start.8 = (bf16[4,2,128,128]{3,2,1,0:T(8,128)(2,1)S(1)}, bf16[4,2,128,128]{3,2,1,0:T(8,128)(2,1)S(1)}, u32[]{:S(2)}, u32[]{:S(2)}) collective-permute-start(bf16[4,2,128,128]{3,2,1,0:T(8,128)(2,1)S(1)} %get-tuple-element.37), channel_id=1, source_target_pairs={{0,2},{1,3},{2,4},{3,5},{4,6},{5,7},{6,8},{7,9},{8,10},{9,11},{10,... | collective-permute-start | bytes 786440 | tf_op jit(solution)/shard_map/right_over_z/ppermute | solution.py:412
  47.5 13.0 %collective-permute-start.9 = (bf16[4,2,128,128]{3,2,1,0:T(8,128)(2,1)S(1)}, bf16[4,2,128,128]{3,2,1,0:T(8,128)(2,1)S(1)}, u32[]{:S(2)}, u32[]{:S(2)}) collective-permute-start(bf16[4,2,128,128]{3,2,1,0:T(8,128)(2,1)S(1)} %get-tuple-element.38), channel_id=1, source_target_pairs={{0,14},{1,15},{2,0},{3,1},{4,2},{5,3},{6,4},{7,5},{8,6},{9,7},{10,... | collective-permute-start | bytes 786440 | tf_op jit(solution)/shard_map/right_over_z/ppermute | solution.py:412
  51.6 8.9 %collective-permute-start.6 = (bf16[2,2,128,128]{3,2,1,0:T(8,128)(2,1)S(1)}, bf16[2,2,128,128]{3,2,1,0:T(8,128)(2,1)S(1)}, u32[]{:S(2)}, u32[]{:S(2)}) collective-permute-start(bf16[2,2,128,128]{3,2,1,0:T(8,128)(2,1)S(1)} %get-tuple-element.35), channel_id=1, source_target_pairs={{0,4},{1,5},{2,6},{3,7},{4,8},{5,9},{6,10},{7,11},{8,12},{9,13},{1... | collective-permute-start | bytes 393224 | tf_op jit(solution)/shard_map/right_over_z/ppermute | solution.py:412
  51.6 8.9 %collective-permute-start.7 = (bf16[2,2,128,128]{3,2,1,0:T(8,128)(2,1)S(1)}, bf16[2,2,128,128]{3,2,1,0:T(8,128)(2,1)S(1)}, u32[]{:S(2)}, u32[]{:S(2)}) collective-permute-start(bf16[2,2,128,128]{3,2,1,0:T(8,128)(2,1)S(1)} %get-tuple-element.36), channel_id=1, source_target_pairs={{0,12},{1,13},{2,14},{3,15},{4,0},{5,1},{6,2},{7,3},{8,4},{9,5},{1... | collective-permute-start | bytes 393224 | tf_op jit(solution)/shard_map/right_over_z/ppermute | solution.py:412
  61.0 5.6 %collective-permute-start.10 = (bf16[6,2,128,128]{3,2,1,0:T(8,128)(2,1)S(1)}, bf16[6,2,128,128]{3,2,1,0:T(8,128)(2,1)S(1)}, u32[]{:S(2)}, u32[]{:S(2)}) collective-permute-start(bf16[6,2,128,128]{3,2,1,0:T(8,128)(2,1)S(1)} %right_over_core.1), channel_id=1, source_target_pairs={{0,1},{1,0},{2,3},{3,2},{4,5},{5,4},{6,7},{7,6},{8,9},{9,8},{10,11... | collective-permute-start | bytes 1179656 | tf_op jit(solution)/shard_map/right_over_core/ppermute | solution.py:422
  65.1 1.5 %collective-permute-start.5 = (bf16[2,2,128,128]{3,2,1,0:T(8,128)(2,1)S(1)}, bf16[2,2,128,128]{3,2,1,0:T(8,128)(2,1)S(1)}, u32[]{:S(2)}, u32[]{:S(2)}) collective-permute-start(bf16[2,2,128,128]{3,2,1,0:T(8,128)(2,1)S(1)} %get-tuple-element.34), channel_id=1, source_target_pairs={{0,1},{1,0},{2,3},{3,2},{4,5},{5,4},{6,7},{7,6},{8,9},{9,8},{10,11... | collective-permute-start | bytes 393224 | tf_op jit(solution)/shard_map/right_over_z/ppermute | solution.py:411
  68.4 7.1 %collective-permute-start.11 = (bf16[2,128,128]{2,1,0:T(8,128)(2,1)S(1)}, bf16[2,128,128]{2,1,0:T(8,128)(2,1)S(1)}, u32[]{:S(2)}, u32[]{:S(2)}) collective-permute-start(bf16[2,128,128]{2,1,0:T(8,128)(2,1)S(1)} %first_image.1.image_here), channel_id=1, source_target_pairs={{0,8},{1,9},{2,10},{3,11},{4,12},{5,13},{6,14},{7,15},{8,0},{9,1},... | collective-permute-start | bytes 196616 | tf_op jit(solution)/shard_map/swap_images/ppermute | solution.py:433

commit v7 on v6

--- a/solution.py
+++ b/solution.py
@@ -77,9 +77,10 @@
         copy.wait()
 
 
-def pack_left_kernel(weights, left_env, *rest):
-    *lefts, stage, wbuf, sem = rest
-    terms, _, width, _ = left_env.shape
+def pack_left_kernel(weights, right_sector, left_env, *rest):
+    *lefts, places, stage, wbuf, sem = rest
+    terms, blocks, width, _ = left_env.shape
+    sec = lax.axis_index("sec")
     own = lax.axis_index("mpo")
     load = pltpu.make_async_copy(left_env, stage, sem.at[0])
     load.start()
@@ -101,20 +102,31 @@
                 rows = pl.ds((place * terms + w) * width, width)
                 copies.append(pltpu.make_async_copy(stage.at[w, q], left.at[rows], sem.at[1]))
         copies.append(pltpu.make_async_copy(wbuf, left.at[pl.ds(len(sectors) * terms * width, PAD)], sem.at[1]))
-    start_all(copies)
+    for copy in copies:
+        copy.start()
+    shift = blocks.bit_length() - 1
+    sources = [lax.shift_right_logical(right_sector[sec * blocks + q], shift) for q in range(blocks)]
+    for q in range(blocks):
+        again = jnp.bool_(False)
+        for other in range(q):
+            again = again | (sources[other] == sources[q])
+        places[q] = sources[q] * SLOTS + jnp.where(again, 1, 0)
+    for copy in copies:
+        copy.wait()
 
 
 def collect_left_kernel(*refs):
-    *lefts, given, sem = refs
+    *lefts, kept, given, sem = refs
     size = given.shape[1] - PAD
     copies = []
     place = 0
     for left, (_, kinds) in zip(lefts, MOVES):
-        for j in range(len(kinds)):
-            rows = pl.ds((len(kinds) + j) * size, size)
-            copies.append(pltpu.make_async_copy(left.at[rows], given.at[place, pl.ds(0, size)], sem))
-            pad = pl.ds(2 * len(kinds) * size, PAD)
-            copies.append(pltpu.make_async_copy(left.at[pad], given.at[place, pl.ds(size, PAD)], sem))
+        count = len(kinds)
+        for j in range(count):
+            for target, first in ((kept, j), (given, count + j)):
+                for start, rows in ((first * size, pl.ds(0, size)), (2 * count * size, pl.ds(size, PAD))):
+                    source = left.at[pl.ds(start, rows.size)]
+                    copies.append(pltpu.make_async_copy(source, target.at[place, rows], sem))
             place += 1
     start_all(copies)
 
@@ -130,36 +142,16 @@
     start_all(copies)
 
 
-def order_kernel(right_sector, arrived, *rest):
-    *rights, stage, places, sem = rest
-    blocks = stage.shape[0]
-    sec = lax.axis_index("sec")
-    own = lax.axis_index("mpo")
-    shift = blocks.bit_length() - 1
-    sources = [lax.shift_right_logical(right_sector[sec * blocks + q], shift) for q in range(blocks)]
-    for q in range(blocks):
-        again = jnp.bool_(False)
-        for other in range(q):
-            again = again | (sources[other] == sources[q])
-        places[q] = sources[q] * SLOTS + jnp.where(again, 1, 0)
-    loads = []
-    for sectors in targets(own, lax.axis_size("mpo") // 2):
-        for q in sectors:
-            index = len(loads)
-            load = pltpu.make_async_copy(arrived.at[places[q]], stage.at[index], sem.at[index])
-            load.start()
-            loads.append(load)
-    stores = []
-    first = 0
+def order_kernel(places, arrived, *rest):
+    *rights, sem = rest
+    sectors = [q for group in targets(lax.axis_index("mpo"), lax.axis_size("mpo") // 2) for q in group]
+    copies = []
     for right in rights:
-        count = right.shape[0]
-        for index in range(first, first + count):
-            loads[index].wait()
-        stores.append(pltpu.make_async_copy(stage.at[pl.ds(first, count)], right, sem.at[blocks]))
-        stores[-1].start()
-        first += count
-    for store in stores:
-        store.wait()
+        for place in range(right.shape[0]):
+            copies.append(pltpu.make_async_copy(arrived.at[places[sectors[len(copies)]]], right.at[place], sem))
+            copies[-1].start()
+    for copy in copies:
+        copy.wait()
 
 
 def live(rows, left, right):
@@ -172,20 +164,20 @@
     return jnp.sum(jnp.sum(x, axis=0, keepdims=True), axis=1, keepdims=True)
 
 
-def apply(block, kind, lefts, given_left, rights, given_right):
-    _, terms, width, _ = given_right.shape
+def apply(block, kind, lefts, rights):
+    _, terms, width, _ = rights[-1].shape
     size = terms * width
     acc = jnp.zeros((width, width), F32)
-    for index, place, other in reversed(parts_of(kind)):
+    for index, place, other in parts_of(kind):
         for side in range(2):
-            if side == 0:
-                left = lefts[index][place * size : (place + 1) * size]
-                scale = lefts[index][lefts[index].shape[0] - PAD :].astype(F32)
-                right = [rights[index + 1 if index else 0][place, w] for w in range(terms)]
+            left = lefts[side][other, :size]
+            scale = lefts[side][other, size:].astype(F32)
+            if index == 0:
+                right = [rights[side][place, w] for w in range(terms)]
+            elif side == 0:
+                right = [rights[1 + index][place, w] for w in range(terms)]
             else:
-                left = given_left[other, :size]
-                scale = given_left[other, size:].astype(F32)
-                right = [rights[1][place, w] if index == 0 else given_right[other - 2, w] for w in range(terms)]
+                right = [rights[-1][other - 2, w] for w in range(terms)]
             half = jnp.dot(left, block, preferred_element_type=F32)
             halves = []
             for w in range(terms):
@@ -219,18 +211,14 @@
 
 def first_kernel(left_size, right_size, right_sector, vectors, *rest):
     *blocks, out, vector, sem = rest
-    half = len(MOVES) + 1
-    lefts, rights = blocks[: half - 1], blocks[half:-1]
     load_vectors(vectors, vector, sem)
     for kind in range(2):
         _, start = start_vector(kind, left_size, right_size, right_sector, vector)
-        out[kind] = apply(start.astype(BF16), kind, lefts, blocks[half - 1], rights, blocks[-1]).astype(BF16)
+        out[kind] = apply(start.astype(BF16), kind, blocks[:2], blocks[2:]).astype(BF16)
 
 
 def second_kernel(left_size, right_size, right_sector, vectors, image_here, image_there, *rest):
     *blocks, out, vector, sem = rest
-    half = len(MOVES) + 1
-    lefts, rights = blocks[: half - 1], blocks[half:-1]
     width = vector.shape[1]
     upper = lax.axis_index("mpo") // 2 >= lax.axis_size("mpo") // 4
     load_vectors(vectors, vector, sem)
@@ -249,7 +237,7 @@
         overlap = total(unit * image)
         ratio = jnp.where(length > 0.0, overlap / jnp.where(length > 0.0, length, 1.0), 0.0)
         rest = image - ratio * unit
-        after = jnp.where(mask, apply(rest.astype(BF16), kind, lefts, blocks[half - 1], rights, blocks[-1]), 0.0)
+        after = jnp.where(mask, apply(rest.astype(BF16), kind, blocks[:2], blocks[2:]), 0.0)
         share = jnp.where(upper == (kind == 1), 1.0, 0.0)
         numbers = (
             share * norm,
@@ -369,30 +357,31 @@
     with jax.named_scope("right_over_sec"):
         arrived = lax.all_to_all(right_out, "sec", 0, 0, tiled=True)
     with jax.named_scope("pack_left"):
-        lefts = pl.pallas_call(
+        *lefts, places = pl.pallas_call(
             pack_left_kernel,
-            out_shape=[jax.ShapeDtypeStruct((count * long + PAD, width), BF16) for count in counts],
-            in_specs=[scalars, anywhere],
-            out_specs=[anywhere] * len(MOVES),
+            out_shape=[jax.ShapeDtypeStruct((count * long + PAD, width), BF16) for count in counts]
+            + [jax.ShapeDtypeStruct((blocks,), jnp.int32)],
+            in_specs=[scalars, scalars, anywhere],
+            out_specs=[anywhere] * len(MOVES) + [scalars],
             scratch_shapes=[
                 pltpu.VMEM(left_environment.shape, BF16),
                 pltpu.VMEM((PAD, width), BF16),
                 pltpu.SemaphoreType.DMA((2,)),
             ],
             compiler_params=pltpu.CompilerParams(vmem_limit_bytes=8 * MIB),
-        )(term_weights, left_environment)
+        )(term_weights, right_sector, left_environment)
     with jax.named_scope("left_over_z"):
         lefts = [lefts[0]] + [lax.ppermute(left, "mpo", route) for left, route in zip(lefts[1:], routes[1:])]
     with jax.named_scope("left_over_core"):
-        given = pl.pallas_call(
+        kept, given = pl.pallas_call(
             collect_left_kernel,
-            out_shape=jax.ShapeDtypeStruct((blocks // 2, long + PAD, width), BF16),
+            out_shape=(jax.ShapeDtypeStruct((blocks // 2, long + PAD, width), BF16),) * 2,
             in_specs=[anywhere] * len(MOVES),
-            out_specs=anywhere,
+            out_specs=(anywhere, anywhere),
             scratch_shapes=[pltpu.SemaphoreType.DMA],
             compiler_params=pltpu.CompilerParams(vmem_limit_bytes=4 * MIB),
         )(*lefts)
-        lefts.append(lax.ppermute(given, "mpo", cores))
+        lefts = [kept, lax.ppermute(given, "mpo", cores)]
         arrived, *lefts = lax.optimization_barrier((arrived, *lefts))
     with jax.named_scope("order"):
         rights = pl.pallas_call(
@@ -400,13 +389,9 @@
             out_shape=[jax.ShapeDtypeStruct((count, terms, width, width), BF16) for count in [2, 2] + counts[1:]],
             in_specs=[scalars, anywhere],
             out_specs=[anywhere] * (len(MOVES) + 1),
-            scratch_shapes=[
-                pltpu.VMEM((blocks, terms, width, width), BF16),
-                pltpu.SMEM((blocks,), jnp.int32),
-                pltpu.SemaphoreType.DMA((blocks + 1,)),
-            ],
-            compiler_params=pltpu.CompilerParams(vmem_limit_bytes=40 * MIB),
-        )(right_sector, arrived.reshape(devices * SLOTS, terms, width, width))
+            scratch_shapes=[pltpu.SemaphoreType.DMA],
+            compiler_params=pltpu.CompilerParams(vmem_limit_bytes=4 * MIB),
+        )(places, arrived.reshape(devices * SLOTS, terms, width, width))
     with jax.named_scope("right_over_z"):
         stayed = [rights[0], lax.ppermute(rights[1], "mpo", cores)]
         rights = [lax.ppermute(right, "mpo", route) for right, route in zip(rights[2:], routes[1:])]
@@ -424,7 +409,7 @@
         image_here = pl.pallas_call(
             first_kernel,
             out_shape=jax.ShapeDtypeStruct((2, width, width), BF16),
-            in_specs=[scalars, scalars, scalars, anywhere] + [vmem] * (2 * len(MOVES) + 3),
+            in_specs=[scalars, scalars, scalars, anywhere] + [vmem] * (len(MOVES) + 4),
             out_specs=vmem,
             scratch_shapes=[pltpu.VMEM((2, width, width), BF16), pltpu.SemaphoreType.DMA],
             compiler_params=pltpu.CompilerParams(vmem_limit_bytes=16 * MIB),
@@ -435,7 +420,7 @@
         pieces = pl.pallas_call(
             second_kernel,
             out_shape=jax.ShapeDtypeStruct((layers, 3 * rows + 8, width), F32),
-            in_specs=[scalars, scalars, scalars, anywhere] + [vmem] * (2 * len(MOVES) + 5),
+            in_specs=[scalars, scalars, scalars, anywhere] + [vmem] * (len(MOVES) + 6),
             out_specs=vmem,
             scratch_shapes=[pltpu.VMEM((2, width, width), BF16), pltpu.SemaphoreType.DMA],
             compiler_params=pltpu.CompilerParams(vmem_limit_bytes=16 * MIB),

time: 110 us -> 108 us (0.982)
  local copies, waits for them, and re-layouts: 2.81 us -> 0.86 us
    unnamed x20 -> x16, local copies, waits for them, and re-layouts: 2.8 us -> 0.85 us
  transfers between devices with their start and end apart: 13 -> 13, of which waited for: 6 -> 6; matrix products, arithmetic and copies ran while one was open for 0% -> 0% of each run, Pallas kernels for 3% -> 4%
where the time goes in v7:
time: 108 us
  starting transfers between devices  36.6 us (34%)
  blocking collectives  30.3 us (28%)
  waiting for transfers between devices  23.8 us (22%)
  Pallas kernels  15.7 us (15%)
    all_to_all x1, blocking collectives, shards(): pieces = lax.all_to_all(pieces, 'mpo', 0, 0, tiled=True)  19.3 us
    all_to_all x1, blocking collectives, shards(): lax.all_to_all(jnp.broadcast_to(line[None], (devices, 8, width)), 'sec',...  10.9 us
    ppermute x4, starting transfers between devices, shards(): lax.ppermute(right, 'mpo', route)  9.32 us
    ppermute x4, starting transfers between devices, shards(): lax.ppermute(left, 'mpo', route)  9.32 us
    all_to_all x1, starting transfers between devices, shards(): arrived = lax.all_to_all(right_out, 'sec', 0, 0, tiled=True)  7.73 us
    ppermute x4, waiting for transfers between devices, shards(): lax.ppermute(left, 'mpo', route)  6.94 us
    ppermute x4, waiting for transfers between devices, shards(): lax.ppermute(right, 'mpo', route)  5.37 us
    all_to_all x1, waiting for transfers between devices, shards(): arrived = lax.all_to_all(right_out, 'sec', 0, 0, tiled=True)  5.3 us
  transfers between devices with their start and end apart: 13, of which 6 were waited for; matrix products, arithmetic and copies ran while one was open for 0% of the time, Pallas kernels for 4%

profile of v7, /device:TPU:1, one launch (start us, length us, event | category | flops | bytes accessed | tf_op | source)
XLA Modules:
  0.0 108.1 jit_solution(5033336965713145954)
XLA Ops:
  0.6 3.3 %pack_right.1 = bf16[16,2,2,128,128]{4,3,2,1,0:T(8,128)(2,1)} custom-call(s32[256]{0:T(256)} %right_sector.9, bf16[2,16,128,128]{3,2,1,0:T(8,128)(2,1)} %right_env.1), custom_call_target="tpu_custom_call" | custom-call | tf_op jit(solution)/shard_map/pack_right/pallas_call | solution.py:349
  3.9 0.0 copy-start.3
  3.9 0.0 copy-start.4
  3.9 0.0 copy-start.7
  3.9 7.7 %all-to-all-start = ((bf16[16,2,2,128,128]{4,3,2,1,0:T(8,128)(2,1)}), bf16[16,2,2,128,128]{4,3,2,1,0:T(8,128)(2,1)S(1)}, u32[]{:S(2)}, u32[]{:S(2)}) async-start(bf16[16,2,2,128,128]{4,3,2,1,0:T(8,128)(2,1)} %pack_right.1), calls=%async_computation | async-start | bytes 4194304 | tf_op jit(solution)/shard_map/right_over_sec/all_to_all | solution.py:358
  11.7 0.0 copy-done.3
  11.7 0.0 copy-done.4
  11.7 0.0 copy-done.7
  11.7 2.9 %pack_left.1 = (bf16[1040,128]{1,0:T(8,128)(2,1)S(1)}, bf16[528,128]{1,0:T(8,128)(2,1)S(1)}, bf16[528,128]{1,0:T(8,128)(2,1)S(1)}, bf16[1040,128]{1,0:T(8,128)(2...) custom-call(f32[2]{0:T(128)S(1)} %copy-done.7, s32[256]{0:T(256)S(1)} %copy-done.4, ...), custom_call_target="tpu_custom_call" | custom-call | tf_op jit(solution)/shard_map/pack_left/pallas_call | solution.py:360
  14.6 1.7 %collective-permute-start.2 = (bf16[1040,128]{1,0:T(8,128)(2,1)S(1)}, bf16[1040,128]{1,0:T(8,128)(2,1)S(1)}, u32[]{:S(2)}, u32[]{:S(2)}) collective-permute-start(bf16[1040,128]{1,0:T(8,128)(2,1)S(1)} %get-tuple-element.23), channel_id=1, source_target_pairs={{0,2},{1,3},{2,4},{3,5},{4,6},{5,7},{6,8},{7,9},{8,10},{9,11},{10,... | collective-permute-start | bytes 798728 | tf_op jit(solution)/shard_map/left_over_z/ppermute | solution.py:374
  16.3 4.0 %collective-permute-start.3 = (bf16[1040,128]{1,0:T(8,128)(2,1)S(1)}, bf16[1040,128]{1,0:T(8,128)(2,1)S(1)}, u32[]{:S(2)}, u32[]{:S(2)}) collective-permute-start(bf16[1040,128]{1,0:T(8,128)(2,1)S(1)} %get-tuple-element.24), channel_id=1, source_target_pairs={{0,14},{1,15},{2,0},{3,1},{4,2},{5,3},{6,4},{7,5},{8,6},{9,7},{10,... | collective-permute-start | bytes 798728 | tf_op jit(solution)/shard_map/left_over_z/ppermute | solution.py:374
  20.3 0.0 collective-permute-start
  20.3 3.6 %collective-permute-start.1 = (bf16[528,128]{1,0:T(8,128)(2,1)S(1)}, bf16[528,128]{1,0:T(8,128)(2,1)S(1)}, u32[]{:S(2)}, u32[]{:S(2)}) collective-permute-start(bf16[528,128]{1,0:T(8,128)(2,1)S(1)} %get-tuple-element.22), channel_id=1, source_target_pairs={{0,12},{1,13},{2,14},{3,15},{4,0},{5,1},{6,2},{7,3},{8,4},{9,5},{1... | collective-permute-start | bytes 405512 | tf_op jit(solution)/shard_map/left_over_z/ppermute | solution.py:374
  23.9 6.9 %collective-permute-done.refs_1_ = bf16[528,128]{1,0:T(8,128)(2,1)S(1)} collective-permute-done((bf16[528,128]{1,0:T(8,128)(2,1)S(1)}, bf16[528,128]{1,0:T(8,128)(2,1)S(1)}, u32[]{:S(2)}, u32[]{:S(2)}) %collective-permute-start) | collective-permute-done | bytes 135200 | tf_op jit(solution)/shard_map/left_over_z/ppermute | solution.py:374
  30.8 0.0 collective-permute-done.1.refs_2_
  30.8 0.0 collective-permute-done.2.refs_3_
  30.9 0.0 collective-permute-done.3.refs_4_
  30.9 0.0 copy-start
  30.9 0.0 copy-start.5
  30.9 0.0 copy-start.6
  30.9 1.5 %left_over_core.1 = (bf16[8,272,128]{2,1,0:T(8,128)(2,1)S(1)}, bf16[8,272,128]{2,1,0:T(8,128)(2,1)S(1)}) custom-call(bf16[1040,128]{1,0:T(8,128)(2,1)S(1)} %get-tuple-element.20.refs_0_, bf16[528,128]{1,0:T(8,128)(2,1)S(1)} %collective-permute-done.refs_1_, bf16[528,128]{1,0:T(8,128)(2,1)S(1)} %collective-permute-done.1.refs_2_, ...), custom_call_target="tpu_custom_call" | custom-call | tf_op jit(solution)/shard_map/left_over_core/pallas_call | solution.py:376
  32.4 2.1 %collective-permute-start.4 = (bf16[8,272,128]{2,1,0:T(8,128)(2,1)S(1)}, bf16[8,272,128]{2,1,0:T(8,128)(2,1)S(1)}, u32[]{:S(2)}, u32[]{:S(2)}) collective-permute-start(bf16[8,272,128]{2,1,0:T(8,128)(2,1)S(1)} %get-tuple-element.26), channel_id=1, source_target_pairs={{0,1},{1,0},{2,3},{3,2},{4,5},{5,4},{6,7},{7,6},{8,9},{9,8},{10,11... | collective-permute-start | bytes 1671176 | tf_op jit(solution)/shard_map/left_over_core/ppermute | solution.py:384
  34.5 1.6 %collective-permute-done.4.rest_1_ = bf16[8,272,128]{2,1,0:T(8,128)(2,1)S(1)} collective-permute-done((bf16[8,272,128]{2,1,0:T(8,128)(2,1)S(1)}, bf16[8,272,128]{2,1,0:T(8,128)(2,1)S(1)}, u32[]{:S(2)}, u32[]{:S(2)}) %collective-permute-start.4) | collective-permute-done | bytes 557088 | tf_op jit(solution)/shard_map/left_over_core/ppermute | solution.py:384
  36.1 0.8 copy-done.1
  36.9 5.3 %all-to-all-done = bf16[16,2,2,128,128]{4,3,2,1,0:T(8,128)(2,1)S(1)} async-done(((bf16[16,2,2,128,128]{4,3,2,1,0:T(8,128)(2,1)}), bf16[16,2,2,128,128]{4,3,2,1,0:T(8,128)(2,1)S(1)}, u32[]{:S(2)}, u32[]{:S(2)}) %all-to-all-start) | async-done | bytes 2097184 | tf_op jit(solution)/shard_map/right_over_sec/all_to_all | solution.py:358
  42.2 2.2 %order.1 = (bf16[2,2,128,128]{3,2,1,0:T(8,128)(2,1)S(1)}, bf16[2,2,128,128]{3,2,1,0:T(8,128)(2,1)S(1)}, bf16[2,2,128,128]{3,2,1,0:T(8,128)(2,1)S(1)}, bf16[2,2,1...) custom-call(s32[16]{0:T(128)S(1)} %get-tuple-element.29.places, ...), custom_call_target="tpu_custom_call" | custom-call | tf_op jit(solution)/shard_map/order/pallas_call | solution.py:387
  44.3 1.7 %collective-permute-start.8 = (bf16[4,2,128,128]{3,2,1,0:T(8,128)(2,1)S(1)}, bf16[4,2,128,128]{3,2,1,0:T(8,128)(2,1)S(1)}, u32[]{:S(2)}, u32[]{:S(2)}) collective-permute-start(bf16[4,2,128,128]{3,2,1,0:T(8,128)(2,1)S(1)} %get-tuple-element.35), channel_id=1, source_target_pairs={{0,2},{1,3},{2,4},{3,5},{4,6},{5,7},{6,8},{7,9},{8,10},{9,11},{10,... | collective-permute-start | bytes 786440 | tf_op jit(solution)/shard_map/right_over_z/ppermute | solution.py:397
  46.0 4.0 %collective-permute-start.9 = (bf16[4,2,128,128]{3,2,1,0:T(8,128)(2,1)S(1)}, bf16[4,2,128,128]{3,2,1,0:T(8,128)(2,1)S(1)}, u32[]{:S(2)}, u32[]{:S(2)}) collective-permute-start(bf16[4,2,128,128]{3,2,1,0:T(8,128)(2,1)S(1)} %get-tuple-element.36), channel_id=1, source_target_pairs={{0,14},{1,15},{2,0},{3,1},{4,2},{5,3},{6,4},{7,5},{8,6},{9,7},{10,... | collective-permute-start | bytes 786440 | tf_op jit(solution)/shard_map/right_over_z/ppermute | solution.py:397
  50.1 0.0 collective-permute-start.6
  50.1 3.6 %collective-permute-start.7 = (bf16[2,2,128,128]{3,2,1,0:T(8,128)(2,1)S(1)}, bf16[2,2,128,128]{3,2,1,0:T(8,128)(2,1)S(1)}, u32[]{:S(2)}, u32[]{:S(2)}) collective-permute-start(bf16[2,2,128,128]{3,2,1,0:T(8,128)(2,1)S(1)} %get-tuple-element.34), channel_id=1, source_target_pairs={{0,12},{1,13},{2,14},{3,15},{4,0},{5,1},{6,2},{7,3},{8,4},{9,5},{1... | collective-permute-start | bytes 393224 | tf_op jit(solution)/shard_map/right_over_z/ppermute | solution.py:397
  53.6 5.4 %collective-permute-done.6.refs_0_.rest_4_ = bf16[2,2,128,128]{3,2,1,0:T(8,128)(2,1)S(1)} collective-permute-done((bf16[2,2,128,128]{3,2,1,0:T(8,128)(2,1)S(1)}, bf16[2,2,128,128]{3,2,1,0:T(8,128)(2,1)S(1)}, u32[]{:S(2)}, u32[]{:S(2)}) %collective-permute-start.6) | collective-permute-done | bytes 131104 | tf_op jit(solution)/shard_map/right_over_z/ppermute | solution.py:397
  59.0 0.0 collective-permute-done.7.refs_1_.rest_5_
  59.0 0.0 collective-permute-done.8.refs_2_.rest_6_
  59.0 0.0 collective-permute-done.9.refs_3_.rest_7_
  59.0 0.5 right_over_core.1
  59.5 4.1 %collective-permute-start.10 = (bf16[6,2,128,128]{3,2,1,0:T(8,128)(2,1)S(1)}, bf16[6,2,128,128]{3,2,1,0:T(8,128)(2,1)S(1)}, u32[]{:S(2)}, u32[]{:S(2)}) collective-permute-start(bf16[6,2,128,128]{3,2,1,0:T(8,128)(2,1)S(1)} %right_over_core.1), channel_id=1, source_target_pairs={{0,1},{1,0},{2,3},{3,2},{4,5},{5,4},{6,7},{7,6},{8,9},{9,8},{10,11... | collective-permute-start | bytes 1179656 | tf_op jit(solution)/shard_map/right_over_core/ppermute | solution.py:407
  63.6 0.1 collective-permute-start.5
  63.7 1.4 %collective-permute-done.5.rest_3_ = bf16[2,2,128,128]{3,2,1,0:T(8,128)(2,1)S(1)} collective-permute-done((bf16[2,2,128,128]{3,2,1,0:T(8,128)(2,1)S(1)}, bf16[2,2,128,128]{3,2,1,0:T(8,128)(2,1)S(1)}, u32[]{:S(2)}, u32[]{:S(2)}) %collective-permute-start.5) | collective-permute-done | bytes 131104 | tf_op jit(solution)/shard_map/right_over_z/ppermute | solution.py:396
  65.2 0.0 collective-permute-done.10.rest_8_
  65.2 0.0 copy-done
  65.2 0.0 copy-done.6
  65.2 1.7 %first_image.1.image_here = bf16[2,128,128]{2,1,0:T(8,128)(2,1)S(1)} custom-call(s32[16]{0:T(128)S(1)} %copy-done.6, s32[256]{0:T(256)S(1)} %copy-done.5, s32[256]{0:T(256)S(1)} %copy-done.4, bf16[16,128,128]{2,1,0:T(8,128)(2,1)S(1)} %copy-done, bf16[8,272,128]{2,1,0:T(8,128)(2,1)S(1)} %get-tuple-element.27.rest_0_, bf16[8,272,128]{2,1,0:T(8,128)(2,1)S(1)} %copy-done.2, ...), custom_call_target="tpu_custom_call" | custom-call | tf_op jit(solution)/shard_map/first_image/pallas_call | solution.py:409
  66.9 3.9 %collective-permute-start.11 = (bf16[2,128,128]{2,1,0:T(8,128)(2,1)S(1)}, bf16[2,128,128]{2,1,0:T(8,128)(2,1)S(1)}, u32[]{:S(2)}, u32[]{:S(2)}) collective-permute-start(bf16[2,128,128]{2,1,0:T(8,128)(2,1)S(1)} %first_image.1.image_here), channel_id=1, source_target_pairs={{0,8},{1,9},{2,10},{3,11},{4,12},{5,13},{6,14},{7,15},{8,0},{9,1},... | collective-permute-start | bytes 196616 | tf_op jit(solution)/shard_map/swap_images/ppermute | solution.py:418
  70.8 3.2 %collective-permute-done.11.image_there = bf16[2,128,128]{2,1,0:T(8,128)(2,1)S(1)} collective-permute-done((bf16[2,128,128]{2,1,0:T(8,128)(2,1)S(1)}, bf16[2,128,128]{2,1,0:T(8,128)(2,1)S(1)}, u32[]{:S(2)}, u32[]{:S(2)}) %collective-permute-start.11) | collective-permute-done | bytes 65568 | tf_op jit(solution)/shard_map/swap_images/ppermute | solution.py:418
  74.0 2.0 %second_image.1 = f32[16,32,128]{2,1,0:T(8,128)S(1)} custom-call(s32[16]{0:T(128)S(1)} %copy-done.6, s32[256]{0:T(256)S(1)} %copy-done.5, s32[256]{0:T(256)S(1)} %copy-done.4, bf16[16,128,128]{2,1,0:T(8,128)(2,1)S(1)} %copy-done, bf16[2,128,128]{2,1,0:T(8,128)(2,1)S(1)} %first_image.1.image_here, ...), custom_call_target="tpu_custom_call" | custom-call | tf_op jit(solution)/shard_map/second_image/pallas_call | solution.py:420
  76.0 19.3 %all_to_all.15.pieces = f32[16,32,128]{2,1,0:T(8,128)S(1)} all-to-all(f32[16,32,128]{2,1,0:T(8,128)S(1)} %second_image.1), channel_id=1, replica_groups=mesh['sec'=16,'mpo'=16] {'mpo'}, dimensions={0} | all-to-all | bytes 524288 | tf_op jit(solution)/shard_map/rows_over_mpo/all_to_all | solution.py:429
  95.4 10.9 %all_to_all.16.shared = f32[16,8,128]{2,1,0:T(8,128)S(1)} all-to-all(f32[16,8,128]{2,1,0:T(8,128)S(1)} %broadcast_in_dim.2), channel_id=1, replica_groups=mesh['sec'=16,'mpo'=16] {'sec'}, dimensions={0} | all-to-all | bytes 131072 | tf_op jit(solution)/shard_map/numbers_over_sec/all_to_all | solution.py:432
  106.3 1.8 %finish.1 = (f32[16,8,128]{2,1,0:T(8,128)}, f32[16,8,128]{2,1,0:T(8,128)}, f32[3]{0:T(128)}) custom-call(s32[16]{0:T(128)S(1)} %copy-done.6, s32[256]{0:T(256)S(1)} %copy-done.5, s32[256]{0:T(256)S(1)} %copy-done.4, bf16[16,128,128]{2,1,0:T(8,128)(2,1)S(1)} %copy-done, f32[16,32,128]{2,1,0:T(8,128)S(1)} %all_to_all.15.pieces, ...), custom_call_target="tpu_custom_call" | custom-call | tf_op jit(solution)/shard_map/finish/pallas_call | solution.py:434
  (6 shorter events, 0.0 us)
Async XLA Ops:
  3.9 7.8 %copy-start.3 = (bf16[2,16,128,128]{3,2,1,0:T(8,128)(2,1)S(1)}, bf16[2,16,128,128]{3,2,1,0:T(8,128)(2,1)}, u32[]{:S(2)}) copy-start(bf16[2,16,128,128]{3,2,1,0:T(8,128)(2,1)} %left_env.1) | copy-start | bytes 3145732
  3.9 7.8 %copy-start.4 = (s32[256]{0:T(256)S(1)}, s32[256]{0:T(256)}, u32[]{:S(2)}) copy-start(s32[256]{0:T(256)} %right_sector.9) | copy-start | bytes 3076
  3.9 7.8 %copy-start.7 = (f32[2]{0:T(128)S(1)}, f32[2]{0:T(128)}, u32[]{:S(2)}) copy-start(f32[2]{0:T(128)} %weights.1) | copy-start | bytes 28
  3.9 38.2 %all-to-all-start = ((bf16[16,2,2,128,128]{4,3,2,1,0:T(8,128)(2,1)}), bf16[16,2,2,128,128]{4,3,2,1,0:T(8,128)(2,1)S(1)}, u32[]{:S(2)}, u32[]{:S(2)}) async-start(bf16[16,2,2,128,128]{4,3,2,1,0:T(8,128)(2,1)} %pack_right.1), calls=%async_computation | async-start | bytes 4194304 | tf_op jit(solution)/shard_map/right_over_sec/all_to_all | solution.py:358
  14.6 16.3 %collective-permute-start.2 = (bf16[1040,128]{1,0:T(8,128)(2,1)S(1)}, bf16[1040,128]{1,0:T(8,128)(2,1)S(1)}, u32[]{:S(2)}, u32[]{:S(2)}) collective-permute-start(bf16[1040,128]{1,0:T(8,128)(2,1)S(1)} %get-tuple-element.23), channel_id=1, source_target_pairs={{0,2},{1,3},{2,4},{3,5},{4,6},{5,7},{6,8},{7,9},{8,10},{9,11},{10,... | collective-permute-start | bytes 798728 | tf_op jit(solution)/shard_map/left_over_z/ppermute | solution.py:374
  16.3 14.5 %collective-permute-start.3 = (bf16[1040,128]{1,0:T(8,128)(2,1)S(1)}, bf16[1040,128]{1,0:T(8,128)(2,1)S(1)}, u32[]{:S(2)}, u32[]{:S(2)}) collective-permute-start(bf16[1040,128]{1,0:T(8,128)(2,1)S(1)} %get-tuple-element.24), channel_id=1, source_target_pairs={{0,14},{1,15},{2,0},{3,1},{4,2},{5,3},{6,4},{7,5},{8,6},{9,7},{10,... | collective-permute-start | bytes 798728 | tf_op jit(solution)/shard_map/left_over_z/ppermute | solution.py:374
  20.3 10.5 %collective-permute-start = (bf16[528,128]{1,0:T(8,128)(2,1)S(1)}, bf16[528,128]{1,0:T(8,128)(2,1)S(1)}, u32[]{:S(2)}, u32[]{:S(2)}) collective-permute-start(bf16[528,128]{1,0:T(8,128)(2,1)S(1)} %get-tuple-element.21), channel_id=1, source_target_pairs={{0,4},{1,5},{2,6},{3,7},{4,8},{5,9},{6,10},{7,11},{8,12},{9,13},{1... | collective-permute-start | bytes 405512 | tf_op jit(solution)/shard_map/left_over_z/ppermute | solution.py:374
  20.3 10.5 %collective-permute-start.1 = (bf16[528,128]{1,0:T(8,128)(2,1)S(1)}, bf16[528,128]{1,0:T(8,128)(2,1)S(1)}, u32[]{:S(2)}, u32[]{:S(2)}) collective-permute-start(bf16[528,128]{1,0:T(8,128)(2,1)S(1)} %get-tuple-element.22), channel_id=1, source_target_pairs={{0,12},{1,13},{2,14},{3,15},{4,0},{5,1},{6,2},{7,3},{8,4},{9,5},{1... | collective-permute-start | bytes 405512 | tf_op jit(solution)/shard_map/left_over_z/ppermute | solution.py:374
  30.9 34.3 %copy-start = (bf16[16,128,128]{2,1,0:T(8,128)(2,1)S(1)}, bf16[16,128,128]{2,1,0:T(8,128)(2,1)}, u32[]{:S(2)}) copy-start(bf16[16,128,128]{2,1,0:T(8,128)(2,1)} %vectors.5) | copy-start | bytes 1572868
  30.9 34.3 %copy-start.5 = (s32[256]{0:T(256)S(1)}, s32[256]{0:T(256)}, u32[]{:S(2)}) copy-start(s32[256]{0:T(256)} %right_size.5) | copy-start | bytes 3076
  30.9 34.3 %copy-start.6 = (s32[16]{0:T(128)S(1)}, s32[16]{0:T(128)}, u32[]{:S(2)}) copy-start(s32[16]{0:T(128)} %left_size.5) | copy-start | bytes 196
  32.4 3.7 %collective-permute-start.4 = (bf16[8,272,128]{2,1,0:T(8,128)(2,1)S(1)}, bf16[8,272,128]{2,1,0:T(8,128)(2,1)S(1)}, u32[]{:S(2)}, u32[]{:S(2)}) collective-permute-start(bf16[8,272,128]{2,1,0:T(8,128)(2,1)S(1)} %get-tuple-element.26), channel_id=1, source_target_pairs={{0,1},{1,0},{2,3},{3,2},{4,5},{5,4},{6,7},{7,6},{8,9},{9,8},{10,11... | collective-permute-start | bytes 1671176 | tf_op jit(solution)/shard_map/left_over_core/ppermute | solution.py:384
  36.1 0.8 copy-start.1
  42.2 23.0 %copy-start.2 = (bf16[8,272,128]{2,1,0:T(8,128)(2,1)S(1)}, bf16[8,272,128]{2,1,0:T(8,128)(2,1)}, u32[]{:S(2)}) copy-start(bf16[8,272,128]{2,1,0:T(8,128)(2,1)} %copy-done.1) | copy-start | bytes 1671172
  44.3 14.7 %collective-permute-start.8 = (bf16[4,2,128,128]{3,2,1,0:T(8,128)(2,1)S(1)}, bf16[4,2,128,128]{3,2,1,0:T(8,128)(2,1)S(1)}, u32[]{:S(2)}, u32[]{:S(2)}) collective-permute-start(bf16[4,2,128,128]{3,2,1,0:T(8,128)(2,1)S(1)} %get-tuple-element.35), channel_id=1, source_target_pairs={{0,2},{1,3},{2,4},{3,5},{4,6},{5,7},{6,8},{7,9},{8,10},{9,11},{10,... | collective-permute-start | bytes 786440 | tf_op jit(solution)/shard_map/right_over_z/ppermute | solution.py:397
  46.0 13.0 %collective-permute-start.9 = (bf16[4,2,128,128]{3,2,1,0:T(8,128)(2,1)S(1)}, bf16[4,2,128,128]{3,2,1,0:T(8,128)(2,1)S(1)}, u32[]{:S(2)}, u32[]{:S(2)}) collective-permute-start(bf16[4,2,128,128]{3,2,1,0:T(8,128)(2,1)S(1)} %get-tuple-element.36), channel_id=1, source_target_pairs={{0,14},{1,15},{2,0},{3,1},{4,2},{5,3},{6,4},{7,5},{8,6},{9,7},{10,... | collective-permute-start | bytes 786440 | tf_op jit(solution)/shard_map/right_over_z/ppermute | solution.py:397
  50.1 8.9 %collective-permute-start.6 = (bf16[2,2,128,128]{3,2,1,0:T(8,128)(2,1)S(1)}, bf16[2,2,128,128]{3,2,1,0:T(8,128)(2,1)S(1)}, u32[]{:S(2)}, u32[]{:S(2)}) collective-permute-start(bf16[2,2,128,128]{3,2,1,0:T(8,128)(2,1)S(1)} %get-tuple-element.33), channel_id=1, source_target_pairs={{0,4},{1,5},{2,6},{3,7},{4,8},{5,9},{6,10},{7,11},{8,12},{9,13},{1... | collective-permute-start | bytes 393224 | tf_op jit(solution)/shard_map/right_over_z/ppermute | solution.py:397
  50.1 8.9 %collective-permute-start.7 = (bf16[2,2,128,128]{3,2,1,0:T(8,128)(2,1)S(1)}, bf16[2,2,128,128]{3,2,1,0:T(8,128)(2,1)S(1)}, u32[]{:S(2)}, u32[]{:S(2)}) collective-permute-start(bf16[2,2,128,128]{3,2,1,0:T(8,128)(2,1)S(1)} %get-tuple-element.34), channel_id=1, source_target_pairs={{0,12},{1,13},{2,14},{3,15},{4,0},{5,1},{6,2},{7,3},{8,4},{9,5},{1... | collective-permute-start | bytes 393224 | tf_op jit(solution)/shard_map/right_over_z/ppermute | solution.py:397
  59.5 5.6 %collective-permute-start.10 = (bf16[6,2,128,128]{3,2,1,0:T(8,128)(2,1)S(1)}, bf16[6,2,128,128]{3,2,1,0:T(8,128)(2,1)S(1)}, u32[]{:S(2)}, u32[]{:S(2)}) collective-permute-start(bf16[6,2,128,128]{3,2,1,0:T(8,128)(2,1)S(1)} %right_over_core.1), channel_id=1, source_target_pairs={{0,1},{1,0},{2,3},{3,2},{4,5},{5,4},{6,7},{7,6},{8,9},{9,8},{10,11... | collective-permute-start | bytes 1179656 | tf_op jit(solution)/shard_map/right_over_core/ppermute | solution.py:407
  63.6 1.5 %collective-permute-start.5 = (bf16[2,2,128,128]{3,2,1,0:T(8,128)(2,1)S(1)}, bf16[2,2,128,128]{3,2,1,0:T(8,128)(2,1)S(1)}, u32[]{:S(2)}, u32[]{:S(2)}) collective-permute-start(bf16[2,2,128,128]{3,2,1,0:T(8,128)(2,1)S(1)} %get-tuple-element.32), channel_id=1, source_target_pairs={{0,1},{1,0},{2,3},{3,2},{4,5},{5,4},{6,7},{7,6},{8,9},{9,8},{10,11... | collective-permute-start | bytes 393224 | tf_op jit(solution)/shard_map/right_over_z/ppermute | solution.py:396
  66.9 7.1 %collective-permute-start.11 = (bf16[2,128,128]{2,1,0:T(8,128)(2,1)S(1)}, bf16[2,128,128]{2,1,0:T(8,128)(2,1)S(1)}, u32[]{:S(2)}, u32[]{:S(2)}) collective-permute-start(bf16[2,128,128]{2,1,0:T(8,128)(2,1)S(1)} %first_image.1.image_here), channel_id=1, source_target_pairs={{0,8},{1,9},{2,10},{3,11},{4,12},{5,13},{6,14},{7,15},{8,0},{9,1},... | collective-permute-start | bytes 196616 | tf_op jit(solution)/shard_map/swap_images/ppermute | solution.py:418

commit v8 on v7

--- a/solution.py
+++ b/solution.py
@@ -164,6 +164,11 @@
     return jnp.sum(jnp.sum(x, axis=0, keepdims=True), axis=1, keepdims=True)
 
 
+def split(x):
+    high = x.astype(BF16)
+    return high, (x - high.astype(F32)).astype(BF16)
+
+
 def apply(block, kind, lefts, rights):
     _, terms, width, _ = rights[-1].shape
     size = terms * width
@@ -179,16 +184,19 @@
             else:
                 right = [rights[-1][other - 2, w] for w in range(terms)]
             half = jnp.dot(left, block, preferred_element_type=F32)
+            if block.shape[1] > width:
+                half = half[:, :width] + half[:, width:]
             halves = []
             for w in range(terms):
                 weight = scale[3 * w : 3 * w + 1] + scale[3 * w + 1 : 3 * w + 2] + scale[3 * w + 2 : 3 * w + 3]
-                halves.append((weight * half[w * width : (w + 1) * width]).astype(BF16))
-            acc = acc + lax.dot_general(
-                jnp.concatenate(halves, axis=1),
+                halves.append(split(weight * half[w * width : (w + 1) * width]))
+            both = lax.dot_general(
+                jnp.concatenate([jnp.concatenate(part, axis=1) for part in zip(*halves)], axis=0),
                 jnp.concatenate(right, axis=1),
                 (((1,), (1,)), ((), ())),
                 preferred_element_type=F32,
             )
+            acc = acc + (both[:width] + both[width:])
     return acc
 
 
@@ -209,15 +217,34 @@
     start_all([pltpu.make_async_copy(vectors.at[own_sector(kind)], vector.at[kind], sem) for kind in range(2)])
 
 
+def scaled(start):
+    cells = float(start.shape[0] * start.shape[1])
+    norm = total(start * start)
+    unit = start * (1.0 / jnp.sqrt(norm / cells + 1e-06))
+    return norm, unit, total(unit * unit)
+
+
+def over(top, bottom):
+    return jnp.where(bottom > 0.0, top / jnp.where(bottom > 0.0, bottom, 1.0), 0.0)
+
+
 def first_kernel(left_size, right_size, right_sector, vectors, *rest):
-    *blocks, out, vector, sem = rest
+    *blocks, out, ratios, vector, sem = rest
     load_vectors(vectors, vector, sem)
+    row = lax.broadcasted_iota(jnp.int32, ratios.shape, 0)
+    found = jnp.zeros(ratios.shape, F32)
     for kind in range(2):
-        _, start = start_vector(kind, left_size, right_size, right_sector, vector)
-        out[kind] = apply(start.astype(BF16), kind, blocks[:2], blocks[2:]).astype(BF16)
-
-
-def second_kernel(left_size, right_size, right_sector, vectors, image_here, image_there, *rest):
+        mask, start = start_vector(kind, left_size, right_size, right_sector, vector)
+        norm, unit, length = scaled(start)
+        scale = 1.0 / jnp.sqrt(norm / float(start.shape[0] * start.shape[1]) + 1e-06)
+        image = jnp.where(mask, apply(start.astype(BF16), kind, blocks[:2], blocks[2:]), 0.0) * scale
+        ratio = over(total(unit * image), length)
+        out[kind] = (image - ratio * unit).astype(BF16)
+        found = jnp.where(row == kind, ratio, found)
+    ratios[...] = found
+
+
+def second_kernel(left_size, right_size, right_sector, vectors, ratios, image_here, image_there, *rest):
     *blocks, out, vector, sem = rest
     width = vector.shape[1]
     upper = lax.axis_index("mpo") // 2 >= lax.axis_size("mpo") // 4
@@ -227,37 +254,43 @@
     lane = lax.broadcasted_iota(jnp.int32, (8, width), 1)
     line = jnp.zeros((8, width), F32)
     rests = []
+    afters = []
     for kind in range(2):
         mask, start = start_vector(kind, left_size, right_size, right_sector, vector)
-        norm = total(start * start)
-        scale = 1.0 / jnp.sqrt(norm / float(width * width) + 1e-06)
-        image = jnp.where(mask, image_here[kind].astype(F32) + image_there[kind].astype(F32), 0.0) * scale
-        unit = start * scale
-        length = total(unit * unit)
-        overlap = total(unit * image)
-        ratio = jnp.where(length > 0.0, overlap / jnp.where(length > 0.0, length, 1.0), 0.0)
-        rest = image - ratio * unit
-        after = jnp.where(mask, apply(rest.astype(BF16), kind, blocks[:2], blocks[2:]), 0.0)
+        norm, unit, length = scaled(start)
+        rest = image_here[kind].astype(F32) + image_there[kind].astype(F32)
+        block = jnp.concatenate(split(rest), axis=1)
+        after = jnp.where(mask, apply(block, kind, blocks[:2], blocks[2:]), 0.0)
+        square = total(rest * rest)
+        on_rest = total(rest * after)
+        on_unit = total(unit * after)
+        rest_ratio = over(on_rest, square)
+        unit_ratio = over(on_unit, length)
         share = jnp.where(upper == (kind == 1), 1.0, 0.0)
         numbers = (
             share * norm,
-            share * overlap,
-            share * ratio,
-            share * total(rest * rest),
-            total(rest * after),
-            total(unit * after) + share * total(rest * image),
+            ratios[kind : kind + 1, :1],
+            share * square,
+            on_rest,
+            on_unit,
             share * total(rest * unit),
+            rest_ratio,
+            unit_ratio,
         )
+        after = after - rest_ratio * rest - unit_ratio * unit
         place = own_sector(kind) * LANES
         for j, number in enumerate(numbers):
             line = jnp.where(lane == place + j, number, line)
         rests.append(rest)
-        for d in range(parts):
-            out[d, (1 + kind) * rows : (2 + kind) * rows] = after[d * rows : (d + 1) * rows]
+        afters.append(after)
     chosen = jnp.where(upper, rests[1], rests[0])
+    high, _ = split(line)
+    mid, low = split(line - high.astype(F32))
+    row = lax.broadcasted_iota(jnp.int32, line.shape, 0)
+    coded = jnp.where(row == 0, high.astype(F32), jnp.where(row == 1, mid.astype(F32), jnp.where(row == 2, low.astype(F32), 0.0)))
     for d in range(parts):
-        out[d, :rows] = chosen[d * rows : (d + 1) * rows]
-        out[d, 3 * rows :] = line
+        own_rows = [x[d * rows : (d + 1) * rows] for x in (chosen, *afters)]
+        out[d] = jnp.concatenate([*own_rows, coded], axis=0).astype(BF16)
 
 
 def finish_kernel(left_size, right_size, right_sector, vectors, pieces, shared, next_out, rest_out, coef_out, vector, sem):
@@ -280,17 +313,17 @@
 
     lead = lane == 0
     norm = jnp.where(lead, field(stats, 0), 0.0)
-    overlap = field(stats, 1)
-    ratio = field(stats, 2)
+    ratio, square, on_rest, on_unit, skew = (field(stats, j) for j in range(1, 6))
     gain = 1.0 / jnp.sqrt(total(norm) / entries + 1e-06)
-    mean = jnp.where(lead, norm, 0.0) / cells + 1e-06
+    mean = norm / cells + 1e-06
     weight = jnp.where(lead, (gain * gain) * mean, 0.0)
     length = norm / mean
+    overlap = ratio * length + skew
     alpha = total(jnp.where(lead, weight * overlap, 0.0)) / entries
     delta = jnp.where(lead, ratio - alpha, 0.0)
-    rest_total = total(jnp.where(lead, weight * (field(stats, 3) + delta * delta * length + 2.0 * delta * field(stats, 6)), 0.0))
+    rest_total = total(jnp.where(lead, weight * (square + delta * delta * length + 2.0 * delta * skew), 0.0))
     beta = jnp.sqrt(rest_total / entries + 1e-06)
-    inner = field(stats, 4) + delta * field(stats, 5) + delta * delta * overlap
+    inner = on_rest + delta * (on_unit + square + ratio * skew) + delta * delta * overlap
     alpha_next = total(jnp.where(lead, weight * inner, 0.0)) / entries / beta / beta
     for j, number in enumerate((alpha, beta, alpha_next)):
         coef_out[j] = number[0, 0]
@@ -299,9 +332,7 @@
         cut, kind, core = q // 4, q // 2 % 2, q % 2
         lower = 2 * ((cut + 1 + kind) % (chips // 2)) + core
         higher = lower + chips
-        lane_one = lax.broadcasted_iota(jnp.int32, line.shape, 1)
-        norm_q = jnp.sum(jnp.where(lane_one == q * LANES, line, 0.0), axis=1, keepdims=True)
-        ratio_q = jnp.sum(jnp.where(lane_one == q * LANES + 2, line, 0.0), axis=1, keepdims=True)
+        norm_q, ratio_q, rest_q, unit_q = (line[:, q * LANES + j : q * LANES + j + 1] for j in (0, 1, 6, 7))
         root = jnp.sqrt(norm_q / cells + 1e-06)
         scale = gain * root
         row = lax.broadcasted_iota(jnp.int32, (rows, width), 0) + part * rows
@@ -312,14 +343,16 @@
         for j in range(1, groups):
             own_rows = jnp.where(part % groups == j, group[j * rows : (j + 1) * rows], own_rows)
         unit = jnp.where(mask, own_rows, 0.0) / root
-        rest = pieces[higher if kind else lower, :rows]
+        sent = [pieces[owner].astype(F32) for owner in (lower, higher)]
+        rest = sent[kind][:rows]
         after_rows = slice((1 + kind) * rows, (2 + kind) * rows)
-        after = pieces[lower, after_rows] + pieces[higher, after_rows]
+        after = sent[0][after_rows] + sent[1][after_rows]
         shift = ratio_q - alpha
         second = (scale / beta) * (rest + shift * unit)
-        image = (scale / beta) * (after + shift * (rest + ratio_q * unit))
         next_out[q] = second
-        rest_out[q] = image - alpha_next * second - (beta * scale) * unit
+        on_second = rest_q + shift - alpha_next
+        on_first = unit_q + shift * (ratio_q - alpha_next)
+        rest_out[q] = (scale / beta) * (after + on_second * rest + on_first * unit) - (beta * scale) * unit
 
 
 def shards(
@@ -406,11 +439,14 @@
         )(*rights)
         rights = stayed + rights + [lax.ppermute(given, "mpo", cores)]
     with jax.named_scope("first_image"):
-        image_here = pl.pallas_call(
+        image_here, ratios = pl.pallas_call(
             first_kernel,
-            out_shape=jax.ShapeDtypeStruct((2, width, width), BF16),
+            out_shape=(
+                jax.ShapeDtypeStruct((2, width, width), BF16),
+                jax.ShapeDtypeStruct((8, width), F32),
+            ),
             in_specs=[scalars, scalars, scalars, anywhere] + [vmem] * (len(MOVES) + 4),
-            out_specs=vmem,
+            out_specs=(vmem, vmem),
             scratch_shapes=[pltpu.VMEM((2, width, width), BF16), pltpu.SemaphoreType.DMA],
             compiler_params=pltpu.CompilerParams(vmem_limit_bytes=16 * MIB),
         )(left_size, right_size, right_sector, wavefunction, *lefts, *rights)
@@ -419,17 +455,17 @@
     with jax.named_scope("second_image"):
         pieces = pl.pallas_call(
             second_kernel,
-            out_shape=jax.ShapeDtypeStruct((layers, 3 * rows + 8, width), F32),
-            in_specs=[scalars, scalars, scalars, anywhere] + [vmem] * (len(MOVES) + 6),
+            out_shape=jax.ShapeDtypeStruct((layers, 3 * rows + 8, width), BF16),
+            in_specs=[scalars, scalars, scalars, anywhere] + [vmem] * (len(MOVES) + 7),
             out_specs=vmem,
             scratch_shapes=[pltpu.VMEM((2, width, width), BF16), pltpu.SemaphoreType.DMA],
             compiler_params=pltpu.CompilerParams(vmem_limit_bytes=16 * MIB),
-        )(left_size, right_size, right_sector, wavefunction, image_here, image_there, *lefts, *rights)
+        )(left_size, right_size, right_sector, wavefunction, ratios, image_here, image_there, *lefts, *rights)
     with jax.named_scope("rows_over_mpo"):
         pieces = lax.all_to_all(pieces, "mpo", 0, 0, tiled=True)
     with jax.named_scope("numbers_over_sec"):
-        line = jnp.sum(pieces[:, 3 * rows :, :], axis=0)
-        shared = lax.all_to_all(jnp.broadcast_to(line[None], (devices, 8, width)), "sec", 0, 0, tiled=True)
+        line = jnp.sum(pieces[:, 3 * rows :, :].astype(F32), axis=(0, 1))
+        shared = lax.all_to_all(jnp.broadcast_to(line[None, None], (devices, 8, width)), "sec", 0, 0, tiled=True)
     with jax.named_scope("finish"):
         next_vector, residual, coefficients = pl.pallas_call(
             finish_kernel,

time: 108 us -> 107 us (level)
  blocking collectives: 30.3 us -> 27.7 us
    all_to_all x1, blocking collectives: 19.3 us -> 16.8 us  [shards(): pieces = lax.all_to_all(pieces, 'mpo', 0, 0, tiled=True)]
where the time goes in v8:
time: 107 us; the launch traced here: 106 us
  starting transfers between devices  36.6 us (34%)
  blocking collectives  27.7 us (26%)
  waiting for transfers between devices  23.8 us (22%)
  Pallas kernels  16.6 us (16%)
    all_to_all x1, blocking collectives, shards(): pieces = lax.all_to_all(pieces, 'mpo', 0, 0, tiled=True)  16.8 us
    all_to_all x1, blocking collectives, shards(): lax.all_to_all(jnp.broadcast_to(line[None, None], (devices, 8, width)), '...  10.9 us
    ppermute x4, starting transfers between devices, shards(): lax.ppermute(left, 'mpo', route)  9.32 us
    ppermute x4, starting transfers between devices, shards(): lax.ppermute(right, 'mpo', route)  9.32 us
    all_to_all x1, starting transfers between devices, shards(): arrived = lax.all_to_all(right_out, 'sec', 0, 0, tiled=True)  7.73 us
    ppermute x4, waiting for transfers between devices, shards(): lax.ppermute(left, 'mpo', route)  6.94 us
    ppermute x4, waiting for transfers between devices, shards(): lax.ppermute(right, 'mpo', route)  5.37 us
    all_to_all x1, waiting for transfers between devices, shards(): arrived = lax.all_to_all(right_out, 'sec', 0, 0, tiled=True)  5.3 us
  transfers between devices with their start and end apart: 13, of which 6 were waited for; matrix products, arithmetic and copies ran while one was open for 0% of the time, Pallas kernels for 4%

profile of v8, /device:TPU:1, one launch (start us, length us, event | category | flops | bytes accessed | tf_op | source)
XLA Modules:
  0.0 106.3 jit_solution(7965406283910422969)
XLA Ops:
  0.6 3.3 %pack_right.1 = bf16[16,2,2,128,128]{4,3,2,1,0:T(8,128)(2,1)} custom-call(s32[256]{0:T(256)} %right_sector.9, bf16[2,16,128,128]{3,2,1,0:T(8,128)(2,1)} %right_env.1), custom_call_target="tpu_custom_call" | custom-call | tf_op jit(solution)/shard_map/pack_right/pallas_call | solution.py:382
  3.9 0.0 copy-start.3
  3.9 0.0 copy-start.4
  3.9 0.0 copy-start.7
  3.9 7.7 %all-to-all-start = ((bf16[16,2,2,128,128]{4,3,2,1,0:T(8,128)(2,1)}), bf16[16,2,2,128,128]{4,3,2,1,0:T(8,128)(2,1)S(1)}, u32[]{:S(2)}, u32[]{:S(2)}) async-start(bf16[16,2,2,128,128]{4,3,2,1,0:T(8,128)(2,1)} %pack_right.1), calls=%async_computation | async-start | bytes 4194304 | tf_op jit(solution)/shard_map/right_over_sec/all_to_all | solution.py:391
  11.7 0.0 copy-done.3
  11.7 0.0 copy-done.4
  11.7 0.0 copy-done.7
  11.7 2.9 %pack_left.1 = (bf16[1040,128]{1,0:T(8,128)(2,1)S(1)}, bf16[528,128]{1,0:T(8,128)(2,1)S(1)}, bf16[528,128]{1,0:T(8,128)(2,1)S(1)}, bf16[1040,128]{1,0:T(8,128)(2...) custom-call(f32[2]{0:T(128)S(1)} %copy-done.7, s32[256]{0:T(256)S(1)} %copy-done.4, ...), custom_call_target="tpu_custom_call" | custom-call | tf_op jit(solution)/shard_map/pack_left/pallas_call | solution.py:393
  14.6 1.7 %collective-permute-start.2 = (bf16[1040,128]{1,0:T(8,128)(2,1)S(1)}, bf16[1040,128]{1,0:T(8,128)(2,1)S(1)}, u32[]{:S(2)}, u32[]{:S(2)}) collective-permute-start(bf16[1040,128]{1,0:T(8,128)(2,1)S(1)} %get-tuple-element.25), channel_id=1, source_target_pairs={{0,2},{1,3},{2,4},{3,5},{4,6},{5,7},{6,8},{7,9},{8,10},{9,11},{10,... | collective-permute-start | bytes 798728 | tf_op jit(solution)/shard_map/left_over_z/ppermute | solution.py:407
  16.3 4.0 %collective-permute-start.3 = (bf16[1040,128]{1,0:T(8,128)(2,1)S(1)}, bf16[1040,128]{1,0:T(8,128)(2,1)S(1)}, u32[]{:S(2)}, u32[]{:S(2)}) collective-permute-start(bf16[1040,128]{1,0:T(8,128)(2,1)S(1)} %get-tuple-element.26), channel_id=1, source_target_pairs={{0,14},{1,15},{2,0},{3,1},{4,2},{5,3},{6,4},{7,5},{8,6},{9,7},{10,... | collective-permute-start | bytes 798728 | tf_op jit(solution)/shard_map/left_over_z/ppermute | solution.py:407
  20.3 0.0 collective-permute-start
  20.3 3.6 %collective-permute-start.1 = (bf16[528,128]{1,0:T(8,128)(2,1)S(1)}, bf16[528,128]{1,0:T(8,128)(2,1)S(1)}, u32[]{:S(2)}, u32[]{:S(2)}) collective-permute-start(bf16[528,128]{1,0:T(8,128)(2,1)S(1)} %get-tuple-element.24), channel_id=1, source_target_pairs={{0,12},{1,13},{2,14},{3,15},{4,0},{5,1},{6,2},{7,3},{8,4},{9,5},{1... | collective-permute-start | bytes 405512 | tf_op jit(solution)/shard_map/left_over_z/ppermute | solution.py:407
  23.9 6.9 %collective-permute-done.refs_1_ = bf16[528,128]{1,0:T(8,128)(2,1)S(1)} collective-permute-done((bf16[528,128]{1,0:T(8,128)(2,1)S(1)}, bf16[528,128]{1,0:T(8,128)(2,1)S(1)}, u32[]{:S(2)}, u32[]{:S(2)}) %collective-permute-start) | collective-permute-done | bytes 135200 | tf_op jit(solution)/shard_map/left_over_z/ppermute | solution.py:407
  30.8 0.0 collective-permute-done.1.refs_2_
  30.8 0.0 collective-permute-done.2.refs_3_
  30.9 0.0 collective-permute-done.3.refs_4_
  30.9 0.0 copy-start
  30.9 0.0 copy-start.5
  30.9 0.0 copy-start.6
  30.9 1.5 %left_over_core.1 = (bf16[8,272,128]{2,1,0:T(8,128)(2,1)S(1)}, bf16[8,272,128]{2,1,0:T(8,128)(2,1)S(1)}) custom-call(bf16[1040,128]{1,0:T(8,128)(2,1)S(1)} %get-tuple-element.22.refs_0_, bf16[528,128]{1,0:T(8,128)(2,1)S(1)} %collective-permute-done.refs_1_, bf16[528,128]{1,0:T(8,128)(2,1)S(1)} %collective-permute-done.1.refs_2_, ...), custom_call_target="tpu_custom_call" | custom-call | tf_op jit(solution)/shard_map/left_over_core/pallas_call | solution.py:409
  32.4 2.1 %collective-permute-start.4 = (bf16[8,272,128]{2,1,0:T(8,128)(2,1)S(1)}, bf16[8,272,128]{2,1,0:T(8,128)(2,1)S(1)}, u32[]{:S(2)}, u32[]{:S(2)}) collective-permute-start(bf16[8,272,128]{2,1,0:T(8,128)(2,1)S(1)} %get-tuple-element.28), channel_id=1, source_target_pairs={{0,1},{1,0},{2,3},{3,2},{4,5},{5,4},{6,7},{7,6},{8,9},{9,8},{10,11... | collective-permute-start | bytes 1671176 | tf_op jit(solution)/shard_map/left_over_core/ppermute | solution.py:417
  34.5 1.6 %collective-permute-done.4.rest_1_ = bf16[8,272,128]{2,1,0:T(8,128)(2,1)S(1)} collective-permute-done((bf16[8,272,128]{2,1,0:T(8,128)(2,1)S(1)}, bf16[8,272,128]{2,1,0:T(8,128)(2,1)S(1)}, u32[]{:S(2)}, u32[]{:S(2)}) %collective-permute-start.4) | collective-permute-done | bytes 557088 | tf_op jit(solution)/shard_map/left_over_core/ppermute | solution.py:417
  36.1 0.8 copy-done.1
  36.9 5.3 %all-to-all-done = bf16[16,2,2,128,128]{4,3,2,1,0:T(8,128)(2,1)S(1)} async-done(((bf16[16,2,2,128,128]{4,3,2,1,0:T(8,128)(2,1)}), bf16[16,2,2,128,128]{4,3,2,1,0:T(8,128)(2,1)S(1)}, u32[]{:S(2)}, u32[]{:S(2)}) %all-to-all-start) | async-done | bytes 2097184 | tf_op jit(solution)/shard_map/right_over_sec/all_to_all | solution.py:391
  42.2 2.2 %order.1 = (bf16[2,2,128,128]{3,2,1,0:T(8,128)(2,1)S(1)}, bf16[2,2,128,128]{3,2,1,0:T(8,128)(2,1)S(1)}, bf16[2,2,128,128]{3,2,1,0:T(8,128)(2,1)S(1)}, bf16[2,2,1...) custom-call(s32[16]{0:T(128)S(1)} %get-tuple-element.31.places, ...), custom_call_target="tpu_custom_call" | custom-call | tf_op jit(solution)/shard_map/order/pallas_call | solution.py:420
  44.3 1.7 %collective-permute-start.8 = (bf16[4,2,128,128]{3,2,1,0:T(8,128)(2,1)S(1)}, bf16[4,2,128,128]{3,2,1,0:T(8,128)(2,1)S(1)}, u32[]{:S(2)}, u32[]{:S(2)}) collective-permute-start(bf16[4,2,128,128]{3,2,1,0:T(8,128)(2,1)S(1)} %get-tuple-element.37), channel_id=1, source_target_pairs={{0,2},{1,3},{2,4},{3,5},{4,6},{5,7},{6,8},{7,9},{8,10},{9,11},{10,... | collective-permute-start | bytes 786440 | tf_op jit(solution)/shard_map/right_over_z/ppermute | solution.py:430
  46.0 4.0 %collective-permute-start.9 = (bf16[4,2,128,128]{3,2,1,0:T(8,128)(2,1)S(1)}, bf16[4,2,128,128]{3,2,1,0:T(8,128)(2,1)S(1)}, u32[]{:S(2)}, u32[]{:S(2)}) collective-permute-start(bf16[4,2,128,128]{3,2,1,0:T(8,128)(2,1)S(1)} %get-tuple-element.38), channel_id=1, source_target_pairs={{0,14},{1,15},{2,0},{3,1},{4,2},{5,3},{6,4},{7,5},{8,6},{9,7},{10,... | collective-permute-start | bytes 786440 | tf_op jit(solution)/shard_map/right_over_z/ppermute | solution.py:430
  50.1 0.0 collective-permute-start.6
  50.1 3.6 %collective-permute-start.7 = (bf16[2,2,128,128]{3,2,1,0:T(8,128)(2,1)S(1)}, bf16[2,2,128,128]{3,2,1,0:T(8,128)(2,1)S(1)}, u32[]{:S(2)}, u32[]{:S(2)}) collective-permute-start(bf16[2,2,128,128]{3,2,1,0:T(8,128)(2,1)S(1)} %get-tuple-element.36), channel_id=1, source_target_pairs={{0,12},{1,13},{2,14},{3,15},{4,0},{5,1},{6,2},{7,3},{8,4},{9,5},{1... | collective-permute-start | bytes 393224 | tf_op jit(solution)/shard_map/right_over_z/ppermute | solution.py:430
  53.6 5.4 %collective-permute-done.6.refs_0_.rest_4_ = bf16[2,2,128,128]{3,2,1,0:T(8,128)(2,1)S(1)} collective-permute-done((bf16[2,2,128,128]{3,2,1,0:T(8,128)(2,1)S(1)}, bf16[2,2,128,128]{3,2,1,0:T(8,128)(2,1)S(1)}, u32[]{:S(2)}, u32[]{:S(2)}) %collective-permute-start.6) | collective-permute-done | bytes 131104 | tf_op jit(solution)/shard_map/right_over_z/ppermute | solution.py:430
  59.0 0.0 collective-permute-done.7.refs_1_.rest_5_
  59.0 0.0 collective-permute-done.8.refs_2_.rest_6_
  59.0 0.0 collective-permute-done.9.refs_3_.rest_7_
  59.0 0.5 right_over_core.1
  59.5 4.1 %collective-permute-start.10 = (bf16[6,2,128,128]{3,2,1,0:T(8,128)(2,1)S(1)}, bf16[6,2,128,128]{3,2,1,0:T(8,128)(2,1)S(1)}, u32[]{:S(2)}, u32[]{:S(2)}) collective-permute-start(bf16[6,2,128,128]{3,2,1,0:T(8,128)(2,1)S(1)} %right_over_core.1), channel_id=1, source_target_pairs={{0,1},{1,0},{2,3},{3,2},{4,5},{5,4},{6,7},{7,6},{8,9},{9,8},{10,11... | collective-permute-start | bytes 1179656 | tf_op jit(solution)/shard_map/right_over_core/ppermute | solution.py:440
  63.6 0.1 collective-permute-start.5
  63.7 1.4 %collective-permute-done.5.rest_3_ = bf16[2,2,128,128]{3,2,1,0:T(8,128)(2,1)S(1)} collective-permute-done((bf16[2,2,128,128]{3,2,1,0:T(8,128)(2,1)S(1)}, bf16[2,2,128,128]{3,2,1,0:T(8,128)(2,1)S(1)}, u32[]{:S(2)}, u32[]{:S(2)}) %collective-permute-start.5) | collective-permute-done | bytes 131104 | tf_op jit(solution)/shard_map/right_over_z/ppermute | solution.py:429
  65.2 0.0 collective-permute-done.10.rest_8_
  65.2 0.0 copy-done
  65.2 0.0 copy-done.5
  65.2 2.2 %first_image.1 = (bf16[2,128,128]{2,1,0:T(8,128)(2,1)S(1)}, f32[8,128]{1,0:T(8,128)S(1)}) custom-call(s32[16]{0:T(128)S(1)} %copy-done.6, s32[256]{0:T(256)S(1)} %copy-done.5, s32[256]{0:T(256)S(1)} %copy-done.4, bf16[16,128,128]{2,1,0:T(8,128)(2,1)S(1)} %copy-done, bf16[8,272,128]{2,1,0:T(8,128)(2,1)S(1)} %get-tuple-element.29.rest_0_, ...), custom_call_target="tpu_custom_call" | custom-call | tf_op jit(solution)/shard_map/first_image/pallas_call | solution.py:442
  67.4 3.9 %collective-permute-start.11 = (bf16[2,128,128]{2,1,0:T(8,128)(2,1)S(1)}, bf16[2,128,128]{2,1,0:T(8,128)(2,1)S(1)}, u32[]{:S(2)}, u32[]{:S(2)}) collective-permute-start(bf16[2,128,128]{2,1,0:T(8,128)(2,1)S(1)} %get-tuple-element.40.image_here), channel_id=1, source_target_pairs={{0,8},{1,9},{2,10},{3,11},{4,12},{5,13},{6,14},{7,15},{8,0},{9,1},... | collective-permute-start | bytes 196616 | tf_op jit(solution)/shard_map/swap_images/ppermute | solution.py:454
  71.3 3.2 %collective-permute-done.11.image_there = bf16[2,128,128]{2,1,0:T(8,128)(2,1)S(1)} collective-permute-done((bf16[2,128,128]{2,1,0:T(8,128)(2,1)S(1)}, bf16[2,128,128]{2,1,0:T(8,128)(2,1)S(1)}, u32[]{:S(2)}, u32[]{:S(2)}) %collective-permute-start.11) | collective-permute-done | bytes 65568 | tf_op jit(solution)/shard_map/swap_images/ppermute | solution.py:454
  74.5 2.2 %second_image.1 = bf16[16,32,128]{2,1,0:T(8,128)(2,1)S(1)} custom-call(s32[16]{0:T(128)S(1)} %copy-done.6, s32[256]{0:T(256)S(1)} %copy-done.5, s32[256]{0:T(256)S(1)} %copy-done.4, bf16[16,128,128]{2,1,0:T(8,128)(2,1)S(1)} %copy-done, f32[8,128]{1,0:T(8,128)S(1)} %get-tuple-element.39.ratios, bf16[2,128,128]{2,1,0:T(8,128)(2,1)S(1)} %get-tuple-element.40.image_here, ...), custom_call_target="tpu_custom_call" | custom-call | tf_op jit(solution)/shard_map/second_image/pallas_call | solution.py:456
  76.8 16.8 %all_to_all.15.pieces = bf16[16,32,128]{2,1,0:T(8,128)(2,1)S(1)} all-to-all(bf16[16,32,128]{2,1,0:T(8,128)(2,1)S(1)} %second_image.1), channel_id=1, replica_groups=mesh['sec'=16,'mpo'=16] {'mpo'}, dimensions={0} | all-to-all | bytes 262144 | tf_op jit(solution)/shard_map/rows_over_mpo/all_to_all | solution.py:465
  93.6 10.9 %all_to_all.16.shared = f32[16,8,128]{2,1,0:T(8,128)S(1)} all-to-all(f32[16,8,128]{2,1,0:T(8,128)S(1)} %broadcast_in_dim.2), channel_id=1, replica_groups=mesh['sec'=16,'mpo'=16] {'sec'}, dimensions={0} | all-to-all | bytes 131072 | tf_op jit(solution)/shard_map/numbers_over_sec/all_to_all | solution.py:468
  104.5 1.8 %finish.1 = (f32[16,8,128]{2,1,0:T(8,128)}, f32[16,8,128]{2,1,0:T(8,128)}, f32[3]{0:T(128)}) custom-call(s32[16]{0:T(128)S(1)} %copy-done.6, s32[256]{0:T(256)S(1)} %copy-done.5, s32[256]{0:T(256)S(1)} %copy-done.4, bf16[16,128,128]{2,1,0:T(8,128)(2,1)S(1)} %copy-done, bf16[16,32,128]{2,1,0:T(8,128)(2,1)S(1)} %all_to_all.15.pieces, ...), custom_call_target="tpu_custom_call" | custom-call | tf_op jit(solution)/shard_map/finish/pallas_call | solution.py:470
  (6 shorter events, 0.1 us)
Async XLA Ops:
  3.9 7.8 %copy-start.3 = (bf16[2,16,128,128]{3,2,1,0:T(8,128)(2,1)S(1)}, bf16[2,16,128,128]{3,2,1,0:T(8,128)(2,1)}, u32[]{:S(2)}) copy-start(bf16[2,16,128,128]{3,2,1,0:T(8,128)(2,1)} %left_env.1) | copy-start | bytes 3145732
  3.9 7.8 %copy-start.4 = (s32[256]{0:T(256)S(1)}, s32[256]{0:T(256)}, u32[]{:S(2)}) copy-start(s32[256]{0:T(256)} %right_sector.9) | copy-start | bytes 3076
  3.9 7.8 %copy-start.7 = (f32[2]{0:T(128)S(1)}, f32[2]{0:T(128)}, u32[]{:S(2)}) copy-start(f32[2]{0:T(128)} %weights.1) | copy-start | bytes 28
  3.9 38.2 %all-to-all-start = ((bf16[16,2,2,128,128]{4,3,2,1,0:T(8,128)(2,1)}), bf16[16,2,2,128,128]{4,3,2,1,0:T(8,128)(2,1)S(1)}, u32[]{:S(2)}, u32[]{:S(2)}) async-start(bf16[16,2,2,128,128]{4,3,2,1,0:T(8,128)(2,1)} %pack_right.1), calls=%async_computation | async-start | bytes 4194304 | tf_op jit(solution)/shard_map/right_over_sec/all_to_all | solution.py:391
  14.6 16.3 %collective-permute-start.2 = (bf16[1040,128]{1,0:T(8,128)(2,1)S(1)}, bf16[1040,128]{1,0:T(8,128)(2,1)S(1)}, u32[]{:S(2)}, u32[]{:S(2)}) collective-permute-start(bf16[1040,128]{1,0:T(8,128)(2,1)S(1)} %get-tuple-element.25), channel_id=1, source_target_pairs={{0,2},{1,3},{2,4},{3,5},{4,6},{5,7},{6,8},{7,9},{8,10},{9,11},{10,... | collective-permute-start | bytes 798728 | tf_op jit(solution)/shard_map/left_over_z/ppermute | solution.py:407
  16.3 14.5 %collective-permute-start.3 = (bf16[1040,128]{1,0:T(8,128)(2,1)S(1)}, bf16[1040,128]{1,0:T(8,128)(2,1)S(1)}, u32[]{:S(2)}, u32[]{:S(2)}) collective-permute-start(bf16[1040,128]{1,0:T(8,128)(2,1)S(1)} %get-tuple-element.26), channel_id=1, source_target_pairs={{0,14},{1,15},{2,0},{3,1},{4,2},{5,3},{6,4},{7,5},{8,6},{9,7},{10,... | collective-permute-start | bytes 798728 | tf_op jit(solution)/shard_map/left_over_z/ppermute | solution.py:407
  20.3 10.5 %collective-permute-start = (bf16[528,128]{1,0:T(8,128)(2,1)S(1)}, bf16[528,128]{1,0:T(8,128)(2,1)S(1)}, u32[]{:S(2)}, u32[]{:S(2)}) collective-permute-start(bf16[528,128]{1,0:T(8,128)(2,1)S(1)} %get-tuple-element.23), channel_id=1, source_target_pairs={{0,4},{1,5},{2,6},{3,7},{4,8},{5,9},{6,10},{7,11},{8,12},{9,13},{1... | collective-permute-start | bytes 405512 | tf_op jit(solution)/shard_map/left_over_z/ppermute | solution.py:407
  20.3 10.5 %collective-permute-start.1 = (bf16[528,128]{1,0:T(8,128)(2,1)S(1)}, bf16[528,128]{1,0:T(8,128)(2,1)S(1)}, u32[]{:S(2)}, u32[]{:S(2)}) collective-permute-start(bf16[528,128]{1,0:T(8,128)(2,1)S(1)} %get-tuple-element.24), channel_id=1, source_target_pairs={{0,12},{1,13},{2,14},{3,15},{4,0},{5,1},{6,2},{7,3},{8,4},{9,5},{1... | collective-permute-start | bytes 405512 | tf_op jit(solution)/shard_map/left_over_z/ppermute | solution.py:407
  30.9 34.3 %copy-start = (bf16[16,128,128]{2,1,0:T(8,128)(2,1)S(1)}, bf16[16,128,128]{2,1,0:T(8,128)(2,1)}, u32[]{:S(2)}) copy-start(bf16[16,128,128]{2,1,0:T(8,128)(2,1)} %vectors.5) | copy-start | bytes 1572868
  30.9 34.3 %copy-start.5 = (s32[256]{0:T(256)S(1)}, s32[256]{0:T(256)}, u32[]{:S(2)}) copy-start(s32[256]{0:T(256)} %right_size.5) | copy-start | bytes 3076
  30.9 34.3 %copy-start.6 = (s32[16]{0:T(128)S(1)}, s32[16]{0:T(128)}, u32[]{:S(2)}) copy-start(s32[16]{0:T(128)} %left_size.5) | copy-start | bytes 196
  32.4 3.7 %collective-permute-start.4 = (bf16[8,272,128]{2,1,0:T(8,128)(2,1)S(1)}, bf16[8,272,128]{2,1,0:T(8,128)(2,1)S(1)}, u32[]{:S(2)}, u32[]{:S(2)}) collective-permute-start(bf16[8,272,128]{2,1,0:T(8,128)(2,1)S(1)} %get-tuple-element.28), channel_id=1, source_target_pairs={{0,1},{1,0},{2,3},{3,2},{4,5},{5,4},{6,7},{7,6},{8,9},{9,8},{10,11... | collective-permute-start | bytes 1671176 | tf_op jit(solution)/shard_map/left_over_core/ppermute | solution.py:417
  36.0 0.8 copy-start.1
  42.2 23.0 %copy-start.2 = (bf16[8,272,128]{2,1,0:T(8,128)(2,1)S(1)}, bf16[8,272,128]{2,1,0:T(8,128)(2,1)}, u32[]{:S(2)}) copy-start(bf16[8,272,128]{2,1,0:T(8,128)(2,1)} %copy-done.1) | copy-start | bytes 1671172
  44.3 14.7 %collective-permute-start.8 = (bf16[4,2,128,128]{3,2,1,0:T(8,128)(2,1)S(1)}, bf16[4,2,128,128]{3,2,1,0:T(8,128)(2,1)S(1)}, u32[]{:S(2)}, u32[]{:S(2)}) collective-permute-start(bf16[4,2,128,128]{3,2,1,0:T(8,128)(2,1)S(1)} %get-tuple-element.37), channel_id=1, source_target_pairs={{0,2},{1,3},{2,4},{3,5},{4,6},{5,7},{6,8},{7,9},{8,10},{9,11},{10,... | collective-permute-start | bytes 786440 | tf_op jit(solution)/shard_map/right_over_z/ppermute | solution.py:430
  46.0 13.0 %collective-permute-start.9 = (bf16[4,2,128,128]{3,2,1,0:T(8,128)(2,1)S(1)}, bf16[4,2,128,128]{3,2,1,0:T(8,128)(2,1)S(1)}, u32[]{:S(2)}, u32[]{:S(2)}) collective-permute-start(bf16[4,2,128,128]{3,2,1,0:T(8,128)(2,1)S(1)} %get-tuple-element.38), channel_id=1, source_target_pairs={{0,14},{1,15},{2,0},{3,1},{4,2},{5,3},{6,4},{7,5},{8,6},{9,7},{10,... | collective-permute-start | bytes 786440 | tf_op jit(solution)/shard_map/right_over_z/ppermute | solution.py:430
  50.1 8.9 %collective-permute-start.6 = (bf16[2,2,128,128]{3,2,1,0:T(8,128)(2,1)S(1)}, bf16[2,2,128,128]{3,2,1,0:T(8,128)(2,1)S(1)}, u32[]{:S(2)}, u32[]{:S(2)}) collective-permute-start(bf16[2,2,128,128]{3,2,1,0:T(8,128)(2,1)S(1)} %get-tuple-element.35), channel_id=1, source_target_pairs={{0,4},{1,5},{2,6},{3,7},{4,8},{5,9},{6,10},{7,11},{8,12},{9,13},{1... | collective-permute-start | bytes 393224 | tf_op jit(solution)/shard_map/right_over_z/ppermute | solution.py:430
  50.1 8.9 %collective-permute-start.7 = (bf16[2,2,128,128]{3,2,1,0:T(8,128)(2,1)S(1)}, bf16[2,2,128,128]{3,2,1,0:T(8,128)(2,1)S(1)}, u32[]{:S(2)}, u32[]{:S(2)}) collective-permute-start(bf16[2,2,128,128]{3,2,1,0:T(8,128)(2,1)S(1)} %get-tuple-element.36), channel_id=1, source_target_pairs={{0,12},{1,13},{2,14},{3,15},{4,0},{5,1},{6,2},{7,3},{8,4},{9,5},{1... | collective-permute-start | bytes 393224 | tf_op jit(solution)/shard_map/right_over_z/ppermute | solution.py:430
  59.5 5.6 %collective-permute-start.10 = (bf16[6,2,128,128]{3,2,1,0:T(8,128)(2,1)S(1)}, bf16[6,2,128,128]{3,2,1,0:T(8,128)(2,1)S(1)}, u32[]{:S(2)}, u32[]{:S(2)}) collective-permute-start(bf16[6,2,128,128]{3,2,1,0:T(8,128)(2,1)S(1)} %right_over_core.1), channel_id=1, source_target_pairs={{0,1},{1,0},{2,3},{3,2},{4,5},{5,4},{6,7},{7,6},{8,9},{9,8},{10,11... | collective-permute-start | bytes 1179656 | tf_op jit(solution)/shard_map/right_over_core/ppermute | solution.py:440
  63.6 1.5 %collective-permute-start.5 = (bf16[2,2,128,128]{3,2,1,0:T(8,128)(2,1)S(1)}, bf16[2,2,128,128]{3,2,1,0:T(8,128)(2,1)S(1)}, u32[]{:S(2)}, u32[]{:S(2)}) collective-permute-start(bf16[2,2,128,128]{3,2,1,0:T(8,128)(2,1)S(1)} %get-tuple-element.34), channel_id=1, source_target_pairs={{0,1},{1,0},{2,3},{3,2},{4,5},{5,4},{6,7},{7,6},{8,9},{9,8},{10,11... | collective-permute-start | bytes 393224 | tf_op jit(solution)/shard_map/right_over_z/ppermute | solution.py:429
  67.4 7.1 %collective-permute-start.11 = (bf16[2,128,128]{2,1,0:T(8,128)(2,1)S(1)}, bf16[2,128,128]{2,1,0:T(8,128)(2,1)S(1)}, u32[]{:S(2)}, u32[]{:S(2)}) collective-permute-start(bf16[2,128,128]{2,1,0:T(8,128)(2,1)S(1)} %get-tuple-element.40.image_here), channel_id=1, source_target_pairs={{0,8},{1,9},{2,10},{3,11},{4,12},{5,13},{6,14},{7,15},{8,0},{9,1},... | collective-permute-start | bytes 196616 | tf_op jit(solution)/shard_map/swap_images/ppermute | solution.py:454

commit v9 on v8

--- a/solution.py
+++ b/solution.py
@@ -55,6 +55,7 @@
     base = sec * blocks
     picks = []
     copies = []
+    seconds = []
     for t in range(devices):
         first = jnp.int32(blocks * blocks)
         last = jnp.int32(0)
@@ -70,11 +71,17 @@
             load.wait()
         for ready in range(t + 1 if t == devices // 4 else 1):
             target = ready if t == devices // 4 else t
-            for k in range(SLOTS):
-                copies.append(pltpu.make_async_copy(stage.at[:, picks[target][k]], right_out.at[target, k], sem.at[1]))
-                copies[-1].start()
+            first, last = picks[target]
+            copy = pltpu.make_async_copy(stage.at[:, first], right_out.at[target, 0], sem.at[1])
+            copy.start()
+            copies.append(copy)
+            copy = pltpu.make_async_copy(stage.at[:, last], right_out.at[target, 1], sem.at[2])
+            pl.when(first != last)(copy.start)
+            seconds.append((first != last, copy))
     for copy in copies:
         copy.wait()
+    for there, copy in seconds:
+        pl.when(there)(copy.wait)
 
 
 def pack_left_kernel(weights, right_sector, left_env, *rest):
@@ -169,12 +176,12 @@
     return high, (x - high.astype(F32)).astype(BF16)
 
 
-def apply(block, kind, lefts, rights):
-    _, terms, width, _ = rights[-1].shape
+def apply(block, kind, lefts, rights, sides=(0, 1)):
+    _, terms, width, _ = rights[sides[0]].shape
     size = terms * width
     acc = jnp.zeros((width, width), F32)
     for index, place, other in parts_of(kind):
-        for side in range(2):
+        for side in sides:
             left = lefts[side][other, :size]
             scale = lefts[side][other, size:].astype(F32)
             if index == 0:
@@ -228,7 +235,15 @@
     return jnp.where(bottom > 0.0, top / jnp.where(bottom > 0.0, bottom, 1.0), 0.0)
 
 
-def first_kernel(left_size, right_size, right_sector, vectors, *rest):
+def begin_kernel(left_size, right_size, right_sector, vectors, *rest):
+    *blocks, out, vector, sem = rest
+    load_vectors(vectors, vector, sem)
+    for kind in range(2):
+        _, start = start_vector(kind, left_size, right_size, right_sector, vector)
+        out[kind] = apply(start.astype(BF16), kind, blocks[:1], (blocks[1], None, *blocks[2:]), (0,))
+
+
+def first_kernel(left_size, right_size, right_sector, vectors, begun, *rest):
     *blocks, out, ratios, vector, sem = rest
     load_vectors(vectors, vector, sem)
     row = lax.broadcasted_iota(jnp.int32, ratios.shape, 0)
@@ -237,7 +252,8 @@
         mask, start = start_vector(kind, left_size, right_size, right_sector, vector)
         norm, unit, length = scaled(start)
         scale = 1.0 / jnp.sqrt(norm / float(start.shape[0] * start.shape[1]) + 1e-06)
-        image = jnp.where(mask, apply(start.astype(BF16), kind, blocks[:2], blocks[2:]), 0.0) * scale
+        image = begun[kind] + apply(start.astype(BF16), kind, (None, blocks[0]), (None, *blocks[1:]), (1,))
+        image = jnp.where(mask, image, 0.0) * scale
         ratio = over(total(unit * image), length)
         out[kind] = (image - ratio * unit).astype(BF16)
         found = jnp.where(row == kind, ratio, found)
@@ -384,7 +400,7 @@
             out_shape=jax.ShapeDtypeStruct((devices, SLOTS, terms, width, width), BF16),
             in_specs=[scalars, anywhere],
             out_specs=anywhere,
-            scratch_shapes=[pltpu.VMEM(right_environment.shape, BF16), pltpu.SemaphoreType.DMA((2,))],
+            scratch_shapes=[pltpu.VMEM(right_environment.shape, BF16), pltpu.SemaphoreType.DMA((3,))],
             compiler_params=pltpu.CompilerParams(vmem_limit_bytes=60 * MIB),
         )(right_sector, right_environment)
     with jax.named_scope("right_over_sec"):
@@ -439,17 +455,26 @@
         )(*rights)
         rights = stayed + rights + [lax.ppermute(given, "mpo", cores)]
     with jax.named_scope("first_image"):
+        begun = pl.pallas_call(
+            begin_kernel,
+            out_shape=jax.ShapeDtypeStruct((2, width, width), F32),
+            in_specs=[scalars, scalars, scalars, anywhere] + [vmem] * (len(MOVES) + 1),
+            out_specs=vmem,
+            scratch_shapes=[pltpu.VMEM((2, width, width), BF16), pltpu.SemaphoreType.DMA],
+            compiler_params=pltpu.CompilerParams(vmem_limit_bytes=16 * MIB),
+            cost_estimate=pl.CostEstimate(flops=6 * width**3 * blocks, bytes_accessed=MIB, transcendentals=0),
+        )(left_size, right_size, right_sector, wavefunction, lefts[0], rights[0], *rights[2:-1])
         image_here, ratios = pl.pallas_call(
             first_kernel,
             out_shape=(
                 jax.ShapeDtypeStruct((2, width, width), BF16),
                 jax.ShapeDtypeStruct((8, width), F32),
             ),
-            in_specs=[scalars, scalars, scalars, anywhere] + [vmem] * (len(MOVES) + 4),
+            in_specs=[scalars, scalars, scalars, anywhere] + [vmem] * 4,
             out_specs=(vmem, vmem),
             scratch_shapes=[pltpu.VMEM((2, width, width), BF16), pltpu.SemaphoreType.DMA],
             compiler_params=pltpu.CompilerParams(vmem_limit_bytes=16 * MIB),
-        )(left_size, right_size, right_sector, wavefunction, *lefts, *rights)
+        )(left_size, right_size, right_sector, wavefunction, begun, lefts[1], rights[1], rights[-1])
     with jax.named_scope("swap_images"):
         image_there = lax.ppermute(image_here, "mpo", [(p, (p + chips) % layers) for p in range(layers)])
     with jax.named_scope("second_image"):

time: 107 us -> 106 us (level)
  waiting for transfers between devices: 23.8 us -> 21.2 us
  local copies, waits for them, and re-layouts: 0.85 us -> 2.07 us
    pallas_call x0 -> x1, Pallas kernels: none -> 1.48 us  [shards(): pl.pallas_call(begin_kernel, out_shape=jax.ShapeDtypeStruct((2, width, wi...]
    ppermute x1, waiting for transfers between devices: 1.44 us -> 0.01 us  [shards(): stayed = [rights[0], lax.ppermute(rights[1], 'mpo', cores)]]
    unnamed x16, local copies, waits for them, and re-layouts: 0.84 us -> 2.06 us
    all_to_all x1, waiting for transfers between devices: 5.3 us -> 4.09 us  [shards(): arrived = lax.all_to_all(right_out, 'sec', 0, 0, tiled=True)]
  transfers between devices with their start and end apart: 13 -> 13, of which waited for: 6 -> 5; matrix products, arithmetic and copies ran while one was open for 0% -> 0% of each run, Pallas kernels for 4% -> 6%
where the time goes in v9:
time: 106 us
  starting transfers between devices  36.4 us (34%)
  blocking collectives  27.7 us (26%)
  waiting for transfers between devices  21.2 us (20%)
  Pallas kernels  17.3 us (16%)
  local copies, waits for them, and re-layouts  2.07 us (2%)
    all_to_all x1, blocking collectives, shards(): pieces = lax.all_to_all(pieces, 'mpo', 0, 0, tiled=True)  16.8 us
    all_to_all x1, blocking collectives, shards(): lax.all_to_all(jnp.broadcast_to(line[None, None], (devices, 8, width)), '...  10.9 us
    ppermute x4, starting transfers between devices, shards(): lax.ppermute(left, 'mpo', route)  9.32 us
    ppermute x4, starting transfers between devices, shards(): lax.ppermute(right, 'mpo', route)  9.32 us
    all_to_all x1, starting transfers between devices, shards(): arrived = lax.all_to_all(right_out, 'sec', 0, 0, tiled=True)  7.6 us
    ppermute x4, waiting for transfers between devices, shards(): lax.ppermute(left, 'mpo', route)  6.94 us
    ppermute x4, waiting for transfers between devices, shards(): lax.ppermute(right, 'mpo', route)  5.37 us
    ppermute x1, starting transfers between devices, shards(): rights = stayed + rights + [lax.ppermute(given, 'mpo', cores)]  4.1 us
  transfers between devices with their start and end apart: 13, of which 5 were waited for; matrix products, arithmetic and copies ran while one was open for 0% of the time, Pallas kernels for 6%

profile of v9, /device:TPU:1, one launch (start us, length us, event | category | flops | bytes accessed | tf_op | source)
XLA Modules:
  0.0 105.6 jit_solution(5367249898352180190)
XLA Ops:
  0.6 2.9 %pack_right.1 = bf16[16,2,2,128,128]{4,3,2,1,0:T(8,128)(2,1)} custom-call(s32[256]{0:T(256)} %right_sector.11, bf16[2,16,128,128]{3,2,1,0:T(8,128)(2,1)} %right_env.1), custom_call_target="tpu_custom_call" | custom-call | tf_op jit(solution)/shard_map/pack_right/pallas_call | solution.py:398
  3.6 0.0 copy-start.4
  3.6 0.0 copy-start.7
  3.6 7.6 %all-to-all-start = ((bf16[16,2,2,128,128]{4,3,2,1,0:T(8,128)(2,1)}), bf16[16,2,2,128,128]{4,3,2,1,0:T(8,128)(2,1)S(1)}, u32[]{:S(2)}, u32[]{:S(2)}) async-start(bf16[16,2,2,128,128]{4,3,2,1,0:T(8,128)(2,1)} %pack_right.1), calls=%async_computation | async-start | bytes 4194304 | tf_op jit(solution)/shard_map/right_over_sec/all_to_all | solution.py:407
  11.2 0.0 copy-done.4
  11.2 0.0 copy-done.7
  11.2 0.0 copy-start.3
  11.2 1.2 %copy-done.3 = bf16[2,16,128,128]{3,2,1,0:T(8,128)(2,1)S(1)} copy-done((bf16[2,16,128,128]{3,2,1,0:T(8,128)(2,1)S(1)}, bf16[2,16,128,128]{3,2,1,0:T(8,128)(2,1)}, u32[]{:S(2)}) %copy-start.3) | copy-done | bytes 1048600
  12.5 2.9 %pack_left.1 = (bf16[1040,128]{1,0:T(8,128)(2,1)S(1)}, bf16[528,128]{1,0:T(8,128)(2,1)S(1)}, bf16[528,128]{1,0:T(8,128)(2,1)S(1)}, bf16[1040,128]{1,0:T(8,128)(2...) custom-call(f32[2]{0:T(128)S(1)} %copy-done.7, s32[256]{0:T(256)S(1)} %copy-done.4, ...), custom_call_target="tpu_custom_call" | custom-call | tf_op jit(solution)/shard_map/pack_left/pallas_call | solution.py:409
  15.4 1.7 %collective-permute-start.2 = (bf16[1040,128]{1,0:T(8,128)(2,1)S(1)}, bf16[1040,128]{1,0:T(8,128)(2,1)S(1)}, u32[]{:S(2)}, u32[]{:S(2)}) collective-permute-start(bf16[1040,128]{1,0:T(8,128)(2,1)S(1)} %get-tuple-element.25), channel_id=1, source_target_pairs={{0,2},{1,3},{2,4},{3,5},{4,6},{5,7},{6,8},{7,9},{8,10},{9,11},{10,... | collective-permute-start | bytes 798728 | tf_op jit(solution)/shard_map/left_over_z/ppermute | solution.py:423
  17.1 4.0 %collective-permute-start.3 = (bf16[1040,128]{1,0:T(8,128)(2,1)S(1)}, bf16[1040,128]{1,0:T(8,128)(2,1)S(1)}, u32[]{:S(2)}, u32[]{:S(2)}) collective-permute-start(bf16[1040,128]{1,0:T(8,128)(2,1)S(1)} %get-tuple-element.26), channel_id=1, source_target_pairs={{0,14},{1,15},{2,0},{3,1},{4,2},{5,3},{6,4},{7,5},{8,6},{9,7},{10,... | collective-permute-start | bytes 798728 | tf_op jit(solution)/shard_map/left_over_z/ppermute | solution.py:423
  21.1 0.0 collective-permute-start
  21.1 3.6 %collective-permute-start.1 = (bf16[528,128]{1,0:T(8,128)(2,1)S(1)}, bf16[528,128]{1,0:T(8,128)(2,1)S(1)}, u32[]{:S(2)}, u32[]{:S(2)}) collective-permute-start(bf16[528,128]{1,0:T(8,128)(2,1)S(1)} %get-tuple-element.24), channel_id=1, source_target_pairs={{0,12},{1,13},{2,14},{3,15},{4,0},{5,1},{6,2},{7,3},{8,4},{9,5},{1... | collective-permute-start | bytes 405512 | tf_op jit(solution)/shard_map/left_over_z/ppermute | solution.py:423
  24.7 6.9 %collective-permute-done.refs_1_ = bf16[528,128]{1,0:T(8,128)(2,1)S(1)} collective-permute-done((bf16[528,128]{1,0:T(8,128)(2,1)S(1)}, bf16[528,128]{1,0:T(8,128)(2,1)S(1)}, u32[]{:S(2)}, u32[]{:S(2)}) %collective-permute-start) | collective-permute-done | bytes 135200 | tf_op jit(solution)/shard_map/left_over_z/ppermute | solution.py:423
  31.6 0.0 collective-permute-done.1.refs_2_
  31.6 0.0 collective-permute-done.2.refs_3_
  31.6 0.0 collective-permute-done.3.refs_4_
  31.6 0.0 copy-start
  31.6 0.0 copy-start.5
  31.6 0.0 copy-start.6
  31.6 1.5 %left_over_core.1 = (bf16[8,272,128]{2,1,0:T(8,128)(2,1)S(1)}, bf16[8,272,128]{2,1,0:T(8,128)(2,1)S(1)}) custom-call(bf16[1040,128]{1,0:T(8,128)(2,1)S(1)} %get-tuple-element.22.refs_0_, bf16[528,128]{1,0:T(8,128)(2,1)S(1)} %collective-permute-done.refs_1_, bf16[528,128]{1,0:T(8,128)(2,1)S(1)} %collective-permute-done.1.refs_2_, ...), custom_call_target="tpu_custom_call" | custom-call | tf_op jit(solution)/shard_map/left_over_core/pallas_call | solution.py:425
  33.1 2.1 %collective-permute-start.4 = (bf16[8,272,128]{2,1,0:T(8,128)(2,1)S(1)}, bf16[8,272,128]{2,1,0:T(8,128)(2,1)S(1)}, u32[]{:S(2)}, u32[]{:S(2)}) collective-permute-start(bf16[8,272,128]{2,1,0:T(8,128)(2,1)S(1)} %get-tuple-element.28), channel_id=1, source_target_pairs={{0,1},{1,0},{2,3},{3,2},{4,5},{5,4},{6,7},{7,6},{8,9},{9,8},{10,11... | collective-permute-start | bytes 1671176 | tf_op jit(solution)/shard_map/left_over_core/ppermute | solution.py:433
  35.2 1.6 %collective-permute-done.4.rest_0_.rest_1_ = bf16[8,272,128]{2,1,0:T(8,128)(2,1)S(1)} collective-permute-done((bf16[8,272,128]{2,1,0:T(8,128)(2,1)S(1)}, bf16[8,272,128]{2,1,0:T(8,128)(2,1)S(1)}, u32[]{:S(2)}, u32[]{:S(2)}) %collective-permute-start.4) | collective-permute-done | bytes 557088 | tf_op jit(solution)/shard_map/left_over_core/ppermute | solution.py:433
  36.8 0.8 copy-done.1
  37.6 4.1 %all-to-all-done = bf16[16,2,2,128,128]{4,3,2,1,0:T(8,128)(2,1)S(1)} async-done(((bf16[16,2,2,128,128]{4,3,2,1,0:T(8,128)(2,1)}), bf16[16,2,2,128,128]{4,3,2,1,0:T(8,128)(2,1)S(1)}, u32[]{:S(2)}, u32[]{:S(2)}) %all-to-all-start) | async-done | bytes 2097184 | tf_op jit(solution)/shard_map/right_over_sec/all_to_all | solution.py:407
  41.7 2.2 %order.1 = (bf16[2,2,128,128]{3,2,1,0:T(8,128)(2,1)S(1)}, bf16[2,2,128,128]{3,2,1,0:T(8,128)(2,1)S(1)}, bf16[2,2,128,128]{3,2,1,0:T(8,128)(2,1)S(1)}, bf16[2,2,1...) custom-call(s32[16]{0:T(128)S(1)} %get-tuple-element.30.places, ...), custom_call_target="tpu_custom_call" | custom-call | tf_op jit(solution)/shard_map/order/pallas_call | solution.py:436
  43.9 1.7 %collective-permute-start.7 = (bf16[4,2,128,128]{3,2,1,0:T(8,128)(2,1)S(1)}, bf16[4,2,128,128]{3,2,1,0:T(8,128)(2,1)S(1)}, u32[]{:S(2)}, u32[]{:S(2)}) collective-permute-start(bf16[4,2,128,128]{3,2,1,0:T(8,128)(2,1)S(1)} %get-tuple-element.35), channel_id=1, source_target_pairs={{0,2},{1,3},{2,4},{3,5},{4,6},{5,7},{6,8},{7,9},{8,10},{9,11},{10,... | collective-permute-start | bytes 786440 | tf_op jit(solution)/shard_map/right_over_z/ppermute | solution.py:446
  45.6 4.0 %collective-permute-start.8 = (bf16[4,2,128,128]{3,2,1,0:T(8,128)(2,1)S(1)}, bf16[4,2,128,128]{3,2,1,0:T(8,128)(2,1)S(1)}, u32[]{:S(2)}, u32[]{:S(2)}) collective-permute-start(bf16[4,2,128,128]{3,2,1,0:T(8,128)(2,1)S(1)} %get-tuple-element.36), channel_id=1, source_target_pairs={{0,14},{1,15},{2,0},{3,1},{4,2},{5,3},{6,4},{7,5},{8,6},{9,7},{10,... | collective-permute-start | bytes 786440 | tf_op jit(solution)/shard_map/right_over_z/ppermute | solution.py:446
  49.6 0.0 collective-permute-start.5
  49.6 3.6 %collective-permute-start.6 = (bf16[2,2,128,128]{3,2,1,0:T(8,128)(2,1)S(1)}, bf16[2,2,128,128]{3,2,1,0:T(8,128)(2,1)S(1)}, u32[]{:S(2)}, u32[]{:S(2)}) collective-permute-start(bf16[2,2,128,128]{3,2,1,0:T(8,128)(2,1)S(1)} %get-tuple-element.34), channel_id=1, source_target_pairs={{0,12},{1,13},{2,14},{3,15},{4,0},{5,1},{6,2},{7,3},{8,4},{9,5},{1... | collective-permute-start | bytes 393224 | tf_op jit(solution)/shard_map/right_over_z/ppermute | solution.py:446
  53.2 5.4 %collective-permute-done.5.rest_2_.refs_0_.rest_4_ = bf16[2,2,128,128]{3,2,1,0:T(8,128)(2,1)S(1)} collective-permute-done((bf16[2,2,128,128]{3,2,1,0:T(8,128)(2,1)S(1)}, bf16[2,2,128,128]{3,2,1,0:T(8,128)(2,1)S(1)}, u32[]{:S(2)}, u32[]{:S(2)}) %collective-permute-start.5) | collective-permute-done | bytes 131104 | tf_op jit(solution)/shard_map/right_over_z/ppermute | solution.py:446
  58.6 0.0 collective-permute-done.6.rest_3_.refs_1_.rest_5_
  58.6 0.0 collective-permute-done.7.rest_4_.refs_2_.rest_6_
  58.6 0.0 collective-permute-done.8.rest_5_.refs_3_.rest_7_
  58.6 0.5 right_over_core.1
  59.1 4.1 %collective-permute-start.10 = (bf16[6,2,128,128]{3,2,1,0:T(8,128)(2,1)S(1)}, bf16[6,2,128,128]{3,2,1,0:T(8,128)(2,1)S(1)}, u32[]{:S(2)}, u32[]{:S(2)}) collective-permute-start(bf16[6,2,128,128]{3,2,1,0:T(8,128)(2,1)S(1)} %right_over_core.1), channel_id=1, source_target_pairs={{0,1},{1,0},{2,3},{3,2},{4,5},{5,4},{6,7},{7,6},{8,9},{9,8},{10,11... | collective-permute-start | bytes 1179656 | tf_op jit(solution)/shard_map/right_over_core/ppermute | solution.py:456
  63.2 0.1 collective-permute-start.9
  63.3 0.0 copy-done.5
  63.3 1.5 %first_image.2.begun = f32[2,128,128]{2,1,0:T(8,128)S(1)} custom-call(s32[16]{0:T(128)S(1)} %copy-done.6, s32[256]{0:T(256)S(1)} %copy-done.5, s32[256]{0:T(256)S(1)} %copy-done.4, bf16[16,128,128]{2,1,0:T(8,128)(2,1)S(1)} %copy-done, bf16[8,272,128]{2,1,0:T(8,128)(2,1)S(1)} %get-tuple-element.29.rest_0_, ...), custom_call_target="tpu_custom_call" | custom-call | flops 201326592 | bytes 1048576 | tf_op jit(solution)/shard_map/first_image/pallas_call | solution.py:458
  64.8 0.0 collective-permute-done.9.rest_1_.rest_3_
  64.8 0.0 collective-permute-done.10.rest_2_.rest_8_
  64.8 1.8 %first_image.3 = (bf16[2,128,128]{2,1,0:T(8,128)(2,1)S(1)}, f32[8,128]{1,0:T(8,128)S(1)}) custom-call(s32[16]{0:T(128)S(1)} %copy-done.6, s32[256]{0:T(256)S(1)} %copy-done.5, s32[256]{0:T(256)S(1)} %copy-done.4, bf16[16,128,128]{2,1,0:T(8,128)(2,1)S(1)} %copy-done, f32[2,128,128]{2,1,0:T(8,128)S(1)} %first_image.2.begun, ...), custom_call_target="tpu_custom_call" | custom-call | tf_op jit(solution)/shard_map/first_image/pallas_call | solution.py:467
  66.6 3.9 %collective-permute-start.11 = (bf16[2,128,128]{2,1,0:T(8,128)(2,1)S(1)}, bf16[2,128,128]{2,1,0:T(8,128)(2,1)S(1)}, u32[]{:S(2)}, u32[]{:S(2)}) collective-permute-start(bf16[2,128,128]{2,1,0:T(8,128)(2,1)S(1)} %get-tuple-element.40.image_here), channel_id=1, source_target_pairs={{0,8},{1,9},{2,10},{3,11},{4,12},{5,13},{6,14},{7,15},{8,0},{9,1},... | collective-permute-start | bytes 196616 | tf_op jit(solution)/shard_map/swap_images/ppermute | solution.py:479
  70.5 3.2 %collective-permute-done.11.image_there = bf16[2,128,128]{2,1,0:T(8,128)(2,1)S(1)} collective-permute-done((bf16[2,128,128]{2,1,0:T(8,128)(2,1)S(1)}, bf16[2,128,128]{2,1,0:T(8,128)(2,1)S(1)}, u32[]{:S(2)}, u32[]{:S(2)}) %collective-permute-start.11) | collective-permute-done | bytes 65568 | tf_op jit(solution)/shard_map/swap_images/ppermute | solution.py:479
  73.8 2.2 %second_image.1 = bf16[16,32,128]{2,1,0:T(8,128)(2,1)S(1)} custom-call(s32[16]{0:T(128)S(1)} %copy-done.6, s32[256]{0:T(256)S(1)} %copy-done.5, s32[256]{0:T(256)S(1)} %copy-done.4, bf16[16,128,128]{2,1,0:T(8,128)(2,1)S(1)} %copy-done, f32[8,128]{1,0:T(8,128)S(1)} %get-tuple-element.39.ratios, bf16[2,128,128]{2,1,0:T(8,128)(2,1)S(1)} %get-tuple-element.40.image_here, ...), custom_call_target="tpu_custom_call" | custom-call | tf_op jit(solution)/shard_map/second_image/pallas_call | solution.py:481
  76.0 16.8 %all_to_all.15.pieces = bf16[16,32,128]{2,1,0:T(8,128)(2,1)S(1)} all-to-all(bf16[16,32,128]{2,1,0:T(8,128)(2,1)S(1)} %second_image.1), channel_id=1, replica_groups=mesh['sec'=16,'mpo'=16] {'mpo'}, dimensions={0} | all-to-all | bytes 262144 | tf_op jit(solution)/shard_map/rows_over_mpo/all_to_all | solution.py:490
  92.8 10.9 %all_to_all.16.shared = f32[16,8,128]{2,1,0:T(8,128)S(1)} all-to-all(f32[16,8,128]{2,1,0:T(8,128)S(1)} %broadcast_in_dim.2), channel_id=1, replica_groups=mesh['sec'=16,'mpo'=16] {'sec'}, dimensions={0} | all-to-all | bytes 131072 | tf_op jit(solution)/shard_map/numbers_over_sec/all_to_all | solution.py:493
  103.7 1.8 %finish.1 = (f32[16,8,128]{2,1,0:T(8,128)}, f32[16,8,128]{2,1,0:T(8,128)}, f32[3]{0:T(128)}) custom-call(s32[16]{0:T(128)S(1)} %copy-done.6, s32[256]{0:T(256)S(1)} %copy-done.5, s32[256]{0:T(256)S(1)} %copy-done.4, bf16[16,128,128]{2,1,0:T(8,128)(2,1)S(1)} %copy-done, bf16[16,32,128]{2,1,0:T(8,128)(2,1)S(1)} %all_to_all.15.pieces, ...), custom_call_target="tpu_custom_call" | custom-call | tf_op jit(solution)/shard_map/finish/pallas_call | solution.py:495
  (7 shorter events, 0.1 us)
Async XLA Ops:
  3.6 7.6 %copy-start.4 = (s32[256]{0:T(256)S(1)}, s32[256]{0:T(256)}, u32[]{:S(2)}) copy-start(s32[256]{0:T(256)} %right_sector.11) | copy-start | bytes 3076
  3.6 7.6 %copy-start.7 = (f32[2]{0:T(128)S(1)}, f32[2]{0:T(128)}, u32[]{:S(2)}) copy-start(f32[2]{0:T(128)} %weights.1) | copy-start | bytes 28
  3.6 38.1 %all-to-all-start = ((bf16[16,2,2,128,128]{4,3,2,1,0:T(8,128)(2,1)}), bf16[16,2,2,128,128]{4,3,2,1,0:T(8,128)(2,1)S(1)}, u32[]{:S(2)}, u32[]{:S(2)}) async-start(bf16[16,2,2,128,128]{4,3,2,1,0:T(8,128)(2,1)} %pack_right.1), calls=%async_computation | async-start | bytes 4194304 | tf_op jit(solution)/shard_map/right_over_sec/all_to_all | solution.py:407
  11.2 1.2 %copy-start.3 = (bf16[2,16,128,128]{3,2,1,0:T(8,128)(2,1)S(1)}, bf16[2,16,128,128]{3,2,1,0:T(8,128)(2,1)}, u32[]{:S(2)}) copy-start(bf16[2,16,128,128]{3,2,1,0:T(8,128)(2,1)} %left_env.1) | copy-start | bytes 3145732
  15.4 16.3 %collective-permute-start.2 = (bf16[1040,128]{1,0:T(8,128)(2,1)S(1)}, bf16[1040,128]{1,0:T(8,128)(2,1)S(1)}, u32[]{:S(2)}, u32[]{:S(2)}) collective-permute-start(bf16[1040,128]{1,0:T(8,128)(2,1)S(1)} %get-tuple-element.25), channel_id=1, source_target_pairs={{0,2},{1,3},{2,4},{3,5},{4,6},{5,7},{6,8},{7,9},{8,10},{9,11},{10,... | collective-permute-start | bytes 798728 | tf_op jit(solution)/shard_map/left_over_z/ppermute | solution.py:423
  17.1 14.5 %collective-permute-start.3 = (bf16[1040,128]{1,0:T(8,128)(2,1)S(1)}, bf16[1040,128]{1,0:T(8,128)(2,1)S(1)}, u32[]{:S(2)}, u32[]{:S(2)}) collective-permute-start(bf16[1040,128]{1,0:T(8,128)(2,1)S(1)} %get-tuple-element.26), channel_id=1, source_target_pairs={{0,14},{1,15},{2,0},{3,1},{4,2},{5,3},{6,4},{7,5},{8,6},{9,7},{10,... | collective-permute-start | bytes 798728 | tf_op jit(solution)/shard_map/left_over_z/ppermute | solution.py:423
  21.1 10.5 %collective-permute-start = (bf16[528,128]{1,0:T(8,128)(2,1)S(1)}, bf16[528,128]{1,0:T(8,128)(2,1)S(1)}, u32[]{:S(2)}, u32[]{:S(2)}) collective-permute-start(bf16[528,128]{1,0:T(8,128)(2,1)S(1)} %get-tuple-element.23), channel_id=1, source_target_pairs={{0,4},{1,5},{2,6},{3,7},{4,8},{5,9},{6,10},{7,11},{8,12},{9,13},{1... | collective-permute-start | bytes 405512 | tf_op jit(solution)/shard_map/left_over_z/ppermute | solution.py:423
  21.1 10.5 %collective-permute-start.1 = (bf16[528,128]{1,0:T(8,128)(2,1)S(1)}, bf16[528,128]{1,0:T(8,128)(2,1)S(1)}, u32[]{:S(2)}, u32[]{:S(2)}) collective-permute-start(bf16[528,128]{1,0:T(8,128)(2,1)S(1)} %get-tuple-element.24), channel_id=1, source_target_pairs={{0,12},{1,13},{2,14},{3,15},{4,0},{5,1},{6,2},{7,3},{8,4},{9,5},{1... | collective-permute-start | bytes 405512 | tf_op jit(solution)/shard_map/left_over_z/ppermute | solution.py:423
  31.6 31.7 %copy-start = (bf16[16,128,128]{2,1,0:T(8,128)(2,1)S(1)}, bf16[16,128,128]{2,1,0:T(8,128)(2,1)}, u32[]{:S(2)}) copy-start(bf16[16,128,128]{2,1,0:T(8,128)(2,1)} %vectors.7) | copy-start | bytes 1572868
  31.6 31.7 %copy-start.5 = (s32[256]{0:T(256)S(1)}, s32[256]{0:T(256)}, u32[]{:S(2)}) copy-start(s32[256]{0:T(256)} %right_size.7) | copy-start | bytes 3076
  31.6 31.7 %copy-start.6 = (s32[16]{0:T(128)S(1)}, s32[16]{0:T(128)}, u32[]{:S(2)}) copy-start(s32[16]{0:T(128)} %left_size.7) | copy-start | bytes 196
  33.1 3.7 %collective-permute-start.4 = (bf16[8,272,128]{2,1,0:T(8,128)(2,1)S(1)}, bf16[8,272,128]{2,1,0:T(8,128)(2,1)S(1)}, u32[]{:S(2)}, u32[]{:S(2)}) collective-permute-start(bf16[8,272,128]{2,1,0:T(8,128)(2,1)S(1)} %get-tuple-element.28), channel_id=1, source_target_pairs={{0,1},{1,0},{2,3},{3,2},{4,5},{5,4},{6,7},{7,6},{8,9},{9,8},{10,11... | collective-permute-start | bytes 1671176 | tf_op jit(solution)/shard_map/left_over_core/ppermute | solution.py:433
  36.8 0.8 copy-start.1
  43.9 20.9 %copy-start.2 = (bf16[8,272,128]{2,1,0:T(8,128)(2,1)S(1)}, bf16[8,272,128]{2,1,0:T(8,128)(2,1)}, u32[]{:S(2)}) copy-start(bf16[8,272,128]{2,1,0:T(8,128)(2,1)} %copy-done.1) | copy-start | bytes 1671172
  43.9 14.7 %collective-permute-start.7 = (bf16[4,2,128,128]{3,2,1,0:T(8,128)(2,1)S(1)}, bf16[4,2,128,128]{3,2,1,0:T(8,128)(2,1)S(1)}, u32[]{:S(2)}, u32[]{:S(2)}) collective-permute-start(bf16[4,2,128,128]{3,2,1,0:T(8,128)(2,1)S(1)} %get-tuple-element.35), channel_id=1, source_target_pairs={{0,2},{1,3},{2,4},{3,5},{4,6},{5,7},{6,8},{7,9},{8,10},{9,11},{10,... | collective-permute-start | bytes 786440 | tf_op jit(solution)/shard_map/right_over_z/ppermute | solution.py:446
  45.6 13.0 %collective-permute-start.8 = (bf16[4,2,128,128]{3,2,1,0:T(8,128)(2,1)S(1)}, bf16[4,2,128,128]{3,2,1,0:T(8,128)(2,1)S(1)}, u32[]{:S(2)}, u32[]{:S(2)}) collective-permute-start(bf16[4,2,128,128]{3,2,1,0:T(8,128)(2,1)S(1)} %get-tuple-element.36), channel_id=1, source_target_pairs={{0,14},{1,15},{2,0},{3,1},{4,2},{5,3},{6,4},{7,5},{8,6},{9,7},{10,... | collective-permute-start | bytes 786440 | tf_op jit(solution)/shard_map/right_over_z/ppermute | solution.py:446
  49.6 8.9 %collective-permute-start.5 = (bf16[2,2,128,128]{3,2,1,0:T(8,128)(2,1)S(1)}, bf16[2,2,128,128]{3,2,1,0:T(8,128)(2,1)S(1)}, u32[]{:S(2)}, u32[]{:S(2)}) collective-permute-start(bf16[2,2,128,128]{3,2,1,0:T(8,128)(2,1)S(1)} %get-tuple-element.33), channel_id=1, source_target_pairs={{0,4},{1,5},{2,6},{3,7},{4,8},{5,9},{6,10},{7,11},{8,12},{9,13},{1... | collective-permute-start | bytes 393224 | tf_op jit(solution)/shard_map/right_over_z/ppermute | solution.py:446
  49.6 8.9 %collective-permute-start.6 = (bf16[2,2,128,128]{3,2,1,0:T(8,128)(2,1)S(1)}, bf16[2,2,128,128]{3,2,1,0:T(8,128)(2,1)S(1)}, u32[]{:S(2)}, u32[]{:S(2)}) collective-permute-start(bf16[2,2,128,128]{3,2,1,0:T(8,128)(2,1)S(1)} %get-tuple-element.34), channel_id=1, source_target_pairs={{0,12},{1,13},{2,14},{3,15},{4,0},{5,1},{6,2},{7,3},{8,4},{9,5},{1... | collective-permute-start | bytes 393224 | tf_op jit(solution)/shard_map/right_over_z/ppermute | solution.py:446
  59.1 5.7 %collective-permute-start.10 = (bf16[6,2,128,128]{3,2,1,0:T(8,128)(2,1)S(1)}, bf16[6,2,128,128]{3,2,1,0:T(8,128)(2,1)S(1)}, u32[]{:S(2)}, u32[]{:S(2)}) collective-permute-start(bf16[6,2,128,128]{3,2,1,0:T(8,128)(2,1)S(1)} %right_over_core.1), channel_id=1, source_target_pairs={{0,1},{1,0},{2,3},{3,2},{4,5},{5,4},{6,7},{7,6},{8,9},{9,8},{10,11... | collective-permute-start | bytes 1179656 | tf_op jit(solution)/shard_map/right_over_core/ppermute | solution.py:456
  63.2 1.6 %collective-permute-start.9 = (bf16[2,2,128,128]{3,2,1,0:T(8,128)(2,1)S(1)}, bf16[2,2,128,128]{3,2,1,0:T(8,128)(2,1)S(1)}, u32[]{:S(2)}, u32[]{:S(2)}) collective-permute-start(bf16[2,2,128,128]{3,2,1,0:T(8,128)(2,1)S(1)} %get-tuple-element.38), channel_id=1, source_target_pairs={{0,1},{1,0},{2,3},{3,2},{4,5},{5,4},{6,7},{7,6},{8,9},{9,8},{10,11... | collective-permute-start | bytes 393224 | tf_op jit(solution)/shard_map/right_over_z/ppermute | solution.py:445
  66.6 7.1 %collective-permute-start.11 = (bf16[2,128,128]{2,1,0:T(8,128)(2,1)S(1)}, bf16[2,128,128]{2,1,0:T(8,128)(2,1)S(1)}, u32[]{:S(2)}, u32[]{:S(2)}) collective-permute-start(bf16[2,128,128]{2,1,0:T(8,128)(2,1)S(1)} %get-tuple-element.40.image_here), channel_id=1, source_target_pairs={{0,8},{1,9},{2,10},{3,11},{4,12},{5,13},{6,14},{7,15},{8,0},{9,1},... | collective-permute-start | bytes 196616 | tf_op jit(solution)/shard_map/swap_images/ppermute | solution.py:479

commit v10 on v9

--- a/solution.py
+++ b/solution.py
@@ -330,8 +330,8 @@
     lead = lane == 0
     norm = jnp.where(lead, field(stats, 0), 0.0)
     ratio, square, on_rest, on_unit, skew = (field(stats, j) for j in range(1, 6))
+    mean = norm / cells + 1e-06
     gain = 1.0 / jnp.sqrt(total(norm) / entries + 1e-06)
-    mean = norm / cells + 1e-06
     weight = jnp.where(lead, (gain * gain) * mean, 0.0)
     length = norm / mean
     overlap = ratio * length + skew
@@ -358,7 +358,7 @@
         own_rows = group[:rows]
         for j in range(1, groups):
             own_rows = jnp.where(part % groups == j, group[j * rows : (j + 1) * rows], own_rows)
-        unit = jnp.where(mask, own_rows, 0.0) / root
+        unit = jnp.where(mask, own_rows, 0.0) * (1.0 / root)
         sent = [pieces[owner].astype(F32) for owner in (lower, higher)]
         rest = sent[kind][:rows]
         after_rows = slice((1 + kind) * rows, (2 + kind) * rows)

time: 106 us -> 106 us (level)
  no operation moved by 1% of the time
where the time goes in v10:
time: 106 us
  starting transfers between devices  36.5 us (34%)
  blocking collectives  27.7 us (26%)
  waiting for transfers between devices  21.2 us (20%)
  Pallas kernels  17.3 us (16%)
  local copies, waits for them, and re-layouts  2.07 us (2%)
    all_to_all x1, blocking collectives, shards(): pieces = lax.all_to_all(pieces, 'mpo', 0, 0, tiled=True)  16.8 us
    all_to_all x1, blocking collectives, shards(): lax.all_to_all(jnp.broadcast_to(line[None, None], (devices, 8, width)), '...  10.9 us
    ppermute x4, starting transfers between devices, shards(): lax.ppermute(left, 'mpo', route)  9.32 us
    ppermute x4, starting transfers between devices, shards(): lax.ppermute(right, 'mpo', route)  9.32 us
    all_to_all x1, starting transfers between devices, shards(): arrived = lax.all_to_all(right_out, 'sec', 0, 0, tiled=True)  7.61 us
    ppermute x4, waiting for transfers between devices, shards(): lax.ppermute(left, 'mpo', route)  6.94 us
    ppermute x4, waiting for transfers between devices, shards(): lax.ppermute(right, 'mpo', route)  5.37 us
    ppermute x1, starting transfers between devices, shards(): rights = stayed + rights + [lax.ppermute(given, 'mpo', cores)]  4.1 us
  transfers between devices with their start and end apart: 13, of which 5 were waited for; matrix products, arithmetic and copies ran while one was open for 0% of the time, Pallas kernels for 6%

profile of v10, /device:TPU:1, one launch (start us, length us, event | category | flops | bytes accessed | tf_op | source)
XLA Modules:
  0.0 105.6 jit_solution(293661826495635702)
XLA Ops:
  0.6 2.9 %pack_right.1 = bf16[16,2,2,128,128]{4,3,2,1,0:T(8,128)(2,1)} custom-call(s32[256]{0:T(256)} %right_sector.11, bf16[2,16,128,128]{3,2,1,0:T(8,128)(2,1)} %right_env.1), custom_call_target="tpu_custom_call" | custom-call | tf_op jit(solution)/shard_map/pack_right/pallas_call | solution.py:398
  3.6 0.0 copy-start.4
  3.6 0.0 copy-start.7
  3.6 7.6 %all-to-all-start = ((bf16[16,2,2,128,128]{4,3,2,1,0:T(8,128)(2,1)}), bf16[16,2,2,128,128]{4,3,2,1,0:T(8,128)(2,1)S(1)}, u32[]{:S(2)}, u32[]{:S(2)}) async-start(bf16[16,2,2,128,128]{4,3,2,1,0:T(8,128)(2,1)} %pack_right.1), calls=%async_computation | async-start | bytes 4194304 | tf_op jit(solution)/shard_map/right_over_sec/all_to_all | solution.py:407
  11.2 0.0 copy-done.4
  11.2 0.0 copy-start.3
  11.3 1.2 %copy-done.3 = bf16[2,16,128,128]{3,2,1,0:T(8,128)(2,1)S(1)} copy-done((bf16[2,16,128,128]{3,2,1,0:T(8,128)(2,1)S(1)}, bf16[2,16,128,128]{3,2,1,0:T(8,128)(2,1)}, u32[]{:S(2)}) %copy-start.3) | copy-done | bytes 1048600
  12.5 2.9 %pack_left.1 = (bf16[1040,128]{1,0:T(8,128)(2,1)S(1)}, bf16[528,128]{1,0:T(8,128)(2,1)S(1)}, bf16[528,128]{1,0:T(8,128)(2,1)S(1)}, bf16[1040,128]{1,0:T(8,128)(2...) custom-call(f32[2]{0:T(128)S(1)} %copy-done.7, s32[256]{0:T(256)S(1)} %copy-done.4, ...), custom_call_target="tpu_custom_call" | custom-call | tf_op jit(solution)/shard_map/pack_left/pallas_call | solution.py:409
  15.4 1.7 %collective-permute-start.2 = (bf16[1040,128]{1,0:T(8,128)(2,1)S(1)}, bf16[1040,128]{1,0:T(8,128)(2,1)S(1)}, u32[]{:S(2)}, u32[]{:S(2)}) collective-permute-start(bf16[1040,128]{1,0:T(8,128)(2,1)S(1)} %get-tuple-element.25), channel_id=1, source_target_pairs={{0,2},{1,3},{2,4},{3,5},{4,6},{5,7},{6,8},{7,9},{8,10},{9,11},{10,... | collective-permute-start | bytes 798728 | tf_op jit(solution)/shard_map/left_over_z/ppermute | solution.py:423
  17.1 4.0 %collective-permute-start.3 = (bf16[1040,128]{1,0:T(8,128)(2,1)S(1)}, bf16[1040,128]{1,0:T(8,128)(2,1)S(1)}, u32[]{:S(2)}, u32[]{:S(2)}) collective-permute-start(bf16[1040,128]{1,0:T(8,128)(2,1)S(1)} %get-tuple-element.26), channel_id=1, source_target_pairs={{0,14},{1,15},{2,0},{3,1},{4,2},{5,3},{6,4},{7,5},{8,6},{9,7},{10,... | collective-permute-start | bytes 798728 | tf_op jit(solution)/shard_map/left_over_z/ppermute | solution.py:423
  21.1 0.0 collective-permute-start
  21.1 3.6 %collective-permute-start.1 = (bf16[528,128]{1,0:T(8,128)(2,1)S(1)}, bf16[528,128]{1,0:T(8,128)(2,1)S(1)}, u32[]{:S(2)}, u32[]{:S(2)}) collective-permute-start(bf16[528,128]{1,0:T(8,128)(2,1)S(1)} %get-tuple-element.24), channel_id=1, source_target_pairs={{0,12},{1,13},{2,14},{3,15},{4,0},{5,1},{6,2},{7,3},{8,4},{9,5},{1... | collective-permute-start | bytes 405512 | tf_op jit(solution)/shard_map/left_over_z/ppermute | solution.py:423
  24.7 6.9 %collective-permute-done.refs_1_ = bf16[528,128]{1,0:T(8,128)(2,1)S(1)} collective-permute-done((bf16[528,128]{1,0:T(8,128)(2,1)S(1)}, bf16[528,128]{1,0:T(8,128)(2,1)S(1)}, u32[]{:S(2)}, u32[]{:S(2)}) %collective-permute-start) | collective-permute-done | bytes 135200 | tf_op jit(solution)/shard_map/left_over_z/ppermute | solution.py:423
  31.6 0.0 collective-permute-done.1.refs_2_
  31.6 0.0 collective-permute-done.2.refs_3_
  31.6 0.0 collective-permute-done.3.refs_4_
  31.6 0.0 copy-start
  31.6 0.0 copy-start.5
  31.7 0.0 copy-start.6
  31.7 1.5 %left_over_core.1 = (bf16[8,272,128]{2,1,0:T(8,128)(2,1)S(1)}, bf16[8,272,128]{2,1,0:T(8,128)(2,1)S(1)}) custom-call(bf16[1040,128]{1,0:T(8,128)(2,1)S(1)} %get-tuple-element.22.refs_0_, bf16[528,128]{1,0:T(8,128)(2,1)S(1)} %collective-permute-done.refs_1_, bf16[528,128]{1,0:T(8,128)(2,1)S(1)} %collective-permute-done.1.refs_2_, ...), custom_call_target="tpu_custom_call" | custom-call | tf_op jit(solution)/shard_map/left_over_core/pallas_call | solution.py:425
  33.1 2.1 %collective-permute-start.4 = (bf16[8,272,128]{2,1,0:T(8,128)(2,1)S(1)}, bf16[8,272,128]{2,1,0:T(8,128)(2,1)S(1)}, u32[]{:S(2)}, u32[]{:S(2)}) collective-permute-start(bf16[8,272,128]{2,1,0:T(8,128)(2,1)S(1)} %get-tuple-element.28), channel_id=1, source_target_pairs={{0,1},{1,0},{2,3},{3,2},{4,5},{5,4},{6,7},{7,6},{8,9},{9,8},{10,11... | collective-permute-start | bytes 1671176 | tf_op jit(solution)/shard_map/left_over_core/ppermute | solution.py:433
  35.2 1.6 %collective-permute-done.4.rest_0_.rest_1_ = bf16[8,272,128]{2,1,0:T(8,128)(2,1)S(1)} collective-permute-done((bf16[8,272,128]{2,1,0:T(8,128)(2,1)S(1)}, bf16[8,272,128]{2,1,0:T(8,128)(2,1)S(1)}, u32[]{:S(2)}, u32[]{:S(2)}) %collective-permute-start.4) | collective-permute-done | bytes 557088 | tf_op jit(solution)/shard_map/left_over_core/ppermute | solution.py:433
  36.8 0.8 copy-done.1
  37.6 4.1 %all-to-all-done = bf16[16,2,2,128,128]{4,3,2,1,0:T(8,128)(2,1)S(1)} async-done(((bf16[16,2,2,128,128]{4,3,2,1,0:T(8,128)(2,1)}), bf16[16,2,2,128,128]{4,3,2,1,0:T(8,128)(2,1)S(1)}, u32[]{:S(2)}, u32[]{:S(2)}) %all-to-all-start) | async-done | bytes 2097184 | tf_op jit(solution)/shard_map/right_over_sec/all_to_all | solution.py:407
  41.7 2.2 %order.1 = (bf16[2,2,128,128]{3,2,1,0:T(8,128)(2,1)S(1)}, bf16[2,2,128,128]{3,2,1,0:T(8,128)(2,1)S(1)}, bf16[2,2,128,128]{3,2,1,0:T(8,128)(2,1)S(1)}, bf16[2,2,1...) custom-call(s32[16]{0:T(128)S(1)} %get-tuple-element.30.places, ...), custom_call_target="tpu_custom_call" | custom-call | tf_op jit(solution)/shard_map/order/pallas_call | solution.py:436
  43.9 1.7 %collective-permute-start.7 = (bf16[4,2,128,128]{3,2,1,0:T(8,128)(2,1)S(1)}, bf16[4,2,128,128]{3,2,1,0:T(8,128)(2,1)S(1)}, u32[]{:S(2)}, u32[]{:S(2)}) collective-permute-start(bf16[4,2,128,128]{3,2,1,0:T(8,128)(2,1)S(1)} %get-tuple-element.35), channel_id=1, source_target_pairs={{0,2},{1,3},{2,4},{3,5},{4,6},{5,7},{6,8},{7,9},{8,10},{9,11},{10,... | collective-permute-start | bytes 786440 | tf_op jit(solution)/shard_map/right_over_z/ppermute | solution.py:446
  45.6 4.0 %collective-permute-start.8 = (bf16[4,2,128,128]{3,2,1,0:T(8,128)(2,1)S(1)}, bf16[4,2,128,128]{3,2,1,0:T(8,128)(2,1)S(1)}, u32[]{:S(2)}, u32[]{:S(2)}) collective-permute-start(bf16[4,2,128,128]{3,2,1,0:T(8,128)(2,1)S(1)} %get-tuple-element.36), channel_id=1, source_target_pairs={{0,14},{1,15},{2,0},{3,1},{4,2},{5,3},{6,4},{7,5},{8,6},{9,7},{10,... | collective-permute-start | bytes 786440 | tf_op jit(solution)/shard_map/right_over_z/ppermute | solution.py:446
  49.6 0.0 collective-permute-start.5
  49.6 3.6 %collective-permute-start.6 = (bf16[2,2,128,128]{3,2,1,0:T(8,128)(2,1)S(1)}, bf16[2,2,128,128]{3,2,1,0:T(8,128)(2,1)S(1)}, u32[]{:S(2)}, u32[]{:S(2)}) collective-permute-start(bf16[2,2,128,128]{3,2,1,0:T(8,128)(2,1)S(1)} %get-tuple-element.34), channel_id=1, source_target_pairs={{0,12},{1,13},{2,14},{3,15},{4,0},{5,1},{6,2},{7,3},{8,4},{9,5},{1... | collective-permute-start | bytes 393224 | tf_op jit(solution)/shard_map/right_over_z/ppermute | solution.py:446
  53.2 5.4 %collective-permute-done.5.rest_2_.refs_0_.rest_4_ = bf16[2,2,128,128]{3,2,1,0:T(8,128)(2,1)S(1)} collective-permute-done((bf16[2,2,128,128]{3,2,1,0:T(8,128)(2,1)S(1)}, bf16[2,2,128,128]{3,2,1,0:T(8,128)(2,1)S(1)}, u32[]{:S(2)}, u32[]{:S(2)}) %collective-permute-start.5) | collective-permute-done | bytes 131104 | tf_op jit(solution)/shard_map/right_over_z/ppermute | solution.py:446
  58.6 0.0 collective-permute-done.6.rest_3_.refs_1_.rest_5_
  58.6 0.0 collective-permute-done.7.rest_4_.refs_2_.rest_6_
  58.6 0.0 collective-permute-done.8.rest_5_.refs_3_.rest_7_
  58.6 0.5 right_over_core.1
  59.1 4.1 %collective-permute-start.10 = (bf16[6,2,128,128]{3,2,1,0:T(8,128)(2,1)S(1)}, bf16[6,2,128,128]{3,2,1,0:T(8,128)(2,1)S(1)}, u32[]{:S(2)}, u32[]{:S(2)}) collective-permute-start(bf16[6,2,128,128]{3,2,1,0:T(8,128)(2,1)S(1)} %right_over_core.1), channel_id=1, source_target_pairs={{0,1},{1,0},{2,3},{3,2},{4,5},{5,4},{6,7},{7,6},{8,9},{9,8},{10,11... | collective-permute-start | bytes 1179656 | tf_op jit(solution)/shard_map/right_over_core/ppermute | solution.py:456
  63.2 0.1 collective-permute-start.9
  63.3 0.0 copy-done
  63.3 0.0 copy-done.6
  63.3 1.5 %first_image.2.begun = f32[2,128,128]{2,1,0:T(8,128)S(1)} custom-call(s32[16]{0:T(128)S(1)} %copy-done.6, s32[256]{0:T(256)S(1)} %copy-done.5, s32[256]{0:T(256)S(1)} %copy-done.4, bf16[16,128,128]{2,1,0:T(8,128)(2,1)S(1)} %copy-done, bf16[8,272,128]{2,1,0:T(8,128)(2,1)S(1)} %get-tuple-element.29.rest_0_, ...), custom_call_target="tpu_custom_call" | custom-call | flops 201326592 | bytes 1048576 | tf_op jit(solution)/shard_map/first_image/pallas_call | solution.py:458
  64.8 0.0 collective-permute-done.9.rest_1_.rest_3_
  64.8 0.0 collective-permute-done.10.rest_2_.rest_8_
  64.8 1.8 %first_image.3 = (bf16[2,128,128]{2,1,0:T(8,128)(2,1)S(1)}, f32[8,128]{1,0:T(8,128)S(1)}) custom-call(s32[16]{0:T(128)S(1)} %copy-done.6, s32[256]{0:T(256)S(1)} %copy-done.5, s32[256]{0:T(256)S(1)} %copy-done.4, bf16[16,128,128]{2,1,0:T(8,128)(2,1)S(1)} %copy-done, f32[2,128,128]{2,1,0:T(8,128)S(1)} %first_image.2.begun, ...), custom_call_target="tpu_custom_call" | custom-call | tf_op jit(solution)/shard_map/first_image/pallas_call | solution.py:467
  66.7 3.9 %collective-permute-start.11 = (bf16[2,128,128]{2,1,0:T(8,128)(2,1)S(1)}, bf16[2,128,128]{2,1,0:T(8,128)(2,1)S(1)}, u32[]{:S(2)}, u32[]{:S(2)}) collective-permute-start(bf16[2,128,128]{2,1,0:T(8,128)(2,1)S(1)} %get-tuple-element.40.image_here), channel_id=1, source_target_pairs={{0,8},{1,9},{2,10},{3,11},{4,12},{5,13},{6,14},{7,15},{8,0},{9,1},... | collective-permute-start | bytes 196616 | tf_op jit(solution)/shard_map/swap_images/ppermute | solution.py:479
  70.6 3.2 %collective-permute-done.11.image_there = bf16[2,128,128]{2,1,0:T(8,128)(2,1)S(1)} collective-permute-done((bf16[2,128,128]{2,1,0:T(8,128)(2,1)S(1)}, bf16[2,128,128]{2,1,0:T(8,128)(2,1)S(1)}, u32[]{:S(2)}, u32[]{:S(2)}) %collective-permute-start.11) | collective-permute-done | bytes 65568 | tf_op jit(solution)/shard_map/swap_images/ppermute | solution.py:479
  73.8 2.2 %second_image.1 = bf16[16,32,128]{2,1,0:T(8,128)(2,1)S(1)} custom-call(s32[16]{0:T(128)S(1)} %copy-done.6, s32[256]{0:T(256)S(1)} %copy-done.5, s32[256]{0:T(256)S(1)} %copy-done.4, bf16[16,128,128]{2,1,0:T(8,128)(2,1)S(1)} %copy-done, f32[8,128]{1,0:T(8,128)S(1)} %get-tuple-element.39.ratios, bf16[2,128,128]{2,1,0:T(8,128)(2,1)S(1)} %get-tuple-element.40.image_here, ...), custom_call_target="tpu_custom_call" | custom-call | tf_op jit(solution)/shard_map/second_image/pallas_call | solution.py:481
  76.0 16.8 %all_to_all.15.pieces = bf16[16,32,128]{2,1,0:T(8,128)(2,1)S(1)} all-to-all(bf16[16,32,128]{2,1,0:T(8,128)(2,1)S(1)} %second_image.1), channel_id=1, replica_groups=mesh['sec'=16,'mpo'=16] {'mpo'}, dimensions={0} | all-to-all | bytes 262144 | tf_op jit(solution)/shard_map/rows_over_mpo/all_to_all | solution.py:490
  92.8 10.9 %all_to_all.16.shared = f32[16,8,128]{2,1,0:T(8,128)S(1)} all-to-all(f32[16,8,128]{2,1,0:T(8,128)S(1)} %broadcast_in_dim.2), channel_id=1, replica_groups=mesh['sec'=16,'mpo'=16] {'sec'}, dimensions={0} | all-to-all | bytes 131072 | tf_op jit(solution)/shard_map/numbers_over_sec/all_to_all | solution.py:493
  103.7 1.8 %finish.1 = (f32[16,8,128]{2,1,0:T(8,128)}, f32[16,8,128]{2,1,0:T(8,128)}, f32[3]{0:T(128)}) custom-call(s32[16]{0:T(128)S(1)} %copy-done.6, s32[256]{0:T(256)S(1)} %copy-done.5, s32[256]{0:T(256)S(1)} %copy-done.4, bf16[16,128,128]{2,1,0:T(8,128)(2,1)S(1)} %copy-done, bf16[16,32,128]{2,1,0:T(8,128)(2,1)S(1)} %all_to_all.15.pieces, ...), custom_call_target="tpu_custom_call" | custom-call | tf_op jit(solution)/shard_map/finish/pallas_call | solution.py:495
  (7 shorter events, 0.1 us)
Async XLA Ops:
  3.6 7.6 %copy-start.4 = (s32[256]{0:T(256)S(1)}, s32[256]{0:T(256)}, u32[]{:S(2)}) copy-start(s32[256]{0:T(256)} %right_sector.11) | copy-start | bytes 3076
  3.6 7.6 %copy-start.7 = (f32[2]{0:T(128)S(1)}, f32[2]{0:T(128)}, u32[]{:S(2)}) copy-start(f32[2]{0:T(128)} %weights.1) | copy-start | bytes 28
  3.6 38.1 %all-to-all-start = ((bf16[16,2,2,128,128]{4,3,2,1,0:T(8,128)(2,1)}), bf16[16,2,2,128,128]{4,3,2,1,0:T(8,128)(2,1)S(1)}, u32[]{:S(2)}, u32[]{:S(2)}) async-start(bf16[16,2,2,128,128]{4,3,2,1,0:T(8,128)(2,1)} %pack_right.1), calls=%async_computation | async-start | bytes 4194304 | tf_op jit(solution)/shard_map/right_over_sec/all_to_all | solution.py:407
  11.2 1.2 %copy-start.3 = (bf16[2,16,128,128]{3,2,1,0:T(8,128)(2,1)S(1)}, bf16[2,16,128,128]{3,2,1,0:T(8,128)(2,1)}, u32[]{:S(2)}) copy-start(bf16[2,16,128,128]{3,2,1,0:T(8,128)(2,1)} %left_env.1) | copy-start | bytes 3145732
  15.4 16.3 %collective-permute-start.2 = (bf16[1040,128]{1,0:T(8,128)(2,1)S(1)}, bf16[1040,128]{1,0:T(8,128)(2,1)S(1)}, u32[]{:S(2)}, u32[]{:S(2)}) collective-permute-start(bf16[1040,128]{1,0:T(8,128)(2,1)S(1)} %get-tuple-element.25), channel_id=1, source_target_pairs={{0,2},{1,3},{2,4},{3,5},{4,6},{5,7},{6,8},{7,9},{8,10},{9,11},{10,... | collective-permute-start | bytes 798728 | tf_op jit(solution)/shard_map/left_over_z/ppermute | solution.py:423
  17.1 14.5 %collective-permute-start.3 = (bf16[1040,128]{1,0:T(8,128)(2,1)S(1)}, bf16[1040,128]{1,0:T(8,128)(2,1)S(1)}, u32[]{:S(2)}, u32[]{:S(2)}) collective-permute-start(bf16[1040,128]{1,0:T(8,128)(2,1)S(1)} %get-tuple-element.26), channel_id=1, source_target_pairs={{0,14},{1,15},{2,0},{3,1},{4,2},{5,3},{6,4},{7,5},{8,6},{9,7},{10,... | collective-permute-start | bytes 798728 | tf_op jit(solution)/shard_map/left_over_z/ppermute | solution.py:423
  21.1 10.5 %collective-permute-start = (bf16[528,128]{1,0:T(8,128)(2,1)S(1)}, bf16[528,128]{1,0:T(8,128)(2,1)S(1)}, u32[]{:S(2)}, u32[]{:S(2)}) collective-permute-start(bf16[528,128]{1,0:T(8,128)(2,1)S(1)} %get-tuple-element.23), channel_id=1, source_target_pairs={{0,4},{1,5},{2,6},{3,7},{4,8},{5,9},{6,10},{7,11},{8,12},{9,13},{1... | collective-permute-start | bytes 405512 | tf_op jit(solution)/shard_map/left_over_z/ppermute | solution.py:423
  21.1 10.5 %collective-permute-start.1 = (bf16[528,128]{1,0:T(8,128)(2,1)S(1)}, bf16[528,128]{1,0:T(8,128)(2,1)S(1)}, u32[]{:S(2)}, u32[]{:S(2)}) collective-permute-start(bf16[528,128]{1,0:T(8,128)(2,1)S(1)} %get-tuple-element.24), channel_id=1, source_target_pairs={{0,12},{1,13},{2,14},{3,15},{4,0},{5,1},{6,2},{7,3},{8,4},{9,5},{1... | collective-permute-start | bytes 405512 | tf_op jit(solution)/shard_map/left_over_z/ppermute | solution.py:423
  31.6 31.7 %copy-start = (bf16[16,128,128]{2,1,0:T(8,128)(2,1)S(1)}, bf16[16,128,128]{2,1,0:T(8,128)(2,1)}, u32[]{:S(2)}) copy-start(bf16[16,128,128]{2,1,0:T(8,128)(2,1)} %vectors.7) | copy-start | bytes 1572868
  31.6 31.7 %copy-start.5 = (s32[256]{0:T(256)S(1)}, s32[256]{0:T(256)}, u32[]{:S(2)}) copy-start(s32[256]{0:T(256)} %right_size.7) | copy-start | bytes 3076
  31.7 31.7 %copy-start.6 = (s32[16]{0:T(128)S(1)}, s32[16]{0:T(128)}, u32[]{:S(2)}) copy-start(s32[16]{0:T(128)} %left_size.7) | copy-start | bytes 196
  33.1 3.7 %collective-permute-start.4 = (bf16[8,272,128]{2,1,0:T(8,128)(2,1)S(1)}, bf16[8,272,128]{2,1,0:T(8,128)(2,1)S(1)}, u32[]{:S(2)}, u32[]{:S(2)}) collective-permute-start(bf16[8,272,128]{2,1,0:T(8,128)(2,1)S(1)} %get-tuple-element.28), channel_id=1, source_target_pairs={{0,1},{1,0},{2,3},{3,2},{4,5},{5,4},{6,7},{7,6},{8,9},{9,8},{10,11... | collective-permute-start | bytes 1671176 | tf_op jit(solution)/shard_map/left_over_core/ppermute | solution.py:433
  36.8 0.8 copy-start.1
  43.9 20.9 %copy-start.2 = (bf16[8,272,128]{2,1,0:T(8,128)(2,1)S(1)}, bf16[8,272,128]{2,1,0:T(8,128)(2,1)}, u32[]{:S(2)}) copy-start(bf16[8,272,128]{2,1,0:T(8,128)(2,1)} %copy-done.1) | copy-start | bytes 1671172
  43.9 14.7 %collective-permute-start.7 = (bf16[4,2,128,128]{3,2,1,0:T(8,128)(2,1)S(1)}, bf16[4,2,128,128]{3,2,1,0:T(8,128)(2,1)S(1)}, u32[]{:S(2)}, u32[]{:S(2)}) collective-permute-start(bf16[4,2,128,128]{3,2,1,0:T(8,128)(2,1)S(1)} %get-tuple-element.35), channel_id=1, source_target_pairs={{0,2},{1,3},{2,4},{3,5},{4,6},{5,7},{6,8},{7,9},{8,10},{9,11},{10,... | collective-permute-start | bytes 786440 | tf_op jit(solution)/shard_map/right_over_z/ppermute | solution.py:446
  45.6 13.0 %collective-permute-start.8 = (bf16[4,2,128,128]{3,2,1,0:T(8,128)(2,1)S(1)}, bf16[4,2,128,128]{3,2,1,0:T(8,128)(2,1)S(1)}, u32[]{:S(2)}, u32[]{:S(2)}) collective-permute-start(bf16[4,2,128,128]{3,2,1,0:T(8,128)(2,1)S(1)} %get-tuple-element.36), channel_id=1, source_target_pairs={{0,14},{1,15},{2,0},{3,1},{4,2},{5,3},{6,4},{7,5},{8,6},{9,7},{10,... | collective-permute-start | bytes 786440 | tf_op jit(solution)/shard_map/right_over_z/ppermute | solution.py:446
  49.6 8.9 %collective-permute-start.5 = (bf16[2,2,128,128]{3,2,1,0:T(8,128)(2,1)S(1)}, bf16[2,2,128,128]{3,2,1,0:T(8,128)(2,1)S(1)}, u32[]{:S(2)}, u32[]{:S(2)}) collective-permute-start(bf16[2,2,128,128]{3,2,1,0:T(8,128)(2,1)S(1)} %get-tuple-element.33), channel_id=1, source_target_pairs={{0,4},{1,5},{2,6},{3,7},{4,8},{5,9},{6,10},{7,11},{8,12},{9,13},{1... | collective-permute-start | bytes 393224 | tf_op jit(solution)/shard_map/right_over_z/ppermute | solution.py:446
  49.6 8.9 %collective-permute-start.6 = (bf16[2,2,128,128]{3,2,1,0:T(8,128)(2,1)S(1)}, bf16[2,2,128,128]{3,2,1,0:T(8,128)(2,1)S(1)}, u32[]{:S(2)}, u32[]{:S(2)}) collective-permute-start(bf16[2,2,128,128]{3,2,1,0:T(8,128)(2,1)S(1)} %get-tuple-element.34), channel_id=1, source_target_pairs={{0,12},{1,13},{2,14},{3,15},{4,0},{5,1},{6,2},{7,3},{8,4},{9,5},{1... | collective-permute-start | bytes 393224 | tf_op jit(solution)/shard_map/right_over_z/ppermute | solution.py:446
  59.1 5.7 %collective-permute-start.10 = (bf16[6,2,128,128]{3,2,1,0:T(8,128)(2,1)S(1)}, bf16[6,2,128,128]{3,2,1,0:T(8,128)(2,1)S(1)}, u32[]{:S(2)}, u32[]{:S(2)}) collective-permute-start(bf16[6,2,128,128]{3,2,1,0:T(8,128)(2,1)S(1)} %right_over_core.1), channel_id=1, source_target_pairs={{0,1},{1,0},{2,3},{3,2},{4,5},{5,4},{6,7},{7,6},{8,9},{9,8},{10,11... | collective-permute-start | bytes 1179656 | tf_op jit(solution)/shard_map/right_over_core/ppermute | solution.py:456
  63.2 1.6 %collective-permute-start.9 = (bf16[2,2,128,128]{3,2,1,0:T(8,128)(2,1)S(1)}, bf16[2,2,128,128]{3,2,1,0:T(8,128)(2,1)S(1)}, u32[]{:S(2)}, u32[]{:S(2)}) collective-permute-start(bf16[2,2,128,128]{3,2,1,0:T(8,128)(2,1)S(1)} %get-tuple-element.38), channel_id=1, source_target_pairs={{0,1},{1,0},{2,3},{3,2},{4,5},{5,4},{6,7},{7,6},{8,9},{9,8},{10,11... | collective-permute-start | bytes 393224 | tf_op jit(solution)/shard_map/right_over_z/ppermute | solution.py:445
  66.7 7.1 %collective-permute-start.11 = (bf16[2,128,128]{2,1,0:T(8,128)(2,1)S(1)}, bf16[2,128,128]{2,1,0:T(8,128)(2,1)S(1)}, u32[]{:S(2)}, u32[]{:S(2)}) collective-permute-start(bf16[2,128,128]{2,1,0:T(8,128)(2,1)S(1)} %get-tuple-element.40.image_here), channel_id=1, source_target_pairs={{0,8},{1,9},{2,10},{3,11},{4,12},{5,13},{6,14},{7,15},{8,0},{9,1},... | collective-permute-start | bytes 196616 | tf_op jit(solution)/shard_map/swap_images/ppermute | solution.py:479
